TPU v7x, 32 devices: a whole 2x2x4 slice. The times are simulated.
32 devices in a mesh: fsdp: 16 (over z, y, core), ctx: 2 (over x).
Axes of the slice: x: 2, y: 2, z: 4, core: 2. Of those that a mesh axis runs over, the one named last changes fastest.
Arguments:
- hidden: bfloat16 [16, 512, 5120], P('fsdp', 'ctx'), may hold values from -6 to 6
- queries: bfloat16 [16, 512, 4096], P('fsdp', 'ctx'), may hold values from -300 to 300, as said below
- norm_gain: float32 [5120], replicated, may hold values from 0.1 to 1.9
- key_gain: float32 [128], replicated, may hold values from 0.1 to 1.9
- k_weight: bfloat16 [5120, 512], P('fsdp'), may hold values from -0.078125 to 0.078125
- v_weight: bfloat16 [5120, 512], P('fsdp'), may hold values from -0.078125 to 0.078125
- segment: int32 [16, 512], P('fsdp', 'ctx'), may hold values from 0 to 3, as said below
- position: int32 [16, 512], P('fsdp', 'ctx'), may hold values from 0 to 8191, as said below
Outputs:
- attended: bfloat16 [16, 512, 4096], P('fsdp', 'ctx')
Inputs may be any that keep to these rules, and one draw needn't show every extreme that they name: queries keep to the stated range. `segment`: in each stretch, read in the tokens' order, rollout numbers never fall; the tokens of a stretch lie in its slots in an order that keeps 256 slots on each index of ctx, one token of every 2 consecutive ones on each. `position`: within one rollout of a stretch positions rise by one from token to token.
All inputs are finite; a program needn't handle non-finite values.
Results may differ from a plain program's by a relative error of at most 0.0075.
The roundings to bfloat16 on the way count: a program that leaves them out, or rounds other values in their place, can miss the bound.
Values may be sent and summed in bfloat16 or wider, within the bound.
No kernel may reach another device: no remote copies, remote signals or barrier semaphores. Data moves between devices by JAX's collectives and lax.ppermute only.
A program may use at most 192 MiB of HBM per device.

v0:
```python
import functools
import math

import jax
import jax.numpy as jnp
import numpy as np
from jax import lax
from jax.experimental import pallas as pl
from jax.experimental.pallas import tpu as pltpu
from jax.sharding import Mesh
from jax.sharding import PartitionSpec as P

KVH = 4
HD = 128
G = 8
EPS = 1e-06
THETA = 1000000.0
MASKED = -1e30
VMEM_LIMIT = 24 * 2**20
NORM_ROWS = 64


def norm_kernel(chunks, hidden, gain, out):
    inputs = hidden[...].astype(jnp.float32)
    scale = lax.rsqrt(jnp.mean(inputs * inputs, axis=-1, keepdims=True) + EPS)
    normed = (inputs * scale * gain[...]).astype(jnp.bfloat16)
    rows = normed.shape[1] // chunks
    for j in range(chunks):
        out[j] = normed[:, j * rows : (j + 1) * rows]


def project_kernel(chips_z, items, first, last, count, place, own, other, *rest):
    z, y, x = place[0], place[1], place[2]
    pieces, rest = dict(zip(items, rest)), rest[len(items) :]
    terms = {}
    for k in range(chips_z):
        p = lax.rem(z - k + chips_z, chips_z)
        for chunk, kinds in (
            (p * 2 + y, ("mine", "across")),
            (p * 2 + 1 - y, ("beside", "corner")),
        ):
            rows = None
            for side, kind in enumerate(kinds):
                if (k, kind) not in pieces:
                    continue
                if rows is None:
                    rows = jnp.concatenate([own[chunk], other[chunk]], axis=0)
                part = jnp.dot(rows, pieces[k, kind][...], preferred_element_type=jnp.float32)
                terms[side] = terms[side] + part if side in terms else part
    acc = rest[-1]
    for side, at in ((0, x), (1, 1 - x)):
        if side in terms:
            acc[at] = terms[side] if first else rest[0][at] + terms[side]
        else:
            acc[at] = rest[0][at]
    if not last:
        return
    cosine, sine, gain = rest[1:4]
    outs = rest[4:8]
    for head in range(2):
        columns = slice(head * HD, (head + 1) * HD)
        for part in range(2):
            at = slice(part * count, (part + 1) * count)
            out = outs[2 * head + part]
            raw = acc[0, at, columns]
            normk = raw * lax.rsqrt(jnp.mean(raw * raw, axis=-1, keepdims=True) + EPS) * gain[...]
            turned = normk * cosine[at, :] + pltpu.roll(normk, HD // 2, 1) * sine[at, :]
            out[:, :HD] = turned.astype(jnp.bfloat16)
            out[:, HD:] = acc[1, at, columns].astype(jnp.bfloat16)


def mask_kernel(seg_q, pos_q, seg_k, pos_k, bias, needs):
    allowed = (seg_k[...] == seg_q[...]) & (pos_k[...] <= pos_q[...])
    bias[...] = jnp.where(allowed, 0.0, MASKED)
    rows, columns = bias.shape[0] // 2, bias.shape[1] // 2
    for tile in range(2):
        found = [
            jnp.max(
                bias[tile * rows : (tile + 1) * rows, half * columns : (half + 1) * columns]
            )
            == 0.0
            for half in range(2)
        ]
        needs[tile] = found[0].astype(jnp.int32) + 2 * found[1].astype(jnp.int32)


def attend_kernel(pieces, count, place, needs, queries, bias, *rest):
    sources, (out, keys, values) = rest[: 2 * pieces], rest[-3:]
    step = pl.program_id(0)
    tile_rows = count // 2
    length = pieces * tile_rows

    for at in range(2):

        @pl.when(step == at)
        def _():
            for i in range(pieces):
                source = sources[at * pieces + i]
                for half in range(2):
                    here = slice(half * tile_rows, (half + 1) * tile_rows)
                    there = half * length + i * tile_rows
                    keys[there : there + tile_rows, :] = source[here, :HD]
                    values[there : there + tile_rows, :] = source[here, HD:]

    factor = math.log2(math.e) / math.sqrt(HD)

    def tile_body(tile, low, high):
        rows = slice(tile * tile_rows, (tile + 1) * tile_rows)
        k, v, b = keys[low:high, :], values[low:high, :], bias[rows, low:high]

        def score(pair):
            q = jnp.concatenate(
                [queries[rows, g * HD : (g + 1) * HD] for g in (2 * pair, 2 * pair + 1)], axis=0
            )
            return lax.dot_general(
                q, k, (((1,), (1,)), ((), ())), preferred_element_type=jnp.float32
            )

        ahead = score(0)
        for pair in range(G // 2):
            scores = ahead.reshape(2, tile_rows, high - low) + b[None]
            if pair + 1 < G // 2:
                ahead = score(pair + 1)
            top = jnp.max(scores, axis=-1, keepdims=True)
            weights = jnp.exp2((scores - top) * factor)
            total = jnp.sum(weights, axis=-1, keepdims=True)
            summed = jnp.dot(
                weights.astype(jnp.bfloat16).reshape(2 * tile_rows, high - low),
                v,
                preferred_element_type=jnp.float32,
            ).reshape(2, tile_rows, HD)
            result = (summed * (1.0 / total)).astype(jnp.bfloat16)
            for i in range(2):
                g = 2 * pair + i
                out[rows, g * HD : (g + 1) * HD] = result[i]

    for tile in range(2):
        for need, low, high in ((1, 0, length), (2, length, 2 * length), (3, 0, 2 * length)):

            @pl.when(needs[tile] == need)
            def _():
                tile_body(tile, low, high)


def swap(array, axis):
    return lax.ppermute(array, axis, [(0, 1), (1, 0)])


def on_device(
    sizes, hidden, queries, norm_gain, key_gain, k_weight, v_weight, segment, position
):
    chips_z, groups = sizes[0], sizes[3]
    count, width = hidden.shape[1:]
    own_rows = k_weight.shape[0]
    rows = 2 * own_rows
    chunks = 2 * chips_z
    m = 2 * groups
    z, y = lax.axis_index("z"), lax.axis_index("y")
    core, x = lax.axis_index("core"), lax.axis_index("x")
    bf16 = jnp.bfloat16
    whole = pl.BlockSpec(memory_space=pltpu.VMEM)
    params = pltpu.CompilerParams(vmem_limit_bytes=VMEM_LIMIT)

    def along_ctx(array, d, cross=False):
        pairs = []
        for c in range(2):
            for i in range(m):
                pairs.append((c * m + i, (c ^ int(cross)) * m + (i + d) % m))
        return lax.ppermute(array, ("core", "ctx", "x"), pairs)

    def columns(which):
        at = which * 2 * HD
        return jnp.stack(
            [lax.dynamic_slice_in_dim(w, at, 2 * HD, 1) for w in (k_weight, v_weight)]
        )

    taken = swap(columns(1 - core), "core")
    kept = columns(core)
    chip = lax.dynamic_update_slice(
        jnp.zeros((2, rows, 2 * HD), bf16), kept, (0, core * own_rows, 0)
    )
    chip = lax.dynamic_update_slice(chip, taken, (0, (1 - core) * own_rows, 0))
    mine = [lax.dynamic_index_in_dim(chip, x, 0, keepdims=False)]
    across = [lax.dynamic_index_in_dim(chip, 1 - x, 0, keepdims=False)]
    hidden, mine[0], across[0] = lax.optimization_barrier((hidden, mine[0], across[0]))
    normed = pl.pallas_call(
        functools.partial(norm_kernel, chunks),
        out_shape=jax.ShapeDtypeStruct((chunks, count, rows), bf16),
        grid=(count // NORM_ROWS,),
        in_specs=[pl.BlockSpec((NORM_ROWS, width), lambda i: (i, 0)), whole],
        out_specs=pl.BlockSpec((chunks, NORM_ROWS, rows), lambda i: (0, i, 0)),
        compiler_params=params,
        cost_estimate=pl.CostEstimate(
            flops=4 * count * width, bytes_accessed=4 * count * width, transcendentals=0
        ),
        name="norm",
    )(hidden[0], norm_gain[None])
    ints = jnp.concatenate([segment, position])
    ints_all = [ints] + [along_ctx(ints, d) for d in range(1, m)]
    where = jnp.concatenate([position[0], swap(position, "core")[0]]).astype(jnp.float32)
    half = HD // 2
    freq = np.exp(np.arange(half, dtype=np.float32) * np.float32(-2.0 * math.log(THETA) / HD))
    angle = where[:, None] * freq[None, :]
    cosine, sine = jnp.cos(angle), jnp.sin(angle)
    cosine = jnp.concatenate([cosine, cosine], axis=1)
    sine = jnp.concatenate([-sine, sine], axis=1)
    order = (
        jnp.stack(ints_all).reshape(m, 2, 2, count // 2).transpose(1, 2, 0, 3).reshape(2, m * count)
    )
    bias, needs = pl.pallas_call(
        mask_kernel,
        out_shape=[
            jax.ShapeDtypeStruct((count, m * count), jnp.float32),
            jax.ShapeDtypeStruct((2,), jnp.int32),
        ],
        in_specs=[whole] * 4,
        out_specs=[whole, pl.BlockSpec(memory_space=pltpu.SMEM)],
        compiler_params=params,
        name="mask",
    )(segment.reshape(count, 1), position.reshape(count, 1), order[:1], order[1:])

    ring = [(i, (i + 1) % chips_z) for i in range(chips_z)]
    end = chips_z - 1
    beside = [swap(mine[0], "y")]
    for k in range(1, chips_z):
        arrived = lax.ppermute(mine[-1], "z", ring)
        if k == 1:
            normed, arrived, beside[0] = lax.optimization_barrier(
                (normed, arrived, beside[0])
            )
        else:
            arrived, beside[k - 1], across[k - 1] = lax.optimization_barrier(
                (arrived, beside[k - 1], across[k - 1])
            )
        if k == end:
            arrived, beside[0], across[1], bias, needs = lax.optimization_barrier(
                (arrived, beside[0], across[1], bias, needs)
            )
        mine.append(arrived)
        beside.append(swap(arrived, "y"))
        across.append(swap(arrived, "x"))
    corner = {0: swap(beside[0], "x"), 1: swap(across[1], "y")}
    tied = lax.optimization_barrier((beside[end], *across[2:end]))
    beside[end], across[2:end] = tied[0], list(tied[1:])
    for k in range(2, chips_z):
        corner[k] = swap(beside[k], "x") if k == end or k % 2 else swap(across[k], "y")

    normed_other = swap(normed, "core")

    place = jnp.stack([z, y, x]).astype(jnp.int32)
    acc_shape = jax.ShapeDtypeStruct((2, 2 * count, 2 * HD), jnp.float32)
    kv_shape = jax.ShapeDtypeStruct((count, 2 * HD), bf16)
    kinds = dict(mine=mine, across=across, beside=beside, corner=corner)
    every = [(k, kind) for k in range(chips_z) for kind in kinds]
    final = [(k, "corner") for k in range(2, chips_z)]
    late = [(end, "across"), (end, "beside"), (0, "corner"), (1, "corner")]
    early = [item for item in every if item not in final + late]
    acc = []
    for items in (early, late, final):
        first, last = items is early, items is final
        outs = pl.pallas_call(
            functools.partial(project_kernel, chips_z, items, first, last, count),
            out_shape=[kv_shape] * 4 if last else [acc_shape],
            in_specs=[pl.BlockSpec(memory_space=pltpu.SMEM)]
            + [whole] * (2 + len(items) + len(acc) + (3 if last else 0)),
            out_specs=[whole] * (4 if last else 1),
            scratch_shapes=[pltpu.VMEM(acc_shape.shape, acc_shape.dtype)] * int(last),
            compiler_params=params,
            cost_estimate=pl.CostEstimate(
                flops=2 * 2 * count * rows * 2 * HD * len(items),
                bytes_accessed=2 * rows * 2 * HD * len(items),
                transcendentals=0,
            ),
            name="project",
        )(
            place, normed, normed_other, *[kinds[kind][k] for k, kind in items], *acc,
            *((cosine, sine, key_gain[None]) if last else ()),
        )
        acc = [outs[-1]]

    result = None
    for s in range(2):
        kv_own, kv_other = outs[2 * s], outs[2 * s + 1]
        sources = [kv_own] + [along_ctx(kv_own, d) for d in range(1, m)]
        sources += [along_ctx(kv_other, d, True) for d in range(m)]

        def block(step, place, needs, s=s):
            return (0, lax.rem(place[0] + step, 2) * 2 + s)

        earlier = [] if result is None else [result]
        result = pl.pallas_call(
            functools.partial(attend_kernel, m, count),
            out_shape=jax.ShapeDtypeStruct((count, KVH * G * HD), bf16),
            grid_spec=pltpu.PrefetchScalarGridSpec(
                num_scalar_prefetch=2,
                grid=(2,),
                in_specs=[pl.BlockSpec((count, G * HD), block)]
                + [whole] * (1 + 2 * m)
                + [pl.BlockSpec(memory_space=pl.ANY)] * len(earlier),
                out_specs=pl.BlockSpec((count, G * HD), block),
                scratch_shapes=[
                    pltpu.VMEM((m * count, HD), bf16),
                    pltpu.VMEM((m * count, HD), bf16),
                ],
            ),
            input_output_aliases={4 + 2 * m: 0} if earlier else {},
            compiler_params=params,
            cost_estimate=pl.CostEstimate(
                flops=2 * count * m * count * KVH * G * HD,
                bytes_accessed=2 * count * KVH * G * HD,
                transcendentals=count * m * count * KVH * G // 2,
            ),
            name="attend",
        )(core.astype(jnp.int32)[None], needs, queries[0], bias, *sources, *earlier)
    return result[None]


def solution(mesh):
    n, m = mesh.shape["fsdp"], mesh.shape["ctx"]
    sizes = (n // 4, 2, 2, m // 2, 2)
    fine = Mesh(mesh.devices.reshape(sizes), ("z", "y", "core", "ctx", "x"))
    fsdp, ctx = ("z", "y", "core"), ("ctx", "x")
    placed = (
        P(fsdp, ctx, None),
        P(fsdp, ctx, None),
        P(),
        P(),
        P(fsdp, None),
        P(fsdp, None),
        P(fsdp, ctx),
        P(fsdp, ctx),
    )
    return jax.shard_map(
        functools.partial(on_device, sizes),
        mesh=fine,
        in_specs=placed,
        out_specs=P(fsdp, ctx, None),
        check_vma=False,
    )
```

profile of v0, /device:TPU:0, one launch (start us, length us, event | category | flops | bytes accessed | tf_op | source)
XLA Modules:
  0.0 87.4 jit_solution(17322620048212110925)
XLA Ops:
  0.0 1.2 %dynamic-slice_bitcast_fusion.2 = (bf16[1,320,256]{2,1,0:T(8,128)(2,1)S(1)}, bf16[1,320,256]{2,1,0:T(8,128)(2,1)S(1)}, bf16[1,320,256]{2,1,0:T(8,128)(2,1)S(1)}, bf16[1,320,256]{2,1,0:T(8,128)(2,1)S(1)}) fusion(bf16[320,512]{1,0:T(8,128)(2,1)} %param.14, s32[]{:T(128)S(6)} %select_n.23, s32[]{:T(128)S(6)} %select_n.21, bf16[320,512]{1,0:T(8,128)(2,1)} %param.13), kind=kLoop, calls=%fused_computation.8 | loop fusion | bytes 1310728 | tf_op jit(solution)/shard_map/stack | solution.py:173
  1.3 0.5 collective-permute-start
  1.9 1.2 %collective-permute-done = bf16[2,320,256]{2,1,0:T(8,128)(2,1)S(1)} collective-permute-done((bf16[2,320,256]{2,1,0:T(8,128)(2,1)S(1)}, bf16[2,320,256]{2,1,0:T(8,128)(2,1)S(1)}, u32[]{:S(2)}, u32[]{:S(2)}) %collective-permute-start) | collective-permute-done | bytes 327712 | tf_op jit(solution)/shard_map/ppermute | solution.py:146
  3.1 0.1 dynamic-slice_bitcast_fusion
  3.1 3.0 %collective-permute-start.1 = (bf16[640,256]{1,0:T(8,128)(2,1)S(1)}, bf16[640,256]{1,0:T(8,128)(2,1)}, u32[]{:S(2)}, u32[]{:S(2)}) collective-permute-start(bf16[640,256]{1,0:T(8,128)(2,1)S(1)} %get-tuple-element.31.rest_0_), channel_id=1, source_target_pairs={{0,8},{8,16},{16,24},{24,0},{1,9},{9,17},{17,25},{25,1},{2,10},{10... | collective-permute-start | bytes 983048 | tf_op jit(solution)/shard_map/ppermute | solution.py:226
  6.1 1.5 %collective-permute-start.2 = (bf16[640,256]{1,0:T(8,128)(2,1)S(1)}, bf16[640,256]{1,0:T(8,128)(2,1)S(1)}, u32[]{:S(2)}, u32[]{:S(2)}) collective-permute-start(bf16[640,256]{1,0:T(8,128)(2,1)S(1)} %get-tuple-element.31.rest_0_), channel_id=1, source_target_pairs={{0,4},{4,0},{1,5},{5,1},{2,6},{6,2},{3,7},{7,3},{8,12},{12,8},{9,1... | collective-permute-start | bytes 983048 | tf_op jit(solution)/shard_map/ppermute | solution.py:146
  7.6 1.7 %copy-done.1 = bf16[1,256,5120]{2,1,0:T(8,128)(2,1)S(1)} copy-done((bf16[1,256,5120]{2,1,0:T(8,128)(2,1)S(1)}, bf16[1,256,5120]{2,1,0:T(8,128)(2,1)}, u32[]{:S(2)}) %copy-start.1) | copy-done | bytes 2621464
  9.4 1.8 %norm.1.own = bf16[8,256,640]{2,1,0:T(8,128)(2,1)S(1)} custom-call(bf16[256,5120]{1,0:T(8,128)(2,1)S(1)} %bitcast.33, f32[1,5120]{1,0:T(1,128)S(1)} %bitcast.34), custom_call_target="tpu_custom_call" | custom-call | flops 5242880 | bytes 5242880 | tf_op jit(solution)/shard_map/norm/pallas_call | solution.py:186
  11.2 5.1 %collective-permute-done.1.rest_3_ = bf16[640,256]{1,0:T(8,128)(2,1)} collective-permute-done((bf16[640,256]{1,0:T(8,128)(2,1)S(1)}, bf16[640,256]{1,0:T(8,128)(2,1)}, u32[]{:S(2)}, u32[]{:S(2)}) %collective-permute-start.1) | collective-permute-done | bytes 327712 | tf_op jit(solution)/shard_map/ppermute | solution.py:226
  16.3 0.7 copy-done.2
  17.0 0.9 %collective-permute-start.3 = (bf16[640,256]{1,0:T(8,128)(2,1)}, bf16[640,256]{1,0:T(8,128)(2,1)}, u32[]{:S(2)}, u32[]{:S(2)}) collective-permute-start(bf16[640,256]{1,0:T(8,128)(2,1)} %collective-permute-done.1.rest_3_), channel_id=1, source_target_pairs={{0,8},{8,16},{16,24},{24,0},{1,9},{9,17},{17,25},{25,1},{2,10},{10... | collective-permute-start | bytes 983048 | tf_op jit(solution)/shard_map/ppermute | solution.py:226
  17.9 1.5 %collective-permute-start.4 = (bf16[640,256]{1,0:T(8,128)(2,1)}, bf16[640,256]{1,0:T(8,128)(2,1)}, u32[]{:S(2)}, u32[]{:S(2)}) collective-permute-start(bf16[640,256]{1,0:T(8,128)(2,1)} %collective-permute-done.1.rest_3_), channel_id=1, source_target_pairs={{0,4},{4,0},{1,5},{5,1},{2,6},{6,2},{3,7},{7,3},{8,12},{12,8},{9,1... | collective-permute-start | bytes 983048 | tf_op jit(solution)/shard_map/ppermute | solution.py:146
  19.4 1.5 %collective-permute-start.5 = (bf16[640,256]{1,0:T(8,128)(2,1)}, bf16[640,256]{1,0:T(8,128)(2,1)}, u32[]{:S(2)}, u32[]{:S(2)}) collective-permute-start(bf16[640,256]{1,0:T(8,128)(2,1)} %collective-permute-done.1.rest_3_), channel_id=1, source_target_pairs={{0,1},{1,0},{2,3},{3,2},{4,5},{5,4},{6,7},{7,6},{8,9},{9,8},{10,11... | collective-permute-start | bytes 983048 | tf_op jit(solution)/shard_map/ppermute | solution.py:146
  20.9 0.6 collective-permute-start.9
  21.5 0.1 pad_add_fusion.1.place
  21.6 0.1 copy.15.seg_q
  21.8 0.1 copy.16.pos_q
  21.9 7.4 %collective-permute-done.9 = s32[2,256]{1,0:T(2,128)} collective-permute-done((s32[2,256]{1,0:T(2,128)S(1)}, s32[2,256]{1,0:T(2,128)}, u32[]{:S(2)}, u32[]{:S(2)}) %collective-permute-start.9) | collective-permute-done | bytes 2080 | tf_op jit(solution)/shard_map/ppermute | solution.py:169
  29.3 0.7 stack.46
  30.1 1.6 %collective-permute-start.6 = (bf16[640,256]{1,0:T(8,128)(2,1)}, bf16[640,256]{1,0:T(8,128)(2,1)S(1)}, u32[]{:S(2)}, u32[]{:S(2)}) collective-permute-start(bf16[640,256]{1,0:T(8,128)(2,1)} %collective-permute-done.3.rest_6_), channel_id=1, source_target_pairs={{0,8},{8,16},{16,24},{24,0},{1,9},{9,17},{17,25},{25,1},{2,10},{10... | collective-permute-start | bytes 983048 | tf_op jit(solution)/shard_map/ppermute | solution.py:226
  31.7 0.5 collective-permute-start.7
  32.2 1.5 %collective-permute-start.8 = (bf16[640,256]{1,0:T(8,128)(2,1)}, bf16[640,256]{1,0:T(8,128)(2,1)S(1)}, u32[]{:S(2)}, u32[]{:S(2)}) collective-permute-start(bf16[640,256]{1,0:T(8,128)(2,1)} %collective-permute-done.3.rest_6_), channel_id=1, source_target_pairs={{0,1},{1,0},{2,3},{3,2},{4,5},{5,4},{6,7},{7,6},{8,9},{9,8},{10,11... | collective-permute-start | bytes 983048 | tf_op jit(solution)/shard_map/ppermute | solution.py:146
  33.7 0.9 mask.1
  34.6 7.7 %collective-permute-done.6.rest_9_ = bf16[640,256]{1,0:T(8,128)(2,1)S(1)} collective-permute-done((bf16[640,256]{1,0:T(8,128)(2,1)}, bf16[640,256]{1,0:T(8,128)(2,1)S(1)}, u32[]{:S(2)}, u32[]{:S(2)}) %collective-permute-start.6) | collective-permute-done | bytes 327712 | tf_op jit(solution)/shard_map/ppermute | solution.py:226
  42.2 1.2 %collective-permute-start.11 = (bf16[640,256]{1,0:T(8,128)(2,1)S(1)}, bf16[640,256]{1,0:T(8,128)(2,1)S(1)}, u32[]{:S(2)}, u32[]{:S(2)}) collective-permute-start(bf16[640,256]{1,0:T(8,128)(2,1)S(1)} %collective-permute-done.6.rest_9_), channel_id=1, source_target_pairs={{0,4},{4,0},{1,5},{5,1},{2,6},{6,2},{3,7},{7,3},{8,12},{12,8},{9,1... | collective-permute-start | bytes 983048 | tf_op jit(solution)/shard_map/ppermute | solution.py:146
  43.5 0.7 add_convert_fusion
  44.2 1.5 %collective-permute-start.14 = (bf16[640,256]{1,0:T(8,128)(2,1)S(1)}, bf16[640,256]{1,0:T(8,128)(2,1)S(1)}, u32[]{:S(2)}, u32[]{:S(2)}) collective-permute-start(bf16[640,256]{1,0:T(8,128)(2,1)S(1)} %collective-permute-done.6.rest_9_), channel_id=1, source_target_pairs={{0,1},{1,0},{2,3},{3,2},{4,5},{5,4},{6,7},{7,6},{8,9},{9,8},{10,11... | collective-permute-start | bytes 983048 | tf_op jit(solution)/shard_map/ppermute | solution.py:146
  45.7 0.5 collective-permute-start.15
  46.2 0.8 collective-permute-start.16
  47.0 1.6 %fusion = (f32[512,64]{1,0:T(8,128)S(1)}, f32[512,64]{1,0:T(8,128)S(1)}, f32[512,64]{1,0:T(8,128)S(1)}) fusion(f32[64]{0:T(128)} %constant.47, f32[512]{0:T(512)S(1)} %add_convert_fusion), kind=kLoop, calls=%fused_computation.12 | loop fusion | flops 65536 | bytes 395520 | tf_op jit(solution)/shard_map/neg | solution.py:206
  48.6 4.2 %collective-permute-done.11.rest_1_ = bf16[640,256]{1,0:T(8,128)(2,1)S(1)} collective-permute-done((bf16[640,256]{1,0:T(8,128)(2,1)S(1)}, bf16[640,256]{1,0:T(8,128)(2,1)S(1)}, u32[]{:S(2)}, u32[]{:S(2)}) %collective-permute-start.11) | collective-permute-done | bytes 327712 | tf_op jit(solution)/shard_map/ppermute | solution.py:146
  52.9 1.3 %collective-permute-start.12 = (bf16[640,256]{1,0:T(8,128)(2,1)S(1)}, bf16[640,256]{1,0:T(8,128)(2,1)S(1)}, u32[]{:S(2)}, u32[]{:S(2)}) collective-permute-start(bf16[640,256]{1,0:T(8,128)(2,1)S(1)} %collective-permute-done.8.rest_7_), channel_id=1, source_target_pairs={{0,4},{4,0},{1,5},{5,1},{2,6},{6,2},{3,7},{7,3},{8,12},{12,8},{9,1... | collective-permute-start | bytes 983048 | tf_op jit(solution)/shard_map/ppermute | solution.py:146
  54.1 1.5 %collective-permute-start.13 = (bf16[640,256]{1,0:T(8,128)(2,1)S(1)}, bf16[640,256]{1,0:T(8,128)(2,1)S(1)}, u32[]{:S(2)}, u32[]{:S(2)}) collective-permute-start(bf16[640,256]{1,0:T(8,128)(2,1)S(1)} %collective-permute-done.11.rest_1_), channel_id=1, source_target_pairs={{0,1},{1,0},{2,3},{3,2},{4,5},{5,4},{6,7},{7,6},{8,9},{9,8},{10,11... | collective-permute-start | bytes 983048 | tf_op jit(solution)/shard_map/ppermute | solution.py:146
  55.6 0.2 pad_maximum_fusion.1
  55.8 4.3 %project.3.rest_4_ = f32[2,512,256]{2,1,0:T(8,128)S(1)} custom-call(s32[3]{0:T(128)S(1)} %pad_add_fusion.1.place, bf16[8,256,640]{2,1,0:T(8,128)(2,1)S(1)} %norm.1.own, bf16[8,256,640]{2,1,0:T(8,128)(2,1)} %collective-permute-done.10.other, bf16[640,256]{1,0:T(8,128)(2,1)S(1)} %get-tuple-element.31.rest_0_, bf16[640,256]{1,0:T(8,128)(2,1)S(1)} %get-tuple-element.48.rest_1_, ...), custom_call_target="tpu_custom_call" | custom-call | flops 1677721600 | bytes 3276800 | tf_op jit(solution)/shard_map/project/pallas_call | solution.py:261
  60.1 0.0 copy-start.5
  60.2 1.7 %collective-permute-done.15.rest_2_ = bf16[640,256]{1,0:T(8,128)(2,1)S(1)} collective-permute-done((bf16[640,256]{1,0:T(8,128)(2,1)}, bf16[640,256]{1,0:T(8,128)(2,1)S(1)}, u32[]{:S(2)}, u32[]{:S(2)}) %collective-permute-start.15) | collective-permute-done | bytes 327712 | tf_op jit(solution)/shard_map/ppermute | solution.py:146
  61.9 2.7 %project.4.rest_2_ = f32[2,512,256]{2,1,0:T(8,128)S(1)} custom-call(s32[3]{0:T(128)S(1)} %pad_add_fusion.1.place, bf16[8,256,640]{2,1,0:T(8,128)(2,1)S(1)} %norm.1.own, bf16[8,256,640]{2,1,0:T(8,128)(2,1)} %collective-permute-done.10.other, bf16[640,256]{1,0:T(8,128)(2,1)S(1)} %collective-permute-done.14.rest_0_, ...), custom_call_target="tpu_custom_call" | custom-call | flops 671088640 | bytes 1310720 | tf_op jit(solution)/shard_map/project/pallas_call | solution.py:261
  64.6 1.0 %collective-permute-done.12.rest_0_ = bf16[640,256]{1,0:T(8,128)(2,1)S(1)} collective-permute-done((bf16[640,256]{1,0:T(8,128)(2,1)S(1)}, bf16[640,256]{1,0:T(8,128)(2,1)S(1)}, u32[]{:S(2)}, u32[]{:S(2)}) %collective-permute-start.12) | collective-permute-done | bytes 327712 | tf_op jit(solution)/shard_map/ppermute | solution.py:146
  65.6 1.0 %collective-permute-done.13.rest_1_ = bf16[640,256]{1,0:T(8,128)(2,1)S(1)} collective-permute-done((bf16[640,256]{1,0:T(8,128)(2,1)S(1)}, bf16[640,256]{1,0:T(8,128)(2,1)S(1)}, u32[]{:S(2)}, u32[]{:S(2)}) %collective-permute-start.13) | collective-permute-done | bytes 327712 | tf_op jit(solution)/shard_map/ppermute | solution.py:146
  66.7 2.8 %project.5 = (bf16[256,256]{1,0:T(8,128)(2,1)S(1)}, bf16[256,256]{1,0:T(8,128)(2,1)S(1)}, bf16[256,256]{1,0:T(8,128)(2,1)S(1)}, bf16[256,256]{1,0:T(8,128)(2,1)S(1)}) custom-call(s32[3]{0:T(128)S(1)} %pad_add_fusion.1.place, bf16[8,256,640]{2,1,0:T(8,128)(2,1)S(1)} %norm.1.own, bf16[8,256,640]{2,1,0:T(8,128)(2,1)} %collective-permute-done.10.other, ...), custom_call_target="tpu_custom_call" | custom-call | flops 335544320 | bytes 655360 | tf_op jit(solution)/shard_map/project/pallas_call | solution.py:261
  69.5 1.6 %collective-permute-start.21 = (bf16[256,256]{1,0:T(8,128)(2,1)S(1)}, bf16[256,256]{1,0:T(8,128)(2,1)S(1)}, u32[]{:S(2)}, u32[]{:S(2)}) collective-permute-start(bf16[256,256]{1,0:T(8,128)(2,1)S(1)} %get-tuple-element.53.rest_0_), channel_id=1, source_target_pairs={{0,1},{1,0},{2,3},{3,2},{4,5},{5,4},{6,7},{7,6},{8,9},{9,8},{10,11... | collective-permute-start | bytes 393224 | tf_op jit(solution)/shard_map/ppermute | solution.py:169
  71.0 0.6 collective-permute-start.23
  71.7 1.5 %collective-permute-start.18 = (bf16[256,256]{1,0:T(8,128)(2,1)S(1)}, bf16[256,256]{1,0:T(8,128)(2,1)S(1)}, u32[]{:S(2)}, u32[]{:S(2)}) collective-permute-start(bf16[256,256]{1,0:T(8,128)(2,1)S(1)} %get-tuple-element.51.rest_0_), channel_id=1, source_target_pairs={{0,1},{1,0},{2,3},{3,2},{4,5},{5,4},{6,7},{7,6},{8,9},{9,8},{10,11... | collective-permute-start | bytes 393224 | tf_op jit(solution)/shard_map/ppermute | solution.py:169
  73.2 1.8 %collective-permute-done.21.rest_1_ = bf16[256,256]{1,0:T(8,128)(2,1)S(1)} collective-permute-done((bf16[256,256]{1,0:T(8,128)(2,1)S(1)}, bf16[256,256]{1,0:T(8,128)(2,1)S(1)}, u32[]{:S(2)}, u32[]{:S(2)}) %collective-permute-start.21) | collective-permute-done | bytes 131104 | tf_op jit(solution)/shard_map/ppermute | solution.py:169
  75.0 2.7 %collective-permute-done.23.rest_3_ = bf16[256,256]{1,0:T(8,128)(2,1)S(1)} collective-permute-done((bf16[256,256]{1,0:T(8,128)(2,1)S(1)}, bf16[256,256]{1,0:T(8,128)(2,1)S(1)}, u32[]{:S(2)}, u32[]{:S(2)}) %collective-permute-start.23) | collective-permute-done | bytes 131104 | tf_op jit(solution)/shard_map/ppermute | solution.py:169
  77.7 4.9 %attend.2.rest_4_ = bf16[256,4096]{1,0:T(8,128)(2,1)} custom-call(s32[1]{0:T(128)} %bitcast.place, s32[2]{0:T(128)S(1)} %get-tuple-element.39.needs, bf16[256,4096]{1,0:T(8,128)(2,1)S(1)} %bitcast.31, f32[256,512]{1,0:T(8,128)S(1)} %get-tuple-element.40.bias, bf16[256,256]{1,0:T(8,128)(2,1)S(1)} %get-tuple-element.53.rest_0_, ...), custom_call_target="tpu_custom_call" | custom-call | flops 1073741824 | bytes 2097152 | tf_op jit(solution)/shard_map/attend/pallas_call | solution.py:291
  82.7 4.8 %attend.3 = bf16[256,4096]{1,0:T(8,128)(2,1)} custom-call(s32[1]{0:T(128)} %bitcast.place, s32[2]{0:T(128)S(1)} %get-tuple-element.39.needs, bf16[256,4096]{1,0:T(8,128)(2,1)S(1)} %bitcast.32, f32[256,512]{1,0:T(8,128)S(1)} %get-tuple-element.40.bias, bf16[256,256]{1,0:T(8,128)(2,1)S(1)} %get-tuple-element.51.rest_0_, ...), custom_call_target="tpu_custom_call", output_to_operand_aliasing={{}: (8, {})} | custom-call | flops 1073741824 | bytes 2097152 | tf_op jit(solution)/shard_map/attend/pallas_call | solution.py:291
  (40 shorter events, 0.2 us)
Async XLA Ops:
  0.0 7.6 %copy-start.4 = (f32[5120]{0:T(1024)S(1)}, f32[5120]{0:T(1024)}, u32[]{:S(2)}) copy-start(f32[5120]{0:T(1024)} %param.11) | copy-start | bytes 61444
  1.3 1.8 %collective-permute-start = (bf16[2,320,256]{2,1,0:T(8,128)(2,1)S(1)}, bf16[2,320,256]{2,1,0:T(8,128)(2,1)S(1)}, u32[]{:S(2)}, u32[]{:S(2)}) collective-permute-start(bf16[2,320,256]{2,1,0:T(8,128)(2,1)S(1)} %pad_maximum_fusion), channel_id=1, source_target_pairs={{0,2},{2,0},{1,3},{3,1},{4,6},{6,4},{5,7},{7,5},{8,10},{10,8},{9,1... | collective-permute-start | bytes 983048 | tf_op jit(solution)/shard_map/ppermute | solution.py:146
  3.1 13.1 %collective-permute-start.1 = (bf16[640,256]{1,0:T(8,128)(2,1)S(1)}, bf16[640,256]{1,0:T(8,128)(2,1)}, u32[]{:S(2)}, u32[]{:S(2)}) collective-permute-start(bf16[640,256]{1,0:T(8,128)(2,1)S(1)} %get-tuple-element.31.rest_0_), channel_id=1, source_target_pairs={{0,8},{8,16},{16,24},{24,0},{1,9},{9,17},{17,25},{25,1},{2,10},{10... | collective-permute-start | bytes 983048 | tf_op jit(solution)/shard_map/ppermute | solution.py:226
  6.1 10.1 %collective-permute-start.2 = (bf16[640,256]{1,0:T(8,128)(2,1)S(1)}, bf16[640,256]{1,0:T(8,128)(2,1)S(1)}, u32[]{:S(2)}, u32[]{:S(2)}) collective-permute-start(bf16[640,256]{1,0:T(8,128)(2,1)S(1)} %get-tuple-element.31.rest_0_), channel_id=1, source_target_pairs={{0,4},{4,0},{1,5},{5,1},{2,6},{6,2},{3,7},{7,3},{8,12},{12,8},{9,1... | collective-permute-start | bytes 983048 | tf_op jit(solution)/shard_map/ppermute | solution.py:146
  7.6 1.7 %copy-start.1 = (bf16[1,256,5120]{2,1,0:T(8,128)(2,1)S(1)}, bf16[1,256,5120]{2,1,0:T(8,128)(2,1)}, u32[]{:S(2)}) copy-start(bf16[1,256,5120]{2,1,0:T(8,128)(2,1)} %param.9) | copy-start | bytes 7864324
  9.4 11.5 %copy-start.6 = (s32[1,256]{1,0:T(1,128)S(1)}, s32[1,256]{1,0:T(1,128)}, u32[]{:S(2)}) copy-start(s32[1,256]{1,0:T(1,128)} %param.16) | copy-start | bytes 3076
  9.4 11.5 %copy-start.7 = (s32[1,256]{1,0:T(1,128)S(1)}, s32[1,256]{1,0:T(1,128)}, u32[]{:S(2)}) copy-start(s32[1,256]{1,0:T(1,128)} %param.15) | copy-start | bytes 3076
  16.3 0.7 copy-start.2
  17.0 37.2 %collective-permute-start.10 = (bf16[8,256,640]{2,1,0:T(8,128)(2,1)S(1)}, bf16[8,256,640]{2,1,0:T(8,128)(2,1)}, u32[]{:S(2)}, u32[]{:S(2)}) collective-permute-start(bf16[8,256,640]{2,1,0:T(8,128)(2,1)S(1)} %norm.1.own), channel_id=1, source_target_pairs={{0,2},{2,0},{1,3},{3,1},{4,6},{6,4},{5,7},{7,5},{8,10},{10,8},{9,1... | collective-permute-start | bytes 7864328 | tf_op jit(solution)/shard_map/ppermute | solution.py:146
  17.0 13.1 %collective-permute-start.3 = (bf16[640,256]{1,0:T(8,128)(2,1)}, bf16[640,256]{1,0:T(8,128)(2,1)}, u32[]{:S(2)}, u32[]{:S(2)}) collective-permute-start(bf16[640,256]{1,0:T(8,128)(2,1)} %collective-permute-done.1.rest_3_), channel_id=1, source_target_pairs={{0,8},{8,16},{16,24},{24,0},{1,9},{9,17},{17,25},{25,1},{2,10},{10... | collective-permute-start | bytes 983048 | tf_op jit(solution)/shard_map/ppermute | solution.py:226
  17.9 12.2 %collective-permute-start.4 = (bf16[640,256]{1,0:T(8,128)(2,1)}, bf16[640,256]{1,0:T(8,128)(2,1)}, u32[]{:S(2)}, u32[]{:S(2)}) collective-permute-start(bf16[640,256]{1,0:T(8,128)(2,1)} %collective-permute-done.1.rest_3_), channel_id=1, source_target_pairs={{0,4},{4,0},{1,5},{5,1},{2,6},{6,2},{3,7},{7,3},{8,12},{12,8},{9,1... | collective-permute-start | bytes 983048 | tf_op jit(solution)/shard_map/ppermute | solution.py:146
  19.4 10.6 %collective-permute-start.5 = (bf16[640,256]{1,0:T(8,128)(2,1)}, bf16[640,256]{1,0:T(8,128)(2,1)}, u32[]{:S(2)}, u32[]{:S(2)}) collective-permute-start(bf16[640,256]{1,0:T(8,128)(2,1)} %collective-permute-done.1.rest_3_), channel_id=1, source_target_pairs={{0,1},{1,0},{2,3},{3,2},{4,5},{5,4},{6,7},{7,6},{8,9},{9,8},{10,11... | collective-permute-start | bytes 983048 | tf_op jit(solution)/shard_map/ppermute | solution.py:146
  20.9 8.4 %collective-permute-start.9 = (s32[2,256]{1,0:T(2,128)S(1)}, s32[2,256]{1,0:T(2,128)}, u32[]{:S(2)}, u32[]{:S(2)}) collective-permute-start(s32[2,256]{1,0:T(2,128)S(1)} %pad_add_fusion), channel_id=1, source_target_pairs={{0,1},{1,0},{2,3},{3,2},{4,5},{5,4},{6,7},{7,6},{8,9},{9,8},{10,11... | collective-permute-start | bytes 6152 | tf_op jit(solution)/shard_map/ppermute | solution.py:169
  29.3 14.2 %collective-permute-start.17 = (s32[1,256]{1,0:T(1,128)S(1)}, s32[1,256]{1,0:T(1,128)}, u32[]{:S(2)}, u32[]{:S(2)}) collective-permute-start(s32[1,256]{1,0:T(1,128)S(1)} %copy-done.6), channel_id=1, source_target_pairs={{0,2},{2,0},{1,3},{3,1},{4,6},{6,4},{5,7},{7,5},{8,10},{10,8},{9,1... | collective-permute-start | bytes 3080 | tf_op jit(solution)/shard_map/ppermute | solution.py:146
  30.0 25.8 %copy-start.3 = (bf16[640,256]{1,0:T(8,128)(2,1)S(1)}, bf16[640,256]{1,0:T(8,128)(2,1)}, u32[]{:S(2)}) copy-start(bf16[640,256]{1,0:T(8,128)(2,1)} %copy-done.2) | copy-start | bytes 983044
  30.1 12.2 %collective-permute-start.6 = (bf16[640,256]{1,0:T(8,128)(2,1)}, bf16[640,256]{1,0:T(8,128)(2,1)S(1)}, u32[]{:S(2)}, u32[]{:S(2)}) collective-permute-start(bf16[640,256]{1,0:T(8,128)(2,1)} %collective-permute-done.3.rest_6_), channel_id=1, source_target_pairs={{0,8},{8,16},{16,24},{24,0},{1,9},{9,17},{17,25},{25,1},{2,10},{10... | collective-permute-start | bytes 983048 | tf_op jit(solution)/shard_map/ppermute | solution.py:226
  31.7 10.6 %collective-permute-start.7 = (bf16[640,256]{1,0:T(8,128)(2,1)}, bf16[640,256]{1,0:T(8,128)(2,1)S(1)}, u32[]{:S(2)}, u32[]{:S(2)}) collective-permute-start(bf16[640,256]{1,0:T(8,128)(2,1)} %collective-permute-done.3.rest_6_), channel_id=1, source_target_pairs={{0,4},{4,0},{1,5},{5,1},{2,6},{6,2},{3,7},{7,3},{8,12},{12,8},{9,1... | collective-permute-start | bytes 983048 | tf_op jit(solution)/shard_map/ppermute | solution.py:146
  32.2 10.1 %collective-permute-start.8 = (bf16[640,256]{1,0:T(8,128)(2,1)}, bf16[640,256]{1,0:T(8,128)(2,1)S(1)}, u32[]{:S(2)}, u32[]{:S(2)}) collective-permute-start(bf16[640,256]{1,0:T(8,128)(2,1)} %collective-permute-done.3.rest_6_), channel_id=1, source_target_pairs={{0,1},{1,0},{2,3},{3,2},{4,5},{5,4},{6,7},{7,6},{8,9},{9,8},{10,11... | collective-permute-start | bytes 983048 | tf_op jit(solution)/shard_map/ppermute | solution.py:146
  42.2 10.6 %collective-permute-start.11 = (bf16[640,256]{1,0:T(8,128)(2,1)S(1)}, bf16[640,256]{1,0:T(8,128)(2,1)S(1)}, u32[]{:S(2)}, u32[]{:S(2)}) collective-permute-start(bf16[640,256]{1,0:T(8,128)(2,1)S(1)} %collective-permute-done.6.rest_9_), channel_id=1, source_target_pairs={{0,4},{4,0},{1,5},{5,1},{2,6},{6,2},{3,7},{7,3},{8,12},{12,8},{9,1... | collective-permute-start | bytes 983048 | tf_op jit(solution)/shard_map/ppermute | solution.py:146
  44.2 16.0 %collective-permute-start.14 = (bf16[640,256]{1,0:T(8,128)(2,1)S(1)}, bf16[640,256]{1,0:T(8,128)(2,1)S(1)}, u32[]{:S(2)}, u32[]{:S(2)}) collective-permute-start(bf16[640,256]{1,0:T(8,128)(2,1)S(1)} %collective-permute-done.6.rest_9_), channel_id=1, source_target_pairs={{0,1},{1,0},{2,3},{3,2},{4,5},{5,4},{6,7},{7,6},{8,9},{9,8},{10,11... | collective-permute-start | bytes 983048 | tf_op jit(solution)/shard_map/ppermute | solution.py:146
  45.7 16.2 %collective-permute-start.15 = (bf16[640,256]{1,0:T(8,128)(2,1)}, bf16[640,256]{1,0:T(8,128)(2,1)S(1)}, u32[]{:S(2)}, u32[]{:S(2)}) collective-permute-start(bf16[640,256]{1,0:T(8,128)(2,1)} %copy-done.2), channel_id=1, source_target_pairs={{0,1},{1,0},{2,3},{3,2},{4,5},{5,4},{6,7},{7,6},{8,9},{9,8},{10,11... | collective-permute-start | bytes 983048 | tf_op jit(solution)/shard_map/ppermute | solution.py:146
  46.2 15.6 %collective-permute-start.16 = (bf16[640,256]{1,0:T(8,128)(2,1)}, bf16[640,256]{1,0:T(8,128)(2,1)S(1)}, u32[]{:S(2)}, u32[]{:S(2)}) collective-permute-start(bf16[640,256]{1,0:T(8,128)(2,1)} %collective-permute-done.5.rest_4_), channel_id=1, source_target_pairs={{0,4},{4,0},{1,5},{5,1},{2,6},{6,2},{3,7},{7,3},{8,12},{12,8},{9,1... | collective-permute-start | bytes 983048 | tf_op jit(solution)/shard_map/ppermute | solution.py:146
  52.9 12.8 %collective-permute-start.12 = (bf16[640,256]{1,0:T(8,128)(2,1)S(1)}, bf16[640,256]{1,0:T(8,128)(2,1)S(1)}, u32[]{:S(2)}, u32[]{:S(2)}) collective-permute-start(bf16[640,256]{1,0:T(8,128)(2,1)S(1)} %collective-permute-done.8.rest_7_), channel_id=1, source_target_pairs={{0,4},{4,0},{1,5},{5,1},{2,6},{6,2},{3,7},{7,3},{8,12},{12,8},{9,1... | collective-permute-start | bytes 983048 | tf_op jit(solution)/shard_map/ppermute | solution.py:146
  54.1 12.5 %collective-permute-start.13 = (bf16[640,256]{1,0:T(8,128)(2,1)S(1)}, bf16[640,256]{1,0:T(8,128)(2,1)S(1)}, u32[]{:S(2)}, u32[]{:S(2)}) collective-permute-start(bf16[640,256]{1,0:T(8,128)(2,1)S(1)} %collective-permute-done.11.rest_1_), channel_id=1, source_target_pairs={{0,1},{1,0},{2,3},{3,2},{4,5},{5,4},{6,7},{7,6},{8,9},{9,8},{10,11... | collective-permute-start | bytes 983048 | tf_op jit(solution)/shard_map/ppermute | solution.py:146
  60.1 6.5 %copy-start.5 = (f32[128]{0:T(128)S(1)}, f32[128]{0:T(128)}, u32[]{:S(2)}) copy-start(f32[128]{0:T(128)} %param.12) | copy-start | bytes 1540
  66.7 11.1 %copy-start = (bf16[1,256,4096]{2,1,0:T(8,128)(2,1)S(1)}, bf16[1,256,4096]{2,1,0:T(8,128)(2,1)}, u32[]{:S(2)}) copy-start(bf16[1,256,4096]{2,1,0:T(8,128)(2,1)} %param.10) | copy-start | bytes 6291460
  69.5 5.5 %collective-permute-start.21 = (bf16[256,256]{1,0:T(8,128)(2,1)S(1)}, bf16[256,256]{1,0:T(8,128)(2,1)S(1)}, u32[]{:S(2)}, u32[]{:S(2)}) collective-permute-start(bf16[256,256]{1,0:T(8,128)(2,1)S(1)} %get-tuple-element.53.rest_0_), channel_id=1, source_target_pairs={{0,1},{1,0},{2,3},{3,2},{4,5},{5,4},{6,7},{7,6},{8,9},{9,8},{10,11... | collective-permute-start | bytes 393224 | tf_op jit(solution)/shard_map/ppermute | solution.py:169
  71.0 4.0 %collective-permute-start.22 = (bf16[256,256]{1,0:T(8,128)(2,1)S(1)}, bf16[256,256]{1,0:T(8,128)(2,1)S(1)}, u32[]{:S(2)}, u32[]{:S(2)}) collective-permute-start(bf16[256,256]{1,0:T(8,128)(2,1)S(1)} %get-tuple-element.54), channel_id=1, source_target_pairs={{0,2},{1,3},{2,0},{3,1},{4,6},{5,7},{6,4},{7,5},{8,10},{9,11},{10,... | collective-permute-start | bytes 393224 | tf_op jit(solution)/shard_map/ppermute | solution.py:169
  71.0 6.7 %collective-permute-start.23 = (bf16[256,256]{1,0:T(8,128)(2,1)S(1)}, bf16[256,256]{1,0:T(8,128)(2,1)S(1)}, u32[]{:S(2)}, u32[]{:S(2)}) collective-permute-start(bf16[256,256]{1,0:T(8,128)(2,1)S(1)} %get-tuple-element.54), channel_id=1, source_target_pairs={{0,3},{1,2},{2,1},{3,0},{4,7},{5,6},{6,5},{7,4},{8,11},{9,10},{10,... | collective-permute-start | bytes 393224 | tf_op jit(solution)/shard_map/ppermute | solution.py:169
  71.7 11.0 %collective-permute-start.18 = (bf16[256,256]{1,0:T(8,128)(2,1)S(1)}, bf16[256,256]{1,0:T(8,128)(2,1)S(1)}, u32[]{:S(2)}, u32[]{:S(2)}) collective-permute-start(bf16[256,256]{1,0:T(8,128)(2,1)S(1)} %get-tuple-element.51.rest_0_), channel_id=1, source_target_pairs={{0,1},{1,0},{2,3},{3,2},{4,5},{5,4},{6,7},{7,6},{8,9},{9,8},{10,11... | collective-permute-start | bytes 393224 | tf_op jit(solution)/shard_map/ppermute | solution.py:169
  73.2 9.5 %collective-permute-start.19 = (bf16[256,256]{1,0:T(8,128)(2,1)S(1)}, bf16[256,256]{1,0:T(8,128)(2,1)S(1)}, u32[]{:S(2)}, u32[]{:S(2)}) collective-permute-start(bf16[256,256]{1,0:T(8,128)(2,1)S(1)} %get-tuple-element.52), channel_id=1, source_target_pairs={{0,2},{1,3},{2,0},{3,1},{4,6},{5,7},{6,4},{7,5},{8,10},{9,11},{10,... | collective-permute-start | bytes 393224 | tf_op jit(solution)/shard_map/ppermute | solution.py:169
  75.0 7.7 %collective-permute-start.20 = (bf16[256,256]{1,0:T(8,128)(2,1)S(1)}, bf16[256,256]{1,0:T(8,128)(2,1)S(1)}, u32[]{:S(2)}, u32[]{:S(2)}) collective-permute-start(bf16[256,256]{1,0:T(8,128)(2,1)S(1)} %get-tuple-element.52), channel_id=1, source_target_pairs={{0,3},{1,2},{2,1},{3,0},{4,7},{5,6},{6,5},{7,4},{8,11},{9,10},{10,... | collective-permute-start | bytes 393224 | tf_op jit(solution)/shard_map/ppermute | solution.py:169
where the time goes:
time: 87.7 us; the launch traced here: 87.4 us
  waiting for transfers between devices  33.9 us (39%)
  starting transfers between devices  23.7 us (27%)
  Pallas kernels  22.2 us (25%)
  local copies, waits for them, and re-layouts  4.81 us (5%)
  other arithmetic  2.69 us (3%)
    ppermute x14, starting transfers between devices, swap(): return lax.ppermute(array, axis, [(0, 1), (1, 0)])  13.9 us
    ppermute x3, waiting for transfers between devices, on_device(): arrived = lax.ppermute(mine[-1], 'z', ring)  12.8 us
    ppermute x7, waiting for transfers between devices, along_ctx(): return lax.ppermute(array, ('core', 'ctx', 'x'), pairs)  12 us
    pallas_call x3, Pallas kernels, on_device(): pl.pallas_call(functools.partial(project_kernel, chips_z, items, first, l...  9.85 us
    pallas_call x2, Pallas kernels, on_device(): pl.pallas_call(functools.partial(attend_kernel, m, count), out_shape=jax....  9.7 us
    ppermute x14, waiting for transfers between devices, swap(): return lax.ppermute(array, axis, [(0, 1), (1, 0)])  9.14 us
    ppermute x3, starting transfers between devices, on_device(): arrived = lax.ppermute(mine[-1], 'z', ring)  5.53 us
    ppermute x7, starting transfers between devices, along_ctx(): return lax.ppermute(array, ('core', 'ctx', 'x'), pairs)  4.3 us
  transfers between devices with their start and end apart: 24, of which 10 were waited for; matrix products, arithmetic and copies ran while one was open for 4% of the time, Pallas kernels for 17%

commit v1 on v0

--- a/solution.py
+++ b/solution.py
@@ -31,7 +31,10 @@
 
 def project_kernel(chips_z, items, first, last, count, place, own, other, *rest):
     z, y, x = place[0], place[1], place[2]
-    pieces, rest = dict(zip(items, rest)), rest[len(items) :]
+    pieces, rest = {}, list(rest)
+    for item in items:
+        halves = 2 if item == (chips_z // 2, "corner") else 1
+        pieces[item] = jnp.concatenate([rest.pop(0)[...] for _ in range(halves)], axis=0)
     terms = {}
     for k in range(chips_z):
         p = lax.rem(z - k + chips_z, chips_z)
@@ -45,7 +48,7 @@
                     continue
                 if rows is None:
                     rows = jnp.concatenate([own[chunk], other[chunk]], axis=0)
-                part = jnp.dot(rows, pieces[k, kind][...], preferred_element_type=jnp.float32)
+                part = jnp.dot(rows, pieces[k, kind], preferred_element_type=jnp.float32)
                 terms[side] = terms[side] + part if side in terms else part
     acc = rest[-1]
     for side, at in ((0, x), (1, 1 - x)):
@@ -84,23 +87,17 @@
         needs[tile] = found[0].astype(jnp.int32) + 2 * found[1].astype(jnp.int32)
 
 
-def attend_kernel(pieces, count, place, needs, queries, bias, *rest):
-    sources, (out, keys, values) = rest[: 2 * pieces], rest[-3:]
-    step = pl.program_id(0)
+def attend_kernel(lefts, count, place, needs, queries, bias, *rest):
+    pieces = len(lefts)
+    sources, (out, keys, values) = rest[:pieces], rest[-3:]
     tile_rows = count // 2
     length = pieces * tile_rows
-
-    for at in range(2):
-
-        @pl.when(step == at)
-        def _():
-            for i in range(pieces):
-                source = sources[at * pieces + i]
-                for half in range(2):
-                    here = slice(half * tile_rows, (half + 1) * tile_rows)
-                    there = half * length + i * tile_rows
-                    keys[there : there + tile_rows, :] = source[here, :HD]
-                    values[there : there + tile_rows, :] = source[here, HD:]
+    for i, (left, source) in enumerate(zip(lefts, sources)):
+        for half in range(2):
+            here = slice(half * tile_rows, (half + 1) * tile_rows)
+            there = half * length + i * tile_rows
+            keys[there : there + tile_rows, :] = source[here, left : left + HD]
+            values[there : there + tile_rows, :] = source[here, left + HD : left + 2 * HD]
 
     factor = math.log2(math.e) / math.sqrt(HD)
 
@@ -180,9 +177,9 @@
         jnp.zeros((2, rows, 2 * HD), bf16), kept, (0, core * own_rows, 0)
     )
     chip = lax.dynamic_update_slice(chip, taken, (0, (1 - core) * own_rows, 0))
-    mine = [lax.dynamic_index_in_dim(chip, x, 0, keepdims=False)]
-    across = [lax.dynamic_index_in_dim(chip, 1 - x, 0, keepdims=False)]
-    hidden, mine[0], across[0] = lax.optimization_barrier((hidden, mine[0], across[0]))
+    half_x = lax.dynamic_index_in_dim(chip, x, 0, keepdims=False)
+    half_o = lax.dynamic_index_in_dim(chip, 1 - x, 0, keepdims=False)
+    hidden, half_x, half_o = lax.optimization_barrier((hidden, half_x, half_o))
     normed = pl.pallas_call(
         functools.partial(norm_kernel, chunks),
         out_shape=jax.ShapeDtypeStruct((chunks, count, rows), bf16),
@@ -195,9 +192,38 @@
         ),
         name="norm",
     )(hidden[0], norm_gain[None])
-    ints = jnp.concatenate([segment, position])
-    ints_all = [ints] + [along_ctx(ints, d) for d in range(1, m)]
-    where = jnp.concatenate([position[0], swap(position, "core")[0]]).astype(jnp.float32)
+    def ring(array, step):
+        return lax.ppermute(array, "z", [(i, (i + step) % chips_z) for i in range(chips_z)])
+
+    middle = chips_z // 2
+    mine, across, beside, corner = {0: half_x}, {0: half_o}, {}, {}
+    beside[0] = swap(mine[0], "y")
+    for r in range(1, middle + 1):
+        arrived = [r] if r == middle else [r, chips_z - r]
+        for k in arrived:
+            mine[k] = ring(mine[k - 1], 1) if k == r else ring(mine[(k + 1) % chips_z], -1)
+        if r == 1:
+            tied = (beside[0], segment, position)
+            beside[0], segment, position = lax.optimization_barrier(tied)
+            corner[0] = swap(beside[0], "x")
+            ints = jnp.concatenate([segment, position])
+            ints_all = [ints] + [along_ctx(ints, d) for d in range(1, m)]
+            position_other = swap(position, "core")
+            tied = (mine[1], mine[chips_z - 1], corner[0], normed, position_other, ints_all)
+            tied = lax.optimization_barrier(tied)
+            mine[1], mine[chips_z - 1], corner[0], normed, position_other, ints_all = tied
+        elif r == middle:
+            tied = (mine[r], across[r - 1], beside[chips_z - r + 1])
+            mine[r], across[r - 1], beside[chips_z - r + 1] = lax.optimization_barrier(tied)
+        for k in arrived:
+            beside[k], across[k] = swap(mine[k], "y"), swap(mine[k], "x")
+    for k in range(1, chips_z):
+        if k < middle:
+            corner[k] = swap(across[k], "y")
+        elif k > middle:
+            corner[k] = swap(beside[k], "x")
+    normed_other = swap(normed, "core")
+    where = jnp.concatenate([position[0], position_other[0]]).astype(jnp.float32)
     half = HD // 2
     freq = np.exp(np.arange(half, dtype=np.float32) * np.float32(-2.0 * math.log(THETA) / HD))
     angle = where[:, None] * freq[None, :]
@@ -219,50 +245,32 @@
         name="mask",
     )(segment.reshape(count, 1), position.reshape(count, 1), order[:1], order[1:])
 
-    ring = [(i, (i + 1) % chips_z) for i in range(chips_z)]
-    end = chips_z - 1
-    beside = [swap(mine[0], "y")]
-    for k in range(1, chips_z):
-        arrived = lax.ppermute(mine[-1], "z", ring)
-        if k == 1:
-            normed, arrived, beside[0] = lax.optimization_barrier(
-                (normed, arrived, beside[0])
-            )
-        else:
-            arrived, beside[k - 1], across[k - 1] = lax.optimization_barrier(
-                (arrived, beside[k - 1], across[k - 1])
-            )
-        if k == end:
-            arrived, beside[0], across[1], bias, needs = lax.optimization_barrier(
-                (arrived, beside[0], across[1], bias, needs)
-            )
-        mine.append(arrived)
-        beside.append(swap(arrived, "y"))
-        across.append(swap(arrived, "x"))
-    corner = {0: swap(beside[0], "x"), 1: swap(across[1], "y")}
-    tied = lax.optimization_barrier((beside[end], *across[2:end]))
-    beside[end], across[2:end] = tied[0], list(tied[1:])
-    for k in range(2, chips_z):
-        corner[k] = swap(beside[k], "x") if k == end or k % 2 else swap(across[k], "y")
-
-    normed_other = swap(normed, "core")
 
     place = jnp.stack([z, y, x]).astype(jnp.int32)
     acc_shape = jax.ShapeDtypeStruct((2, 2 * count, 2 * HD), jnp.float32)
     kv_shape = jax.ShapeDtypeStruct((count, 2 * HD), bf16)
     kinds = dict(mine=mine, across=across, beside=beside, corner=corner)
     every = [(k, kind) for k in range(chips_z) for kind in kinds]
-    final = [(k, "corner") for k in range(2, chips_z)]
-    late = [(end, "across"), (end, "beside"), (0, "corner"), (1, "corner")]
+    final = [(middle, "corner")]
+    late = [(middle, "beside"), (middle, "across")]
+    late += [(k, "corner") for k in range(1, chips_z) if k != middle]
     early = [item for item in every if item not in final + late]
     acc = []
     for items in (early, late, final):
         first, last = items is early, items is final
+        if items is late:
+            tied = (beside[middle], across[middle], acc[0], bias, needs)
+            tied = lax.optimization_barrier(tied)
+            beside[middle], across[middle], acc[0], bias, needs = tied
+            corner[middle] = (
+                swap(beside[middle][: rows // 2], "x"), swap(across[middle][rows // 2 :], "y")
+            )
+        arrays = jax.tree.leaves([kinds[kind][k] for k, kind in items])
         outs = pl.pallas_call(
             functools.partial(project_kernel, chips_z, items, first, last, count),
             out_shape=[kv_shape] * 4 if last else [acc_shape],
             in_specs=[pl.BlockSpec(memory_space=pltpu.SMEM)]
-            + [whole] * (2 + len(items) + len(acc) + (3 if last else 0)),
+            + [whole] * (2 + len(arrays) + len(acc) + (3 if last else 0)),
             out_specs=[whole] * (4 if last else 1),
             scratch_shapes=[pltpu.VMEM(acc_shape.shape, acc_shape.dtype)] * int(last),
             compiler_params=params,
@@ -273,29 +281,32 @@
             ),
             name="project",
         )(
-            place, normed, normed_other, *[kinds[kind][k] for k, kind in items], *acc,
+            place, normed, normed_other, *arrays, *acc,
             *((cosine, sine, key_gain[None]) if last else ()),
         )
         acc = [outs[-1]]
 
+    beyond = [[kv] + [along_ctx(kv, d) for d in range(1, m)] for kv in (outs[0], outs[2])]
+    joined = jnp.concatenate([outs[1], outs[3]], axis=1)
+    local = along_ctx(joined, 0, True)
+    beyond += [[local] + [along_ctx(kv, d, True) for d in range(1, m)] for kv in (outs[1], outs[3])]
     result = None
-    for s in range(2):
-        kv_own, kv_other = outs[2 * s], outs[2 * s + 1]
-        sources = [kv_own] + [along_ctx(kv_own, d) for d in range(1, m)]
-        sources += [along_ctx(kv_other, d, True) for d in range(m)]
-
-        def block(step, place, needs, s=s):
-            return (0, lax.rem(place[0] + step, 2) * 2 + s)
+    for step, sources in enumerate(beyond):
+
+        def block(i, place, needs, step=step):
+            return (0, lax.rem(place[0] + step // 2, 2) * 2 + step % 2)
 
         earlier = [] if result is None else [result]
         result = pl.pallas_call(
-            functools.partial(attend_kernel, m, count),
+            functools.partial(
+                attend_kernel, [2 * HD * (step % 2) if a is local else 0 for a in sources], count
+            ),
             out_shape=jax.ShapeDtypeStruct((count, KVH * G * HD), bf16),
             grid_spec=pltpu.PrefetchScalarGridSpec(
                 num_scalar_prefetch=2,
-                grid=(2,),
+                grid=(1,),
                 in_specs=[pl.BlockSpec((count, G * HD), block)]
-                + [whole] * (1 + 2 * m)
+                + [whole] * (1 + m)
                 + [pl.BlockSpec(memory_space=pl.ANY)] * len(earlier),
                 out_specs=pl.BlockSpec((count, G * HD), block),
                 scratch_shapes=[
@@ -303,12 +314,12 @@
                     pltpu.VMEM((m * count, HD), bf16),
                 ],
             ),
-            input_output_aliases={4 + 2 * m: 0} if earlier else {},
+            input_output_aliases={4 + m: 0} if earlier else {},
             compiler_params=params,
             cost_estimate=pl.CostEstimate(
-                flops=2 * count * m * count * KVH * G * HD,
-                bytes_accessed=2 * count * KVH * G * HD,
-                transcendentals=count * m * count * KVH * G // 2,
+                flops=count * m * count * KVH * G * HD,
+                bytes_accessed=count * KVH * G * HD,
+                transcendentals=count * m * count * KVH * G // 4,
             ),
             name="attend",
         )(core.astype(jnp.int32)[None], needs, queries[0], bias, *sources, *earlier)

time: 87.7 us -> 87.8 us (level)
  waiting for transfers between devices: 33.9 us -> 24.2 us
  local copies, waits for them, and re-layouts: 4.81 us -> 9.97 us
  Pallas kernels: 22.2 us -> 24.6 us
  starting transfers between devices: 23.7 us -> 24.9 us
    ppermute x7 -> x6, waiting for transfers between devices: 12 us -> 2.54 us  [along_ctx(): return lax.ppermute(array, ('core', 'ctx', 'x'), pairs)]
    ppermute x3, waiting for transfers between devices: 12.8 us -> 8.08 us  [ring(): lax.ppermute(array, 'z', [(i, (i + step) % chips_z) for i in range(chips_...]
    unnamed x16 -> x32, local copies, waits for them, and re-layouts: 2.49 us -> 7.08 us
    ppermute x14 -> x15, waiting for transfers between devices: 9.14 us -> 13.5 us  [swap(): return lax.ppermute(array, axis, [(0, 1), (1, 0)])]
    pallas_call x2 -> x4, Pallas kernels: 9.7 us -> 12.2 us  [on_device(): pl.pallas_call(functools.partial(attend_kernel, [2 * HD * (step % 2) if a...]
    ppermute x14 -> x15, starting transfers between devices: 13.9 us -> 15.6 us  [swap(): return lax.ppermute(array, axis, [(0, 1), (1, 0)])]
    ppermute x7 -> x6, starting transfers between devices: 4.3 us -> 4.29 us  [along_ctx(): return lax.ppermute(array, ('core', 'ctx', 'x'), pairs)]
  transfers between devices with their start and end apart: 24 -> 24, of which waited for: 10 -> 8; matrix products, arithmetic and copies ran while one was open for 4% -> 6% of each run, Pallas kernels for 17% -> 22%
where the time goes in v1:
time: 87.8 us; the launch traced here: 87.4 us
  starting transfers between devices  24.9 us (28%)
  Pallas kernels  24.6 us (28%)
  waiting for transfers between devices  24.2 us (28%)
  local copies, waits for them, and re-layouts  9.97 us (11%)
  other arithmetic  3.44 us (4%)
    ppermute x15, starting transfers between devices, swap(): return lax.ppermute(array, axis, [(0, 1), (1, 0)])  15.6 us
    ppermute x15, waiting for transfers between devices, swap(): return lax.ppermute(array, axis, [(0, 1), (1, 0)])  13.5 us
    pallas_call x4, Pallas kernels, on_device(): pl.pallas_call(functools.partial(attend_kernel, [2 * HD * (step % 2) if a...  12.2 us
    pallas_call x3, Pallas kernels, on_device(): pl.pallas_call(functools.partial(project_kernel, chips_z, items, first, l...  9.83 us
    ppermute x3, waiting for transfers between devices, ring(): lax.ppermute(array, 'z', [(i, (i + step) % chips_z) for i in range(chips_...  8.08 us
    unnamed x32, local copies, waits for them, and re-layouts  7.08 us
    ppermute x3, starting transfers between devices, ring(): lax.ppermute(array, 'z', [(i, (i + step) % chips_z) for i in range(chips_...  5.01 us
    ppermute x6, starting transfers between devices, along_ctx(): return lax.ppermute(array, ('core', 'ctx', 'x'), pairs)  4.29 us
  transfers between devices with their start and end apart: 24, of which 8 were waited for; matrix products, arithmetic and copies ran while one was open for 6% of the time, Pallas kernels for 22%

profile of v1, /device:TPU:0, one launch (start us, length us, event | category | flops | bytes accessed | tf_op | source)
XLA Modules:
  0.0 87.4 jit_solution(9502795630568902445)
XLA Ops:
  0.0 1.2 %dynamic-slice_bitcast_fusion.2 = (bf16[1,320,256]{2,1,0:T(8,128)(2,1)S(1)}, bf16[1,320,256]{2,1,0:T(8,128)(2,1)S(1)}, bf16[1,320,256]{2,1,0:T(8,128)(2,1)S(1)}, bf16[1,320,256]{2,1,0:T(8,128)(2,1)S(1)}) fusion(bf16[320,512]{1,0:T(8,128)(2,1)} %param.14, s32[]{:T(128)S(6)} %select_n.23, s32[]{:T(128)S(6)} %select_n.21, bf16[320,512]{1,0:T(8,128)(2,1)} %param.13), kind=kLoop, calls=%fused_computation.9 | loop fusion | bytes 1310728 | tf_op jit(solution)/shard_map/stack | solution.py:170
  1.3 0.5 collective-permute-start
  1.9 1.2 %collective-permute-done = bf16[2,320,256]{2,1,0:T(8,128)(2,1)S(1)} collective-permute-done((bf16[2,320,256]{2,1,0:T(8,128)(2,1)S(1)}, bf16[2,320,256]{2,1,0:T(8,128)(2,1)S(1)}, u32[]{:S(2)}, u32[]{:S(2)}) %collective-permute-start) | collective-permute-done | bytes 327712 | tf_op jit(solution)/shard_map/ppermute | solution.py:143
  3.1 3.0 %collective-permute-start.3 = (bf16[640,256]{1,0:T(8,128)(2,1)S(1)}, bf16[640,256]{1,0:T(8,128)(2,1)S(1)}, u32[]{:S(2)}, u32[]{:S(2)}) collective-permute-start(bf16[640,256]{1,0:T(8,128)(2,1)S(1)} %get-tuple-element.32.rest_0_), channel_id=1, source_target_pairs={{0,4},{4,0},{1,5},{5,1},{2,6},{6,2},{3,7},{7,3},{8,12},{12,8},{9,1... | collective-permute-start | bytes 983048 | tf_op jit(solution)/shard_map/ppermute | solution.py:143
  6.1 1.6 %collective-permute-start.1 = (bf16[640,256]{1,0:T(8,128)(2,1)S(1)}, bf16[640,256]{1,0:T(8,128)(2,1)S(1)}, u32[]{:S(2)}, u32[]{:S(2)}) collective-permute-start(bf16[640,256]{1,0:T(8,128)(2,1)S(1)} %get-tuple-element.32.rest_0_), channel_id=1, source_target_pairs={{0,8},{8,16},{16,24},{24,0},{1,9},{9,17},{17,25},{25,1},{2,10},{10... | collective-permute-start | bytes 983048 | tf_op jit(solution)/shard_map/ppermute | solution.py:196
  7.7 2.2 %collective-permute-start.2 = (bf16[640,256]{1,0:T(8,128)(2,1)S(1)}, bf16[640,256]{1,0:T(8,128)(2,1)S(1)}, u32[]{:S(2)}, u32[]{:S(2)}) collective-permute-start(bf16[640,256]{1,0:T(8,128)(2,1)S(1)} %get-tuple-element.32.rest_0_), channel_id=1, source_target_pairs={{0,24},{8,0},{16,8},{24,16},{1,25},{9,1},{17,9},{25,17},{2,26},{10... | collective-permute-start | bytes 983048 | tf_op jit(solution)/shard_map/ppermute | solution.py:196
  9.9 4.2 %collective-permute-done.3.rest_2_ = bf16[640,256]{1,0:T(8,128)(2,1)S(1)} collective-permute-done((bf16[640,256]{1,0:T(8,128)(2,1)S(1)}, bf16[640,256]{1,0:T(8,128)(2,1)S(1)}, u32[]{:S(2)}, u32[]{:S(2)}) %collective-permute-start.3) | collective-permute-done | bytes 327712 | tf_op jit(solution)/shard_map/ppermute | solution.py:143
  14.1 1.7 %collective-permute-start.4 = (bf16[640,256]{1,0:T(8,128)(2,1)S(1)}, bf16[640,256]{1,0:T(8,128)(2,1)S(1)}, u32[]{:S(2)}, u32[]{:S(2)}) collective-permute-start(bf16[640,256]{1,0:T(8,128)(2,1)S(1)} %collective-permute-done.3.rest_2_), channel_id=1, source_target_pairs={{0,1},{1,0},{2,3},{3,2},{4,5},{5,4},{6,7},{7,6},{8,9},{9,8},{10,11... | collective-permute-start | bytes 983048 | tf_op jit(solution)/shard_map/ppermute | solution.py:143
  16.2 1.7 %copy-done.1 = bf16[1,256,5120]{2,1,0:T(8,128)(2,1)S(1)} copy-done((bf16[1,256,5120]{2,1,0:T(8,128)(2,1)S(1)}, bf16[1,256,5120]{2,1,0:T(8,128)(2,1)}, u32[]{:S(2)}) %copy-start.1) | copy-done | bytes 2621464
  18.0 1.8 %norm.1.own = bf16[8,256,640]{2,1,0:T(8,128)(2,1)S(1)} custom-call(bf16[256,5120]{1,0:T(8,128)(2,1)S(1)} %bitcast.35, f32[1,5120]{1,0:T(1,128)S(1)} %bitcast.36), custom_call_target="tpu_custom_call" | custom-call | flops 5242880 | bytes 5242880 | tf_op jit(solution)/shard_map/norm/pallas_call | solution.py:183
  19.8 4.1 %collective-permute-done.2.rest_8_ = bf16[640,256]{1,0:T(8,128)(2,1)S(1)} collective-permute-done((bf16[640,256]{1,0:T(8,128)(2,1)S(1)}, bf16[640,256]{1,0:T(8,128)(2,1)S(1)}, u32[]{:S(2)}, u32[]{:S(2)}) %collective-permute-start.2) | collective-permute-done | bytes 327712 | tf_op jit(solution)/shard_map/ppermute | solution.py:196
  23.9 0.7 copy-done.6
  24.6 0.7 copy-done.8
  25.7 1.2 %collective-permute-start.7 = (bf16[640,256]{1,0:T(8,128)(2,1)}, bf16[640,256]{1,0:T(8,128)(2,1)}, u32[]{:S(2)}, u32[]{:S(2)}) collective-permute-start(bf16[640,256]{1,0:T(8,128)(2,1)} %copy-done.4), channel_id=1, source_target_pairs={{0,8},{8,16},{16,24},{24,0},{1,9},{9,17},{17,25},{25,1},{2,10},{10... | collective-permute-start | bytes 983048 | tf_op jit(solution)/shard_map/ppermute | solution.py:196
  26.9 1.5 %collective-permute-start.8 = (bf16[640,256]{1,0:T(8,128)(2,1)}, bf16[640,256]{1,0:T(8,128)(2,1)}, u32[]{:S(2)}, u32[]{:S(2)}) collective-permute-start(bf16[640,256]{1,0:T(8,128)(2,1)} %copy-done.4), channel_id=1, source_target_pairs={{0,1},{1,0},{2,3},{3,2},{4,5},{5,4},{6,7},{7,6},{8,9},{9,8},{10,11... | collective-permute-start | bytes 983048 | tf_op jit(solution)/shard_map/ppermute | solution.py:143
  28.4 0.7 collective-permute-start.13
  29.1 1.4 %collective-permute-start.9 = (bf16[640,256]{1,0:T(8,128)(2,1)}, bf16[640,256]{1,0:T(8,128)(2,1)}, u32[]{:S(2)}, u32[]{:S(2)}) collective-permute-start(bf16[640,256]{1,0:T(8,128)(2,1)} %copy-done.6), channel_id=1, source_target_pairs={{0,4},{4,0},{1,5},{5,1},{2,6},{6,2},{3,7},{7,3},{8,12},{12,8},{9,1... | collective-permute-start | bytes 983048 | tf_op jit(solution)/shard_map/ppermute | solution.py:143
  30.4 0.7 stack.50
  31.1 0.6 stack.49
  31.7 0.7 add_convert_fusion
  32.4 1.6 %fusion = (f32[512,64]{1,0:T(8,128)S(1)}, f32[512,64]{1,0:T(8,128)S(1)}, f32[512,64]{1,0:T(8,128)S(1)}) fusion(f32[64]{0:T(128)} %constant.47, f32[512]{0:T(512)S(1)} %add_convert_fusion), kind=kLoop, calls=%fused_computation.13 | loop fusion | flops 65536 | bytes 395520 | tf_op jit(solution)/shard_map/neg | solution.py:232
  34.0 4.0 %collective-permute-done.7.rest_7_ = bf16[640,256]{1,0:T(8,128)(2,1)} collective-permute-done((bf16[640,256]{1,0:T(8,128)(2,1)}, bf16[640,256]{1,0:T(8,128)(2,1)}, u32[]{:S(2)}, u32[]{:S(2)}) %collective-permute-start.7) | collective-permute-done | bytes 327712 | tf_op jit(solution)/shard_map/ppermute | solution.py:196
  38.0 1.5 %collective-permute-start.14 = (bf16[640,256]{1,0:T(8,128)(2,1)}, bf16[640,256]{1,0:T(8,128)(2,1)S(1)}, u32[]{:S(2)}, u32[]{:S(2)}) collective-permute-start(bf16[640,256]{1,0:T(8,128)(2,1)} %copy-done.6), channel_id=1, source_target_pairs={{0,1},{1,0},{2,3},{3,2},{4,5},{5,4},{6,7},{7,6},{8,9},{9,8},{10,11... | collective-permute-start | bytes 983048 | tf_op jit(solution)/shard_map/ppermute | solution.py:143
  39.5 0.7 add_bitcast_fusion
  40.2 5.1 %collective-permute-done.9.rest_10_ = bf16[640,256]{1,0:T(8,128)(2,1)} collective-permute-done((bf16[640,256]{1,0:T(8,128)(2,1)}, bf16[640,256]{1,0:T(8,128)(2,1)}, u32[]{:S(2)}, u32[]{:S(2)}) %collective-permute-start.9) | collective-permute-done | bytes 327712 | tf_op jit(solution)/shard_map/ppermute | solution.py:143
  45.3 0.7 collective-permute-start.10
  46.0 0.5 collective-permute-start.11
  46.5 1.3 %collective-permute-start.17 = (bf16[640,256]{1,0:T(8,128)(2,1)}, bf16[640,256]{1,0:T(8,128)(2,1)S(1)}, u32[]{:S(2)}, u32[]{:S(2)}) collective-permute-start(bf16[640,256]{1,0:T(8,128)(2,1)} %collective-permute-done.8.rest_5_), channel_id=1, source_target_pairs={{0,4},{4,0},{1,5},{5,1},{2,6},{6,2},{3,7},{7,3},{8,12},{12,8},{9,1... | collective-permute-start | bytes 983048 | tf_op jit(solution)/shard_map/ppermute | solution.py:143
  47.8 2.1 %collective-permute-start.18 = (bf16[640,256]{1,0:T(8,128)(2,1)}, bf16[640,256]{1,0:T(8,128)(2,1)S(1)}, u32[]{:S(2)}, u32[]{:S(2)}) collective-permute-start(bf16[640,256]{1,0:T(8,128)(2,1)} %collective-permute-done.9.rest_10_), channel_id=1, source_target_pairs={{0,1},{1,0},{2,3},{3,2},{4,5},{5,4},{6,7},{7,6},{8,9},{9,8},{10,11... | collective-permute-start | bytes 983048 | tf_op jit(solution)/shard_map/ppermute | solution.py:143
  50.0 0.9 %mask.1 = (f32[256,512]{1,0:T(8,128)S(1)}, s32[2]{0:T(128)S(1)}) custom-call(s32[256,1]{1,0:T(8,128)S(1)} %copy.17.seg_q, s32[256,1]{1,0:T(8,128)S(1)} %copy.18.pos_q, s32[1,512]{1,0:T(1,128)S(1)} %bitcast.38, s32[1,512]{1,0:T(1,128)S(1)} %bitcast.37), custom_call_target="tpu_custom_call" | custom-call | tf_op jit(solution)/shard_map/mask/pallas_call | solution.py:236
  50.9 1.0 %copy-done.3 = bf16[640,256]{1,0:T(8,128)(2,1)S(1)} copy-done((bf16[640,256]{1,0:T(8,128)(2,1)S(1)}, bf16[640,256]{1,0:T(8,128)(2,1)}, u32[]{:S(2)}) %copy-start.3) | copy-done | bytes 327704
  51.9 1.0 %copy-done.5 = bf16[640,256]{1,0:T(8,128)(2,1)S(1)} copy-done((bf16[640,256]{1,0:T(8,128)(2,1)S(1)}, bf16[640,256]{1,0:T(8,128)(2,1)}, u32[]{:S(2)}) %copy-start.5) | copy-done | bytes 327704
  52.9 1.0 %copy-done.7 = bf16[640,256]{1,0:T(8,128)(2,1)S(1)} copy-done((bf16[640,256]{1,0:T(8,128)(2,1)S(1)}, bf16[640,256]{1,0:T(8,128)(2,1)}, u32[]{:S(2)}) %copy-start.7) | copy-done | bytes 327704
  53.9 1.0 %copy-done.9 = bf16[640,256]{1,0:T(8,128)(2,1)S(1)} copy-done((bf16[640,256]{1,0:T(8,128)(2,1)S(1)}, bf16[640,256]{1,0:T(8,128)(2,1)}, u32[]{:S(2)}) %copy-start.9) | copy-done | bytes 327704
  54.8 4.5 %project.3.rest_4_ = f32[2,512,256]{2,1,0:T(8,128)S(1)} custom-call(s32[3]{0:T(128)S(1)} %pad_add_fusion.1.place, bf16[8,256,640]{2,1,0:T(8,128)(2,1)S(1)} %norm.1.own, bf16[8,256,640]{2,1,0:T(8,128)(2,1)} %collective-permute-done.12.other, bf16[640,256]{1,0:T(8,128)(2,1)S(1)} %get-tuple-element.32.rest_0_, bf16[640,256]{1,0:T(8,128)(2,1)S(1)} %get-tuple-element.41.rest_1_, ...), custom_call_target="tpu_custom_call" | custom-call | flops 1845493760 | bytes 3604480 | tf_op jit(solution)/shard_map/project/pallas_call | solution.py:269
  59.5 0.7 collective-permute-start.16
  60.3 1.9 %collective-permute-done.17.rest_2_ = bf16[640,256]{1,0:T(8,128)(2,1)S(1)} collective-permute-done((bf16[640,256]{1,0:T(8,128)(2,1)}, bf16[640,256]{1,0:T(8,128)(2,1)S(1)}, u32[]{:S(2)}, u32[]{:S(2)}) %collective-permute-start.17) | collective-permute-done | bytes 327712 | tf_op jit(solution)/shard_map/ppermute | solution.py:143
  62.3 1.1 %collective-permute-done.18.rest_3_ = bf16[640,256]{1,0:T(8,128)(2,1)S(1)} collective-permute-done((bf16[640,256]{1,0:T(8,128)(2,1)}, bf16[640,256]{1,0:T(8,128)(2,1)S(1)}, u32[]{:S(2)}, u32[]{:S(2)}) %collective-permute-start.18) | collective-permute-done | bytes 327712 | tf_op jit(solution)/shard_map/ppermute | solution.py:143
  63.4 2.7 %project.4.rest_2_ = f32[2,512,256]{2,1,0:T(8,128)S(1)} custom-call(s32[3]{0:T(128)S(1)} %pad_add_fusion.1.place, bf16[8,256,640]{2,1,0:T(8,128)(2,1)S(1)} %norm.1.own, bf16[8,256,640]{2,1,0:T(8,128)(2,1)} %collective-permute-done.12.other, bf16[640,256]{1,0:T(8,128)(2,1)S(1)} %collective-permute-done.10.rest_0_, ...), custom_call_target="tpu_custom_call" | custom-call | flops 671088640 | bytes 1310720 | tf_op jit(solution)/shard_map/project/pallas_call | solution.py:269
  66.1 2.6 %project.5 = (bf16[256,256]{1,0:T(8,128)(2,1)S(1)}, bf16[256,256]{1,0:T(8,128)(2,1)S(1)}, bf16[256,256]{1,0:T(8,128)(2,1)S(1)}, bf16[256,256]{1,0:T(8,128)(2,1)S(1)}) custom-call(s32[3]{0:T(128)S(1)} %pad_add_fusion.1.place, bf16[8,256,640]{2,1,0:T(8,128)(2,1)S(1)} %norm.1.own, bf16[8,256,640]{2,1,0:T(8,128)(2,1)} %collective-permute-done.12.other, ...), custom_call_target="tpu_custom_call" | custom-call | flops 167772160 | bytes 327680 | tf_op jit(solution)/shard_map/project/pallas_call | solution.py:269
  68.9 1.1 %collective-permute-start.23 = (bf16[256,256]{1,0:T(8,128)(2,1)S(1)}, bf16[256,256]{1,0:T(8,128)(2,1)S(1)}, u32[]{:S(2)}, u32[]{:S(2)}) collective-permute-start(bf16[256,256]{1,0:T(8,128)(2,1)S(1)} %get-tuple-element.58.rest_0_), channel_id=1, source_target_pairs={{0,1},{1,0},{2,3},{3,2},{4,5},{5,4},{6,7},{7,6},{8,9},{9,8},{10,11... | collective-permute-start | bytes 393224 | tf_op jit(solution)/shard_map/ppermute | solution.py:166
  69.9 1.0 %collective-permute-start.22 = (bf16[256,256]{1,0:T(8,128)(2,1)S(1)}, bf16[256,256]{1,0:T(8,128)(2,1)S(1)}, u32[]{:S(2)}, u32[]{:S(2)}) collective-permute-start(bf16[256,256]{1,0:T(8,128)(2,1)S(1)} %get-tuple-element.57.rest_0_), channel_id=1, source_target_pairs={{0,1},{1,0},{2,3},{3,2},{4,5},{5,4},{6,7},{7,6},{8,9},{9,8},{10,11... | collective-permute-start | bytes 393224 | tf_op jit(solution)/shard_map/ppermute | solution.py:166
  71.5 1.3 %collective-permute-start.20 = (bf16[256,256]{1,0:T(8,128)(2,1)S(1)}, bf16[256,256]{1,0:T(8,128)(2,1)S(1)}, u32[]{:S(2)}, u32[]{:S(2)}) collective-permute-start(bf16[256,256]{1,0:T(8,128)(2,1)S(1)} %get-tuple-element.56), channel_id=1, source_target_pairs={{0,3},{1,2},{2,1},{3,0},{4,7},{5,6},{6,5},{7,4},{8,11},{9,10},{10,... | collective-permute-start | bytes 393224 | tf_op jit(solution)/shard_map/ppermute | solution.py:166
  72.7 2.5 %collective-permute-done.23.rest_1_ = bf16[256,256]{1,0:T(8,128)(2,1)S(1)} collective-permute-done((bf16[256,256]{1,0:T(8,128)(2,1)S(1)}, bf16[256,256]{1,0:T(8,128)(2,1)S(1)}, u32[]{:S(2)}, u32[]{:S(2)}) %collective-permute-start.23) | collective-permute-done | bytes 131104 | tf_op jit(solution)/shard_map/ppermute | solution.py:166
  75.2 3.0 %attend.4.rest_2_ = bf16[256,4096]{1,0:T(8,128)(2,1)} custom-call(s32[1]{0:T(128)} %bitcast.place, s32[2]{0:T(128)S(1)} %get-tuple-element.49.needs, bf16[256,4096]{1,0:T(8,128)(2,1)S(1)} %bitcast.31, f32[256,512]{1,0:T(8,128)S(1)} %get-tuple-element.50.bias, bf16[256,256]{1,0:T(8,128)(2,1)S(1)} %get-tuple-element.58.rest_0_, ...), custom_call_target="tpu_custom_call" | custom-call | flops 536870912 | bytes 1048576 | tf_op jit(solution)/shard_map/attend/pallas_call | solution.py:300
  78.2 3.2 %attend.5.rest_2_ = bf16[256,4096]{1,0:T(8,128)(2,1)} custom-call(s32[1]{0:T(128)} %bitcast.place, s32[2]{0:T(128)S(1)} %get-tuple-element.49.needs, bf16[256,4096]{1,0:T(8,128)(2,1)S(1)} %bitcast.32, f32[256,512]{1,0:T(8,128)S(1)} %get-tuple-element.50.bias, bf16[256,256]{1,0:T(8,128)(2,1)S(1)} %get-tuple-element.57.rest_0_, ...), custom_call_target="tpu_custom_call", output_to_operand_aliasing={{}: (6, {})} | custom-call | flops 536870912 | bytes 1048576 | tf_op jit(solution)/shard_map/attend/pallas_call | solution.py:300
  81.4 3.0 %attend.6.rest_2_ = bf16[256,4096]{1,0:T(8,128)(2,1)} custom-call(s32[1]{0:T(128)} %bitcast.place, s32[2]{0:T(128)S(1)} %get-tuple-element.49.needs, bf16[256,4096]{1,0:T(8,128)(2,1)S(1)} %bitcast.33, f32[256,512]{1,0:T(8,128)S(1)} %get-tuple-element.50.bias, bf16[256,512]{1,0:T(8,128)(2,1)S(1)} %collective-permute-done.19.rest_0_, ...), custom_call_target="tpu_custom_call", output_to_operand_aliasing={{}: (6, {})} | custom-call | flops 536870912 | bytes 1048576 | tf_op jit(solution)/shard_map/attend/pallas_call | solution.py:300
  84.4 3.0 %attend.7 = bf16[256,4096]{1,0:T(8,128)(2,1)} custom-call(s32[1]{0:T(128)} %bitcast.place, s32[2]{0:T(128)S(1)} %get-tuple-element.49.needs, bf16[256,4096]{1,0:T(8,128)(2,1)S(1)} %bitcast.34, f32[256,512]{1,0:T(8,128)S(1)} %get-tuple-element.50.bias, bf16[256,512]{1,0:T(8,128)(2,1)S(1)} %collective-permute-done.19.rest_0_, ...), custom_call_target="tpu_custom_call", output_to_operand_aliasing={{}: (6, {})} | custom-call | flops 536870912 | bytes 1048576 | tf_op jit(solution)/shard_map/attend/pallas_call | solution.py:300
  (62 shorter events, 2.0 us)
Async XLA Ops:
  1.2 14.6 %copy-start.12 = (s32[1,256]{1,0:T(1,128)S(1)}, s32[1,256]{1,0:T(1,128)}, u32[]{:S(2)}) copy-start(s32[1,256]{1,0:T(1,128)} %param.16) | copy-start | bytes 3076
  1.2 14.6 %copy-start.13 = (s32[1,256]{1,0:T(1,128)S(1)}, s32[1,256]{1,0:T(1,128)}, u32[]{:S(2)}) copy-start(s32[1,256]{1,0:T(1,128)} %param.15) | copy-start | bytes 3076
  1.2 15.0 %copy-start.10 = (f32[5120]{0:T(1024)S(1)}, f32[5120]{0:T(1024)}, u32[]{:S(2)}) copy-start(f32[5120]{0:T(1024)} %param.11) | copy-start | bytes 61444
  1.3 1.8 %collective-permute-start = (bf16[2,320,256]{2,1,0:T(8,128)(2,1)S(1)}, bf16[2,320,256]{2,1,0:T(8,128)(2,1)S(1)}, u32[]{:S(2)}, u32[]{:S(2)}) collective-permute-start(bf16[2,320,256]{2,1,0:T(8,128)(2,1)S(1)} %pad_maximum_fusion), channel_id=1, source_target_pairs={{0,2},{2,0},{1,3},{3,1},{4,6},{6,4},{5,7},{7,5},{8,10},{10,8},{9,1... | collective-permute-start | bytes 983048 | tf_op jit(solution)/shard_map/ppermute | solution.py:143
  3.1 11.0 %collective-permute-start.3 = (bf16[640,256]{1,0:T(8,128)(2,1)S(1)}, bf16[640,256]{1,0:T(8,128)(2,1)S(1)}, u32[]{:S(2)}, u32[]{:S(2)}) collective-permute-start(bf16[640,256]{1,0:T(8,128)(2,1)S(1)} %get-tuple-element.32.rest_0_), channel_id=1, source_target_pairs={{0,4},{4,0},{1,5},{5,1},{2,6},{6,2},{3,7},{7,3},{8,12},{12,8},{9,1... | collective-permute-start | bytes 983048 | tf_op jit(solution)/shard_map/ppermute | solution.py:143
  6.1 13.7 %collective-permute-start.1 = (bf16[640,256]{1,0:T(8,128)(2,1)S(1)}, bf16[640,256]{1,0:T(8,128)(2,1)S(1)}, u32[]{:S(2)}, u32[]{:S(2)}) collective-permute-start(bf16[640,256]{1,0:T(8,128)(2,1)S(1)} %get-tuple-element.32.rest_0_), channel_id=1, source_target_pairs={{0,8},{8,16},{16,24},{24,0},{1,9},{9,17},{17,25},{25,1},{2,10},{10... | collective-permute-start | bytes 983048 | tf_op jit(solution)/shard_map/ppermute | solution.py:196
  7.7 16.2 %collective-permute-start.2 = (bf16[640,256]{1,0:T(8,128)(2,1)S(1)}, bf16[640,256]{1,0:T(8,128)(2,1)S(1)}, u32[]{:S(2)}, u32[]{:S(2)}) collective-permute-start(bf16[640,256]{1,0:T(8,128)(2,1)S(1)} %get-tuple-element.32.rest_0_), channel_id=1, source_target_pairs={{0,24},{8,0},{16,8},{24,16},{1,25},{9,1},{17,9},{25,17},{2,26},{10... | collective-permute-start | bytes 983048 | tf_op jit(solution)/shard_map/ppermute | solution.py:196
  14.1 5.6 %copy-start.2 = (bf16[640,256]{1,0:T(8,128)(2,1)}, bf16[640,256]{1,0:T(8,128)(2,1)S(1)}, u32[]{:S(2)}) copy-start(bf16[640,256]{1,0:T(8,128)(2,1)S(1)} %collective-permute-done.3.rest_2_) | copy-start | bytes 983044
  14.1 9.8 %collective-permute-start.4 = (bf16[640,256]{1,0:T(8,128)(2,1)S(1)}, bf16[640,256]{1,0:T(8,128)(2,1)S(1)}, u32[]{:S(2)}, u32[]{:S(2)}) collective-permute-start(bf16[640,256]{1,0:T(8,128)(2,1)S(1)} %collective-permute-done.3.rest_2_), channel_id=1, source_target_pairs={{0,1},{1,0},{2,3},{3,2},{4,5},{5,4},{6,7},{7,6},{8,9},{9,8},{10,11... | collective-permute-start | bytes 983048 | tf_op jit(solution)/shard_map/ppermute | solution.py:143
  15.8 8.1 %collective-permute-start.6 = (s32[2,256]{1,0:T(2,128)S(1)}, s32[2,256]{1,0:T(2,128)S(1)}, u32[]{:S(2)}, u32[]{:S(2)}) collective-permute-start(s32[2,256]{1,0:T(2,128)S(1)} %pad_add_fusion), channel_id=1, source_target_pairs={{0,1},{1,0},{2,3},{3,2},{4,5},{5,4},{6,7},{7,6},{8,9},{9,8},{10,11... | collective-permute-start | bytes 6152 | tf_op jit(solution)/shard_map/ppermute | solution.py:166
  16.2 7.7 %collective-permute-start.5 = (s32[1,256]{1,0:T(1,128)S(1)}, s32[1,256]{1,0:T(1,128)S(1)}, u32[]{:S(2)}, u32[]{:S(2)}) collective-permute-start(s32[1,256]{1,0:T(1,128)S(1)} %copy-done.12), channel_id=1, source_target_pairs={{0,2},{2,0},{1,3},{3,1},{4,6},{6,4},{5,7},{7,5},{8,10},{10,8},{9,1... | collective-permute-start | bytes 3080 | tf_op jit(solution)/shard_map/ppermute | solution.py:143
  16.2 1.7 %copy-start.1 = (bf16[1,256,5120]{2,1,0:T(8,128)(2,1)S(1)}, bf16[1,256,5120]{2,1,0:T(8,128)(2,1)}, u32[]{:S(2)}) copy-start(bf16[1,256,5120]{2,1,0:T(8,128)(2,1)} %param.9) | copy-start | bytes 7864324
  19.8 4.2 %copy-start.4 = (bf16[640,256]{1,0:T(8,128)(2,1)}, bf16[640,256]{1,0:T(8,128)(2,1)S(1)}, u32[]{:S(2)}) copy-start(bf16[640,256]{1,0:T(8,128)(2,1)S(1)} %collective-permute-done.1.rest_4_) | copy-start | bytes 983044
  23.9 0.7 copy-start.6
  23.9 1.5 %copy-start.15 = (s32[1,256]{1,0:T(1,128)}, s32[1,256]{1,0:T(1,128)S(1)}, u32[]{:S(2)}) copy-start(s32[1,256]{1,0:T(1,128)S(1)} %collective-permute-done.5) | copy-start | bytes 3076
  23.9 1.5 %copy-start.14 = (s32[2,256]{1,0:T(2,128)}, s32[2,256]{1,0:T(2,128)S(1)}, u32[]{:S(2)}) copy-start(s32[2,256]{1,0:T(2,128)S(1)} %collective-permute-done.6) | copy-start | bytes 6148
  24.6 0.7 copy-start.8
  25.3 25.6 %collective-permute-start.12 = (bf16[8,256,640]{2,1,0:T(8,128)(2,1)S(1)}, bf16[8,256,640]{2,1,0:T(8,128)(2,1)}, u32[]{:S(2)}, u32[]{:S(2)}) collective-permute-start(bf16[8,256,640]{2,1,0:T(8,128)(2,1)S(1)} %norm.1.own), channel_id=1, source_target_pairs={{0,2},{2,0},{1,3},{3,1},{4,6},{6,4},{5,7},{7,5},{8,10},{10,8},{9,1... | collective-permute-start | bytes 7864328 | tf_op jit(solution)/shard_map/ppermute | solution.py:143
  25.7 12.3 %collective-permute-start.7 = (bf16[640,256]{1,0:T(8,128)(2,1)}, bf16[640,256]{1,0:T(8,128)(2,1)}, u32[]{:S(2)}, u32[]{:S(2)}) collective-permute-start(bf16[640,256]{1,0:T(8,128)(2,1)} %copy-done.4), channel_id=1, source_target_pairs={{0,8},{8,16},{16,24},{24,0},{1,9},{9,17},{17,25},{25,1},{2,10},{10... | collective-permute-start | bytes 983048 | tf_op jit(solution)/shard_map/ppermute | solution.py:196
  26.9 13.3 %collective-permute-start.8 = (bf16[640,256]{1,0:T(8,128)(2,1)}, bf16[640,256]{1,0:T(8,128)(2,1)}, u32[]{:S(2)}, u32[]{:S(2)}) collective-permute-start(bf16[640,256]{1,0:T(8,128)(2,1)} %copy-done.4), channel_id=1, source_target_pairs={{0,1},{1,0},{2,3},{3,2},{4,5},{5,4},{6,7},{7,6},{8,9},{9,8},{10,11... | collective-permute-start | bytes 983048 | tf_op jit(solution)/shard_map/ppermute | solution.py:143
  28.4 18.1 %collective-permute-start.13 = (bf16[640,256]{1,0:T(8,128)(2,1)}, bf16[640,256]{1,0:T(8,128)(2,1)}, u32[]{:S(2)}, u32[]{:S(2)}) collective-permute-start(bf16[640,256]{1,0:T(8,128)(2,1)} %copy-done.4), channel_id=1, source_target_pairs={{0,4},{4,0},{1,5},{5,1},{2,6},{6,2},{3,7},{7,3},{8,12},{12,8},{9,1... | collective-permute-start | bytes 983048 | tf_op jit(solution)/shard_map/ppermute | solution.py:143
  29.1 16.2 %collective-permute-start.9 = (bf16[640,256]{1,0:T(8,128)(2,1)}, bf16[640,256]{1,0:T(8,128)(2,1)}, u32[]{:S(2)}, u32[]{:S(2)}) collective-permute-start(bf16[640,256]{1,0:T(8,128)(2,1)} %copy-done.6), channel_id=1, source_target_pairs={{0,4},{4,0},{1,5},{5,1},{2,6},{6,2},{3,7},{7,3},{8,12},{12,8},{9,1... | collective-permute-start | bytes 983048 | tf_op jit(solution)/shard_map/ppermute | solution.py:143
  38.0 9.9 %collective-permute-start.14 = (bf16[640,256]{1,0:T(8,128)(2,1)}, bf16[640,256]{1,0:T(8,128)(2,1)S(1)}, u32[]{:S(2)}, u32[]{:S(2)}) collective-permute-start(bf16[640,256]{1,0:T(8,128)(2,1)} %copy-done.6), channel_id=1, source_target_pairs={{0,1},{1,0},{2,3},{3,2},{4,5},{5,4},{6,7},{7,6},{8,9},{9,8},{10,11... | collective-permute-start | bytes 983048 | tf_op jit(solution)/shard_map/ppermute | solution.py:143
  45.3 14.1 %collective-permute-start.10 = (bf16[640,256]{1,0:T(8,128)(2,1)}, bf16[640,256]{1,0:T(8,128)(2,1)S(1)}, u32[]{:S(2)}, u32[]{:S(2)}) collective-permute-start(bf16[640,256]{1,0:T(8,128)(2,1)} %collective-permute-done.7.rest_7_), channel_id=1, source_target_pairs={{0,4},{4,0},{1,5},{5,1},{2,6},{6,2},{3,7},{7,3},{8,12},{12,8},{9,1... | collective-permute-start | bytes 983048 | tf_op jit(solution)/shard_map/ppermute | solution.py:143
  46.0 13.4 %collective-permute-start.11 = (bf16[640,256]{1,0:T(8,128)(2,1)}, bf16[640,256]{1,0:T(8,128)(2,1)S(1)}, u32[]{:S(2)}, u32[]{:S(2)}) collective-permute-start(bf16[640,256]{1,0:T(8,128)(2,1)} %collective-permute-done.7.rest_7_), channel_id=1, source_target_pairs={{0,1},{1,0},{2,3},{3,2},{4,5},{5,4},{6,7},{7,6},{8,9},{9,8},{10,11... | collective-permute-start | bytes 983048 | tf_op jit(solution)/shard_map/ppermute | solution.py:143
  46.5 15.8 %collective-permute-start.17 = (bf16[640,256]{1,0:T(8,128)(2,1)}, bf16[640,256]{1,0:T(8,128)(2,1)S(1)}, u32[]{:S(2)}, u32[]{:S(2)}) collective-permute-start(bf16[640,256]{1,0:T(8,128)(2,1)} %collective-permute-done.8.rest_5_), channel_id=1, source_target_pairs={{0,4},{4,0},{1,5},{5,1},{2,6},{6,2},{3,7},{7,3},{8,12},{12,8},{9,1... | collective-permute-start | bytes 983048 | tf_op jit(solution)/shard_map/ppermute | solution.py:143
  47.8 15.5 %collective-permute-start.18 = (bf16[640,256]{1,0:T(8,128)(2,1)}, bf16[640,256]{1,0:T(8,128)(2,1)S(1)}, u32[]{:S(2)}, u32[]{:S(2)}) collective-permute-start(bf16[640,256]{1,0:T(8,128)(2,1)} %collective-permute-done.9.rest_10_), channel_id=1, source_target_pairs={{0,1},{1,0},{2,3},{3,2},{4,5},{5,4},{6,7},{7,6},{8,9},{9,8},{10,11... | collective-permute-start | bytes 983048 | tf_op jit(solution)/shard_map/ppermute | solution.py:143
  50.9 1.0 %copy-start.3 = (bf16[640,256]{1,0:T(8,128)(2,1)S(1)}, bf16[640,256]{1,0:T(8,128)(2,1)}, u32[]{:S(2)}) copy-start(bf16[640,256]{1,0:T(8,128)(2,1)} %copy-done.2) | copy-start | bytes 983044
  51.9 1.0 %copy-start.5 = (bf16[640,256]{1,0:T(8,128)(2,1)S(1)}, bf16[640,256]{1,0:T(8,128)(2,1)}, u32[]{:S(2)}) copy-start(bf16[640,256]{1,0:T(8,128)(2,1)} %copy-done.4) | copy-start | bytes 983044
  52.9 1.0 %copy-start.7 = (bf16[640,256]{1,0:T(8,128)(2,1)S(1)}, bf16[640,256]{1,0:T(8,128)(2,1)}, u32[]{:S(2)}) copy-start(bf16[640,256]{1,0:T(8,128)(2,1)} %copy-done.6) | copy-start | bytes 983044
  53.9 1.0 %copy-start.9 = (bf16[640,256]{1,0:T(8,128)(2,1)S(1)}, bf16[640,256]{1,0:T(8,128)(2,1)}, u32[]{:S(2)}) copy-start(bf16[640,256]{1,0:T(8,128)(2,1)} %copy-done.8) | copy-start | bytes 983044
  59.4 6.7 %collective-permute-start.15 = (bf16[320,256]{1,0:T(8,128)(2,1)S(1)}, bf16[320,256]{1,0:T(8,128)(2,1)S(1)}, u32[]{:S(2)}, u32[]{:S(2)}) collective-permute-start(bf16[320,256]{1,0:T(8,128)(2,1)S(1)} %slice.22), channel_id=1, source_target_pairs={{0,1},{1,0},{2,3},{3,2},{4,5},{5,4},{6,7},{7,6},{8,9},{9,8},{10,11... | collective-permute-start | bytes 491528 | tf_op jit(solution)/shard_map/ppermute | solution.py:143
  59.5 6.6 %collective-permute-start.16 = (bf16[320,256]{1,0:T(8,128)(2,1)S(1)}, bf16[320,256]{1,0:T(8,128)(2,1)S(1)}, u32[]{:S(2)}, u32[]{:S(2)}) collective-permute-start(bf16[320,256]{1,0:T(8,128)(2,1)S(1)} %slice.23), channel_id=1, source_target_pairs={{0,4},{4,0},{1,5},{5,1},{2,6},{6,2},{3,7},{7,3},{8,12},{12,8},{9,1... | collective-permute-start | bytes 491528 | tf_op jit(solution)/shard_map/ppermute | solution.py:143
  60.3 5.8 %copy-start.11 = (f32[128]{0:T(128)S(1)}, f32[128]{0:T(128)}, u32[]{:S(2)}) copy-start(f32[128]{0:T(128)} %param.12) | copy-start | bytes 1540
  66.1 9.1 %copy-start = (bf16[1,256,4096]{2,1,0:T(8,128)(2,1)S(1)}, bf16[1,256,4096]{2,1,0:T(8,128)(2,1)}, u32[]{:S(2)}) copy-start(bf16[1,256,4096]{2,1,0:T(8,128)(2,1)} %param.10) | copy-start | bytes 6291460
  68.8 12.6 %collective-permute-start.19 = (bf16[256,512]{1,0:T(8,128)(2,1)S(1)}, bf16[256,512]{1,0:T(8,128)(2,1)S(1)}, u32[]{:S(2)}, u32[]{:S(2)}) collective-permute-start(bf16[256,512]{1,0:T(8,128)(2,1)S(1)} %pad_maximum_fusion.3), channel_id=1, source_target_pairs={{0,2},{1,3},{2,0},{3,1},{4,6},{5,7},{6,4},{7,5},{8,10},{9,11},{10,... | collective-permute-start | bytes 786440 | tf_op jit(solution)/shard_map/ppermute | solution.py:166
  68.9 6.4 %collective-permute-start.23 = (bf16[256,256]{1,0:T(8,128)(2,1)S(1)}, bf16[256,256]{1,0:T(8,128)(2,1)S(1)}, u32[]{:S(2)}, u32[]{:S(2)}) collective-permute-start(bf16[256,256]{1,0:T(8,128)(2,1)S(1)} %get-tuple-element.58.rest_0_), channel_id=1, source_target_pairs={{0,1},{1,0},{2,3},{3,2},{4,5},{5,4},{6,7},{7,6},{8,9},{9,8},{10,11... | collective-permute-start | bytes 393224 | tf_op jit(solution)/shard_map/ppermute | solution.py:166
  69.9 8.3 %collective-permute-start.22 = (bf16[256,256]{1,0:T(8,128)(2,1)S(1)}, bf16[256,256]{1,0:T(8,128)(2,1)S(1)}, u32[]{:S(2)}, u32[]{:S(2)}) collective-permute-start(bf16[256,256]{1,0:T(8,128)(2,1)S(1)} %get-tuple-element.57.rest_0_), channel_id=1, source_target_pairs={{0,1},{1,0},{2,3},{3,2},{4,5},{5,4},{6,7},{7,6},{8,9},{9,8},{10,11... | collective-permute-start | bytes 393224 | tf_op jit(solution)/shard_map/ppermute | solution.py:166
  71.0 10.4 %collective-permute-start.21 = (bf16[256,256]{1,0:T(8,128)(2,1)S(1)}, bf16[256,256]{1,0:T(8,128)(2,1)S(1)}, u32[]{:S(2)}, u32[]{:S(2)}) collective-permute-start(bf16[256,256]{1,0:T(8,128)(2,1)S(1)} %get-tuple-element.55), channel_id=1, source_target_pairs={{0,3},{1,2},{2,1},{3,0},{4,7},{5,6},{6,5},{7,4},{8,11},{9,10},{10,... | collective-permute-start | bytes 393224 | tf_op jit(solution)/shard_map/ppermute | solution.py:166
  71.5 13.0 %collective-permute-start.20 = (bf16[256,256]{1,0:T(8,128)(2,1)S(1)}, bf16[256,256]{1,0:T(8,128)(2,1)S(1)}, u32[]{:S(2)}, u32[]{:S(2)}) collective-permute-start(bf16[256,256]{1,0:T(8,128)(2,1)S(1)} %get-tuple-element.56), channel_id=1, source_target_pairs={{0,3},{1,2},{2,1},{3,0},{4,7},{5,6},{6,5},{7,4},{8,11},{9,10},{10,... | collective-permute-start | bytes 393224 | tf_op jit(solution)/shard_map/ppermute | solution.py:166

commit v2 on v1

v2 whole, which is shorter than its diff:
```python
import functools
import math

import jax
import jax.numpy as jnp
import numpy as np
from jax import lax
from jax.experimental import pallas as pl
from jax.experimental.pallas import tpu as pltpu
from jax.sharding import Mesh
from jax.sharding import PartitionSpec as P

KVH = 4
HD = 128
G = 8
EPS = 1e-06
THETA = 1000000.0
MASKED = -1e30
VMEM_LIMIT = 24 * 2**20
NORM_ROWS = 64


def norm_kernel(chunks, hidden, gain, out):
    inputs = hidden[...].astype(jnp.float32)
    scale = lax.rsqrt(jnp.mean(inputs * inputs, axis=-1, keepdims=True) + EPS)
    normed = (inputs * scale * gain[...]).astype(jnp.bfloat16)
    rows = normed.shape[1] // chunks
    for j in range(chunks):
        out[j] = normed[:, j * rows : (j + 1) * rows]


def project_kernel(chips_z, groups, first, last, count, tokens, place, own, other, *rest):
    z, y, x = place[0], place[1], place[2]
    rest = list(rest)
    weight, lhs, sems = rest[-3:]
    rows = weight.shape[2]
    waits = []
    for g, (k, near) in enumerate(groups):
        p = lax.rem(z - k + chips_z, chips_z)
        chunk = p * 2 + (y if near else 1 - y)
        pairs = [
            (own.at[chunk], lhs.at[g, pl.ds(0, count)]),
            (other.at[chunk], lhs.at[g, pl.ds(count, count)]),
        ]
        if k == 0:
            pairs.append((rest.pop(0), weight.at[g]))
        elif near or k != chips_z // 2:
            pairs.append((rest.pop(0), weight.at[g, x]))
            pairs.append((rest.pop(0), weight.at[g, 1 - x]))
        else:
            pairs.append((rest.pop(0), weight.at[g, x]))
            for part in range(2):
                at = pl.ds(part * (rows // 2), rows // 2)
                pairs.append((rest.pop(0), weight.at[g, 1 - x, at]))
        copies = [
            pltpu.make_async_copy(source, target, sems.at[g, i])
            for i, (source, target) in enumerate(pairs)
        ]
        for copy in copies:
            copy.start()
        waits.append(copies)
    if last:
        rest = rest[tokens:]
    earlier = None if first else rest.pop(0)
    terms = [None, None]
    for g, copies in enumerate(waits):
        for copy in copies:
            copy.wait()
        for half in range(2):
            part = jnp.dot(lhs[g], weight[g, half], preferred_element_type=jnp.float32)
            terms[half] = part if terms[half] is None else terms[half] + part
    for half in range(2):
        if not first:
            terms[half] += earlier[half]
        if not last:
            rest[0][half] = terms[half]
    if not last:
        return
    cosine, sine, gain = rest[:3]
    outs = rest[3:5]
    for head in range(2):
        columns = slice(head * HD, (head + 1) * HD)
        for part, out in enumerate(outs):
            at = slice(part * count, (part + 1) * count)
            raw = terms[0][at, columns]
            normk = raw * lax.rsqrt(jnp.mean(raw * raw, axis=-1, keepdims=True) + EPS) * gain[...]
            turned = normk * cosine[at, :] + pltpu.roll(normk, HD // 2, 1) * sine[at, :]
            out[:, 2 * head * HD : (2 * head + 1) * HD] = turned.astype(jnp.bfloat16)
            out[:, (2 * head + 1) * HD : (2 * head + 2) * HD] = terms[1][at, columns].astype(
                jnp.bfloat16
            )


def mask_kernel(seg_q, pos_q, seg_k, pos_k, bias, needs):
    allowed = (seg_k[...] == seg_q[...]) & (pos_k[...] <= pos_q[...])
    bias[...] = jnp.where(allowed, 0.0, MASKED)
    rows, columns = bias.shape[0] // 2, bias.shape[1] // 2
    for tile in range(2):
        found = [
            jnp.max(
                bias[tile * rows : (tile + 1) * rows, half * columns : (half + 1) * columns]
            )
            == 0.0
            for half in range(2)
        ]
        needs[tile] = found[0].astype(jnp.int32) + 2 * found[1].astype(jnp.int32)


def attend_kernel(pieces, count, place, needs, queries, bias, *rest):
    sources, (out, keys, values) = rest[:pieces], rest[-3:]
    step = pl.program_id(0)
    tile_rows = count // 2
    length = pieces * tile_rows

    for head in range(2):

        @pl.when(step == head)
        def _():
            left = 2 * head * HD
            for i, source in enumerate(sources):
                for half in range(2):
                    here = slice(half * tile_rows, (half + 1) * tile_rows)
                    there = half * length + i * tile_rows
                    keys[there : there + tile_rows, :] = source[here, left : left + HD]
                    values[there : there + tile_rows, :] = source[here, left + HD : left + 2 * HD]

    factor = math.log2(math.e) / math.sqrt(HD)

    def tile_body(tile, low, high):
        rows = slice(tile * tile_rows, (tile + 1) * tile_rows)
        k, v, b = keys[low:high, :], values[low:high, :], bias[rows, low:high]

        def score(pair):
            q = jnp.concatenate(
                [queries[rows, g * HD : (g + 1) * HD] for g in (2 * pair, 2 * pair + 1)], axis=0
            )
            return lax.dot_general(
                q, k, (((1,), (1,)), ((), ())), preferred_element_type=jnp.float32
            )

        ahead = score(0)
        for pair in range(G // 2):
            scores = ahead.reshape(2, tile_rows, high - low) + b[None]
            if pair + 1 < G // 2:
                ahead = score(pair + 1)
            top = jnp.max(scores, axis=-1, keepdims=True)
            weights = jnp.exp2((scores - top) * factor)
            total = jnp.sum(weights, axis=-1, keepdims=True)
            summed = jnp.dot(
                weights.astype(jnp.bfloat16).reshape(2 * tile_rows, high - low),
                v,
                preferred_element_type=jnp.float32,
            ).reshape(2, tile_rows, HD)
            result = (summed * (1.0 / total)).astype(jnp.bfloat16)
            for i in range(2):
                g = 2 * pair + i
                out[rows, g * HD : (g + 1) * HD] = result[i]

    for tile in range(2):
        for need, low, high in ((1, 0, length), (2, length, 2 * length), (3, 0, 2 * length)):

            @pl.when(needs[tile] == need)
            def _():
                tile_body(tile, low, high)


def swap(array, axis):
    return lax.ppermute(array, axis, [(0, 1), (1, 0)])


def on_device(
    sizes, hidden, queries, norm_gain, key_gain, k_weight, v_weight, segment, position
):
    chips_z, groups = sizes[0], sizes[3]
    count, width = hidden.shape[1:]
    own_rows = k_weight.shape[0]
    rows = 2 * own_rows
    chunks = 2 * chips_z
    m = 2 * groups
    z, y = lax.axis_index("z"), lax.axis_index("y")
    core, x = lax.axis_index("core"), lax.axis_index("x")
    bf16 = jnp.bfloat16
    whole = pl.BlockSpec(memory_space=pltpu.VMEM)
    params = pltpu.CompilerParams(vmem_limit_bytes=VMEM_LIMIT)

    def along_ctx(array, d, cross=False):
        pairs = []
        for c in range(2):
            for i in range(m):
                pairs.append((c * m + i, (c ^ int(cross)) * m + (i + d) % m))
        return lax.ppermute(array, ("core", "ctx", "x"), pairs)

    def columns(which):
        at = which * 2 * HD
        return jnp.stack(
            [lax.dynamic_slice_in_dim(w, at, 2 * HD, 1) for w in (k_weight, v_weight)]
        )

    tokens = []

    def after(array, *others):
        corners = [
            other[tuple(slice(0, size) for size in (1, 16, 128)[-other.ndim :])]
            for other in others
        ]
        array, corners = lax.optimization_barrier((array, corners))
        tokens.extend(corners)
        return array

    def norm(array):
        return pl.pallas_call(
            functools.partial(norm_kernel, chunks),
            out_shape=jax.ShapeDtypeStruct((chunks, count, rows), bf16),
            grid=(count // NORM_ROWS,),
            in_specs=[pl.BlockSpec((NORM_ROWS, width), lambda i: (i, 0)), whole],
            out_specs=pl.BlockSpec((chunks, NORM_ROWS, rows), lambda i: (0, i, 0)),
            compiler_params=params,
            cost_estimate=pl.CostEstimate(
                flops=4 * count * width, bytes_accessed=4 * count * width, transcendentals=0
            ),
            name="norm",
        )(array[0], norm_gain[None])

    taken = swap(columns(1 - core), "core")
    kept = columns(core)
    hidden_other = swap(hidden, "core")
    chip = lax.dynamic_update_slice(
        jnp.zeros((2, rows, 2 * HD), bf16), kept, (0, core * own_rows, 0)
    )
    chip = lax.dynamic_update_slice(chip, taken, (0, (1 - core) * own_rows, 0))
    normed = norm(after(hidden, chip))
    segment, position = after(segment, normed), after(position, normed)
    normed_other = norm(hidden_other)
    position_other = swap(position, "core")
    ints = jnp.concatenate([segment, position])
    ints_all = [ints] + [along_ctx(ints, d) for d in range(1, m)]

    def ring(array, step):
        return lax.ppermute(array, "z", [(i, (i + step) % chips_z) for i in range(chips_z)])

    middle = chips_z // 2
    mine = {0: lax.dynamic_index_in_dim(chip, x, 0, keepdims=False)}
    across, beside, corner = {}, {}, {}
    chip_beside = swap(chip, "y")
    for r in range(1, middle + 1):
        arrived = [r] if r == middle else [r, chips_z - r]
        for k in arrived:
            mine[k] = ring(mine[k - 1], 1) if k == r else ring(mine[(k + 1) % chips_z], -1)
        if r == 1:
            tied = (mine[1], mine[chips_z - 1])
            others = (chip_beside, normed_other, position_other, *ints_all[1:])
            mine[1], mine[chips_z - 1] = after(tied, *others)
        elif r == middle:
            mine[r] = after(mine[r], beside[r - 1], across[chips_z - r + 1])
        for k in arrived:
            beside[k], across[k] = swap(mine[k], "y"), swap(mine[k], "x")
    for k in range(1, chips_z):
        if k < middle:
            corner[k] = swap(across[k], "y")
        elif k > middle:
            corner[k] = swap(beside[k], "x")

    where = jnp.concatenate([position[0], position_other[0]]).astype(jnp.float32)
    half = HD // 2
    freq = np.exp(np.arange(half, dtype=np.float32) * np.float32(-2.0 * math.log(THETA) / HD))
    angle = where[:, None] * freq[None, :]
    cosine, sine = jnp.cos(angle), jnp.sin(angle)
    cosine = jnp.concatenate([cosine, cosine], axis=1)
    sine = jnp.concatenate([-sine, sine], axis=1)
    order = (
        jnp.stack(ints_all).reshape(m, 2, 2, count // 2).transpose(1, 2, 0, 3).reshape(2, m * count)
    )
    bias, needs = pl.pallas_call(
        mask_kernel,
        out_shape=[
            jax.ShapeDtypeStruct((count, m * count), jnp.float32),
            jax.ShapeDtypeStruct((2,), jnp.int32),
        ],
        in_specs=[whole] * 4,
        out_specs=[whole, pl.BlockSpec(memory_space=pltpu.SMEM)],
        compiler_params=params,
        name="mask",
    )(segment.reshape(count, 1), position.reshape(count, 1), order[:1], order[1:])


    place = jnp.stack([z, y, x]).astype(jnp.int32)
    acc_shape = jax.ShapeDtypeStruct((2, 2 * count, 2 * HD), jnp.float32)
    kv_shape = jax.ShapeDtypeStruct((count, 4 * HD), bf16)
    early = [(0, True), (0, False)]
    early += [(k, True) for k in range(1, chips_z) if k != middle]
    late = [(middle, True)] + [(k, False) for k in range(1, chips_z) if k != middle]
    final = [(middle, False)]
    acc = []
    for groups in (early, late, final):
        first, last = groups is early, groups is final
        if groups is late:
            top, bottom = beside[middle][: rows // 2], across[middle][rows // 2 :]
            corner[middle] = (
                swap(after(top, acc[0]), "x"), swap(after(bottom, bias), "y")
            )
        arrays = []
        for k, near in groups:
            if k == 0:
                arrays.append(chip if near else chip_beside)
            else:
                arrays += [mine[k], across[k]] if near else [beside[k], corner[k]]
        arrays = jax.tree.leaves(arrays)
        anywhere = pl.BlockSpec(memory_space=pl.ANY)
        outs = pl.pallas_call(
            functools.partial(
                project_kernel, chips_z, groups, first, last, count, len(tokens)
            ),
            out_shape=[kv_shape] * 2 if last else [acc_shape],
            in_specs=[pl.BlockSpec(memory_space=pltpu.SMEM)]
            + [anywhere] * (2 + len(arrays) + (len(tokens) if last else 0))
            + [whole] * (len(acc) + (3 if last else 0)),
            out_specs=[whole] * (2 if last else 1),
            scratch_shapes=[
                pltpu.VMEM((len(groups), 2, rows, 2 * HD), bf16),
                pltpu.VMEM((len(groups), 2 * count, rows), bf16),
                pltpu.SemaphoreType.DMA((len(groups), 5)),
            ],
            compiler_params=params,
            cost_estimate=pl.CostEstimate(
                flops=2 * 2 * count * rows * 4 * HD * len(groups),
                bytes_accessed=2 * rows * (4 * HD + 2 * count) * len(groups),
                transcendentals=0,
            ),
            name="project",
        )(
            place, normed, normed_other, *arrays, *(tokens if last else []), *acc,
            *((cosine, sine, key_gain[None]) if last else ()),
        )
        acc = [outs[-1]]

    kv_own, kv_other = outs
    result = None
    for cross, kv in enumerate((kv_own, kv_other)):
        sources = [kv if d == 0 and not cross else along_ctx(kv, d, cross) for d in range(m)]

        def block(step, place, needs, cross=cross):
            return (0, lax.rem(place[0] + cross, 2) * 2 + step)

        earlier = [] if result is None else [result]
        result = pl.pallas_call(
            functools.partial(attend_kernel, m, count),
            out_shape=jax.ShapeDtypeStruct((count, KVH * G * HD), bf16),
            grid_spec=pltpu.PrefetchScalarGridSpec(
                num_scalar_prefetch=2,
                grid=(2,),
                in_specs=[pl.BlockSpec((count, G * HD), block)]
                + [whole] * (1 + m)
                + [pl.BlockSpec(memory_space=pl.ANY)] * len(earlier),
                out_specs=pl.BlockSpec((count, G * HD), block),
                scratch_shapes=[
                    pltpu.VMEM((m * count, HD), bf16),
                    pltpu.VMEM((m * count, HD), bf16),
                ],
            ),
            input_output_aliases={4 + m: 0} if earlier else {},
            compiler_params=params,
            cost_estimate=pl.CostEstimate(
                flops=2 * count * m * count * KVH * G * HD,
                bytes_accessed=2 * count * KVH * G * HD,
                transcendentals=count * m * count * KVH * G // 2,
            ),
            name="attend",
        )(core.astype(jnp.int32)[None], needs, queries[0], bias, *sources, *earlier)
    return result[None]


def solution(mesh):
    n, m = mesh.shape["fsdp"], mesh.shape["ctx"]
    sizes = (n // 4, 2, 2, m // 2, 2)
    fine = Mesh(mesh.devices.reshape(sizes), ("z", "y", "core", "ctx", "x"))
    fsdp, ctx = ("z", "y", "core"), ("ctx", "x")
    placed = (
        P(fsdp, ctx, None),
        P(fsdp, ctx, None),
        P(),
        P(),
        P(fsdp, None),
        P(fsdp, None),
        P(fsdp, ctx),
        P(fsdp, ctx),
    )
    return jax.shard_map(
        functools.partial(on_device, sizes),
        mesh=fine,
        in_specs=placed,
        out_specs=P(fsdp, ctx, None),
        check_vma=False,
    )
```

time: 87.8 us -> 90.6 us (1.032)
  local copies, waits for them, and re-layouts: 9.97 us -> 16.1 us
  waiting for transfers between devices: 24.2 us -> 20.1 us
  Pallas kernels: 24.6 us -> 26.4 us
  starting transfers between devices: 24.9 us -> 23.9 us
    ppermute x3, waiting for transfers between devices: 8.08 us -> 0.01 us  [ring(): lax.ppermute(array, 'z', [(i, (i + step) % chips_z) for i in range(chips_...]
    ppermute x6 -> x4, waiting for transfers between devices: 2.54 us -> 8.37 us  [along_ctx(): return lax.ppermute(array, ('core', 'ctx', 'x'), pairs)]
    slice x2 -> x13, local copies, waits for them, and re-layouts: 0.03 us -> 3.21 us  [the longest x10 3.18 us: after(): other[tuple((slice(0, size) for size in (1, 16, 128)[-other.ndim:]))]]
    ppermute x15 -> x14, waiting for transfers between devices: 13.5 us -> 11.7 us  [swap(): return lax.ppermute(array, axis, [(0, 1), (1, 0)])]
    pallas_call x8 -> x7, Pallas kernels: 23.8 us -> 25.5 us  [the longest x3 10.5 us: on_device(): pl.pallas_call(functools.partial(project_kernel, chips_z, groups, first,...]
    ppermute x15 -> x14, starting transfers between devices: 15.6 us -> 14.8 us  [swap(): return lax.ppermute(array, axis, [(0, 1), (1, 0)])]
    ppermute x6 -> x4, starting transfers between devices: 4.29 us -> 3.7 us  [along_ctx(): return lax.ppermute(array, ('core', 'ctx', 'x'), pairs)]
    unnamed x32 -> x36, local copies, waits for them, and re-layouts: 7.08 us -> 7.4 us
  transfers between devices with their start and end apart: 24 -> 21, of which waited for: 8 -> 6; matrix products, arithmetic and copies ran while one was open for 6% -> 13% of each run, Pallas kernels for 22% -> 21%
where the time goes in v2:
time: 90.6 us; the launch traced here: 90.2 us
  Pallas kernels  26.4 us (29%)
  starting transfers between devices  23.9 us (26%)
  waiting for transfers between devices  20.1 us (22%)
  local copies, waits for them, and re-layouts  16.1 us (18%)
  other arithmetic  3.43 us (4%)
    ppermute x14, starting transfers between devices, swap(): return lax.ppermute(array, axis, [(0, 1), (1, 0)])  14.8 us
    ppermute x14, waiting for transfers between devices, swap(): return lax.ppermute(array, axis, [(0, 1), (1, 0)])  11.7 us
    pallas_call x3, Pallas kernels, on_device(): pl.pallas_call(functools.partial(project_kernel, chips_z, groups, first,...  10.5 us
    pallas_call x2, Pallas kernels, on_device(): pl.pallas_call(functools.partial(attend_kernel, m, count), out_shape=jax....  9.67 us
    ppermute x4, waiting for transfers between devices, along_ctx(): return lax.ppermute(array, ('core', 'ctx', 'x'), pairs)  8.37 us
    unnamed x36, local copies, waits for them, and re-layouts  7.4 us
    ppermute x3, starting transfers between devices, ring(): lax.ppermute(array, 'z', [(i, (i + step) % chips_z) for i in range(chips_...  5.4 us
    pallas_call x2, Pallas kernels, norm(): pl.pallas_call(functools.partial(norm_kernel, chunks), out_shape=jax.Shap...  5.33 us
  transfers between devices with their start and end apart: 21, of which 6 were waited for; matrix products, arithmetic and copies ran while one was open for 13% of the time, Pallas kernels for 21%

profile of v2, /device:TPU:0, one launch (start us, length us, event | category | flops | bytes accessed | tf_op | source)
XLA Modules:
  0.0 90.2 jit_solution(7449520438565282100)
XLA Ops:
  0.5 1.2 %dynamic-slice_bitcast_fusion.1 = (bf16[1,320,256]{2,1,0:T(8,128)(2,1)S(1)}, bf16[1,320,256]{2,1,0:T(8,128)(2,1)S(1)}, bf16[1,320,256]{2,1,0:T(8,128)(2,1)S(1)}, bf16[1,320,256]{2,1,0:T(8,128)(2,1)S(1)}) fusion(bf16[320,512]{1,0:T(8,128)(2,1)} %param.14, s32[]{:T(128)S(6)} %select_n.20, s32[]{:T(128)S(6)} %select_n.18, bf16[320,512]{1,0:T(8,128)(2,1)} %param.13), kind=kLoop, calls=%fused_computation.7 | loop fusion | bytes 1310728 | tf_op jit(solution)/shard_map/stack | solution.py:195
  1.9 3.6 %collective-permute-done = bf16[2,320,256]{2,1,0:T(8,128)(2,1)S(1)} collective-permute-done((bf16[2,320,256]{2,1,0:T(8,128)(2,1)S(1)}, bf16[2,320,256]{2,1,0:T(8,128)(2,1)S(1)}, u32[]{:S(2)}, u32[]{:S(2)}) %collective-permute-start) | collective-permute-done | bytes 327712 | tf_op jit(solution)/shard_map/ppermute | solution.py:168
  5.5 3.0 %collective-permute-start.5 = (bf16[2,640,256]{2,1,0:T(8,128)(2,1)S(1)}, bf16[2,640,256]{2,1,0:T(8,128)(2,1)}, u32[]{:S(2)}, u32[]{:S(2)}) collective-permute-start(bf16[2,640,256]{2,1,0:T(8,128)(2,1)S(1)} %constant_dynamic-update-slice_fusion.rest_0_), channel_id=1, source_target_pairs={{0,4},{4,0},{1,5},{5,1},{2,6},{6,2},{3,7},{7,3},{8,12},{12,8},{9,1... | collective-permute-start | bytes 1966088 | tf_op jit(solution)/shard_map/ppermute | solution.py:168
  8.4 0.7 dynamic-slice_bitcast_fusion
  9.2 1.6 %collective-permute-start.3 = (bf16[640,256]{1,0:T(8,128)(2,1)}, bf16[640,256]{1,0:T(8,128)(2,1)}, u32[]{:S(2)}, u32[]{:S(2)}) collective-permute-start(bf16[640,256]{1,0:T(8,128)(2,1)} %dynamic-slice_bitcast_fusion), channel_id=1, source_target_pairs={{0,8},{8,16},{16,24},{24,0},{1,9},{9,17},{17,25},{25,1},{2,10},{10... | collective-permute-start | bytes 983048 | tf_op jit(solution)/shard_map/ppermute | solution.py:239
  10.8 2.2 %collective-permute-start.4 = (bf16[640,256]{1,0:T(8,128)(2,1)}, bf16[640,256]{1,0:T(8,128)(2,1)}, u32[]{:S(2)}, u32[]{:S(2)}) collective-permute-start(bf16[640,256]{1,0:T(8,128)(2,1)} %dynamic-slice_bitcast_fusion), channel_id=1, source_target_pairs={{0,24},{8,0},{16,8},{24,16},{1,25},{9,1},{17,9},{25,17},{2,26},{10... | collective-permute-start | bytes 983048 | tf_op jit(solution)/shard_map/ppermute | solution.py:239
  13.0 0.6 pad_add_fusion.1.place
  13.6 1.7 %copy-done.3 = bf16[1,256,5120]{2,1,0:T(8,128)(2,1)S(1)} copy-done((bf16[1,256,5120]{2,1,0:T(8,128)(2,1)S(1)}, bf16[1,256,5120]{2,1,0:T(8,128)(2,1)}, u32[]{:S(2)}) %copy-start.3) | copy-done | bytes 2621464
  15.4 1.8 %norm.2.own = bf16[8,256,640]{2,1,0:T(8,128)(2,1)S(1)} custom-call(bf16[256,5120]{1,0:T(8,128)(2,1)S(1)} %bitcast.30, f32[1,5120]{1,0:T(1,128)S(1)} %bitcast.31), custom_call_target="tpu_custom_call" | custom-call | flops 5242880 | bytes 5242880 | tf_op jit(solution)/shard_map/norm/pallas_call | solution.py:211
  17.3 0.6 stack.45
  17.9 0.8 copy.15.seg_q
  18.7 0.8 copy.16.pos_q
  19.5 1.5 %collective-permute-start.1 = (s32[2,256]{1,0:T(2,128)S(1)}, s32[2,256]{1,0:T(2,128)S(1)}, u32[]{:S(2)}, u32[]{:S(2)}) collective-permute-start(s32[2,256]{1,0:T(2,128)S(1)} %pad_add_fusion), channel_id=1, source_target_pairs={{0,1},{1,0},{2,3},{3,2},{4,5},{5,4},{6,7},{7,6},{8,9},{9,8},{10,11... | collective-permute-start | bytes 6152 | tf_op jit(solution)/shard_map/ppermute | solution.py:191
  21.0 0.6 slice.71.rest_8_
  21.5 1.5 %collective-permute-done.1 = s32[2,256]{1,0:T(2,128)S(1)} collective-permute-done((s32[2,256]{1,0:T(2,128)S(1)}, s32[2,256]{1,0:T(2,128)S(1)}, u32[]{:S(2)}, u32[]{:S(2)}) %collective-permute-start.1) | collective-permute-done | bytes 2080 | tf_op jit(solution)/shard_map/ppermute | solution.py:191
  23.0 0.6 slice.72.rest_9_
  23.6 0.7 slice.69.rest_6_
  24.3 3.6 %norm.3.other = bf16[8,256,640]{2,1,0:T(8,128)(2,1)S(1)} custom-call(bf16[256,5120]{1,0:T(8,128)(2,1)} %bitcast.16.hidden, f32[1,5120]{1,0:T(1,128)S(1)} %bitcast.32), custom_call_target="tpu_custom_call" | custom-call | flops 5242880 | bytes 5242880 | tf_op jit(solution)/shard_map/norm/pallas_call | solution.py:211
  27.9 1.5 %copy-done = bf16[8,256,640]{2,1,0:T(8,128)(2,1)} copy-done((bf16[8,256,640]{2,1,0:T(8,128)(2,1)}, bf16[8,256,640]{2,1,0:T(8,128)(2,1)S(1)}, u32[]{:S(2)}) %copy-start) | copy-done | bytes 2621464
  29.4 1.7 %collective-permute-start.11 = (bf16[640,256]{1,0:T(8,128)(2,1)}, bf16[640,256]{1,0:T(8,128)(2,1)}, u32[]{:S(2)}, u32[]{:S(2)}) collective-permute-start(bf16[640,256]{1,0:T(8,128)(2,1)} %collective-permute-done.3.rest_2_), channel_id=1, source_target_pairs={{0,1},{1,0},{2,3},{3,2},{4,5},{5,4},{6,7},{7,6},{8,9},{9,8},{10,11... | collective-permute-start | bytes 983048 | tf_op jit(solution)/shard_map/ppermute | solution.py:168
  31.0 1.5 %collective-permute-start.8 = (bf16[640,256]{1,0:T(8,128)(2,1)}, bf16[640,256]{1,0:T(8,128)(2,1)}, u32[]{:S(2)}, u32[]{:S(2)}) collective-permute-start(bf16[640,256]{1,0:T(8,128)(2,1)} %collective-permute-done.3.rest_2_), channel_id=1, source_target_pairs={{0,4},{4,0},{1,5},{5,1},{2,6},{6,2},{3,7},{7,3},{8,12},{12,8},{9,1... | collective-permute-start | bytes 983048 | tf_op jit(solution)/shard_map/ppermute | solution.py:168
  32.6 1.6 %collective-permute-start.7 = (bf16[640,256]{1,0:T(8,128)(2,1)}, bf16[640,256]{1,0:T(8,128)(2,1)}, u32[]{:S(2)}, u32[]{:S(2)}) collective-permute-start(bf16[640,256]{1,0:T(8,128)(2,1)} %collective-permute-done.3.rest_2_), channel_id=1, source_target_pairs={{0,8},{8,16},{16,24},{24,0},{1,9},{9,17},{17,25},{25,1},{2,10},{10... | collective-permute-start | bytes 983048 | tf_op jit(solution)/shard_map/ppermute | solution.py:239
  35.2 1.8 %fusion = (f32[512,64]{1,0:T(8,128)}, f32[512,64]{1,0:T(8,128)}, f32[512,64]{1,0:T(8,128)S(1)}) fusion(f32[64]{0:T(128)S(1)} %copy-done.17, f32[512]{0:T(512)S(1)} %add_convert_fusion), kind=kLoop, calls=%fused_computation.11 | loop fusion | flops 65536 | bytes 395520 | tf_op jit(solution)/shard_map/neg | solution.py:269
  37.1 1.3 %stack.46 = s32[1,2,2,128]{3,2,1,0:T(2,128)} reshape(s32[2,256]{1,0:T(2,128)} %copy-done.15) | data formatting | bytes 4096 | tf_op jit(solution)/shard_map/stack | solution.py:271
  38.4 0.7 add_bitcast_fusion
  39.1 2.9 %collective-permute-done.8.rest_2_ = bf16[640,256]{1,0:T(8,128)(2,1)} collective-permute-done((bf16[640,256]{1,0:T(8,128)(2,1)}, bf16[640,256]{1,0:T(8,128)(2,1)}, u32[]{:S(2)}, u32[]{:S(2)}) %collective-permute-start.8) | collective-permute-done | bytes 327712 | tf_op jit(solution)/shard_map/ppermute | solution.py:168
  42.0 0.7 slice.73.rest_10_
  42.7 3.4 %collective-permute-done.9.rest_5_ = bf16[640,256]{1,0:T(8,128)(2,1)} collective-permute-done((bf16[640,256]{1,0:T(8,128)(2,1)}, bf16[640,256]{1,0:T(8,128)(2,1)}, u32[]{:S(2)}, u32[]{:S(2)}) %collective-permute-start.9) | collective-permute-done | bytes 327712 | tf_op jit(solution)/shard_map/ppermute | solution.py:168
  46.0 0.7 slice.74.rest_11_
  46.7 1.5 %collective-permute-start.13 = (bf16[640,256]{1,0:T(8,128)(2,1)}, bf16[640,256]{1,0:T(8,128)(2,1)S(1)}, u32[]{:S(2)}, u32[]{:S(2)}) collective-permute-start(bf16[640,256]{1,0:T(8,128)(2,1)} %collective-permute-done.7.rest_0_), channel_id=1, source_target_pairs={{0,1},{1,0},{2,3},{3,2},{4,5},{5,4},{6,7},{7,6},{8,9},{9,8},{10,11... | collective-permute-start | bytes 983048 | tf_op jit(solution)/shard_map/ppermute | solution.py:168
  48.2 1.3 %collective-permute-start.10 = (bf16[640,256]{1,0:T(8,128)(2,1)}, bf16[640,256]{1,0:T(8,128)(2,1)S(1)}, u32[]{:S(2)}, u32[]{:S(2)}) collective-permute-start(bf16[640,256]{1,0:T(8,128)(2,1)} %collective-permute-done.7.rest_0_), channel_id=1, source_target_pairs={{0,4},{4,0},{1,5},{5,1},{2,6},{6,2},{3,7},{7,3},{8,12},{12,8},{9,1... | collective-permute-start | bytes 983048 | tf_op jit(solution)/shard_map/ppermute | solution.py:168
  49.5 0.7 collective-permute-start.15
  50.8 0.9 %copy-done.4 = s32[256,1]{1,0:T(8,128)S(1)} copy-done((s32[256,1]{1,0:T(8,128)S(1)}, s32[256,1]{1,0:T(8,128)}, u32[]{:S(2)}) %copy-start.4) | copy-done | bytes 1048
  51.7 0.9 %copy-done.5 = s32[256,1]{1,0:T(8,128)S(1)} copy-done((s32[256,1]{1,0:T(8,128)S(1)}, s32[256,1]{1,0:T(8,128)}, u32[]{:S(2)}) %copy-start.5) | copy-done | bytes 1048
  52.6 0.9 mask.1
  53.5 1.7 %copy-done.1 = bf16[8,256,640]{2,1,0:T(8,128)(2,1)S(1)} copy-done((bf16[8,256,640]{2,1,0:T(8,128)(2,1)S(1)}, bf16[8,256,640]{2,1,0:T(8,128)(2,1)}, u32[]{:S(2)}) %copy-start.1) | copy-done | bytes 2621464
  55.2 0.6 copy-done.7
  55.9 4.3 %project.3.rest_6_ = f32[2,512,256]{2,1,0:T(8,128)S(1)} custom-call(s32[3]{0:T(128)S(1)} %copy-done.7, bf16[8,256,640]{2,1,0:T(8,128)(2,1)S(1)} %norm.2.own, bf16[8,256,640]{2,1,0:T(8,128)(2,1)S(1)} %copy-done.1, bf16[2,640,256]{2,1,0:T(8,128)(2,1)S(1)} %constant_dynamic-update-slice_fusion.rest_0_, bf16[2,640,256]{2,1,0:T(8,128)(2,1)} %collective-permute-done.5.rest_1_, ...), custom_call_target="tpu_custom_call" | custom-call | flops 1342177280 | bytes 5242880 | tf_op jit(solution)/shard_map/project/pallas_call | solution.py:309
  60.2 1.3 %collective-permute-start.14 = (bf16[320,256]{1,0:T(8,128)(2,1)S(1)}, bf16[320,256]{1,0:T(8,128)(2,1)S(1)}, u32[]{:S(2)}, u32[]{:S(2)}) collective-permute-start(bf16[320,256]{1,0:T(8,128)(2,1)S(1)} %slice.77), channel_id=1, source_target_pairs={{0,4},{4,0},{1,5},{5,1},{2,6},{6,2},{3,7},{7,3},{8,12},{12,8},{9,1... | collective-permute-start | bytes 491528 | tf_op jit(solution)/shard_map/ppermute | solution.py:168
  61.6 1.6 %collective-permute-start.12 = (bf16[320,256]{1,0:T(8,128)(2,1)S(1)}, bf16[320,256]{1,0:T(8,128)(2,1)S(1)}, u32[]{:S(2)}, u32[]{:S(2)}) collective-permute-start(bf16[320,256]{1,0:T(8,128)(2,1)S(1)} %slice.75), channel_id=1, source_target_pairs={{0,1},{1,0},{2,3},{3,2},{4,5},{5,4},{6,7},{7,6},{8,9},{9,8},{10,11... | collective-permute-start | bytes 491528 | tf_op jit(solution)/shard_map/ppermute | solution.py:168
  63.3 1.8 %collective-permute-done.15.rest_3_ = bf16[640,256]{1,0:T(8,128)(2,1)S(1)} collective-permute-done((bf16[640,256]{1,0:T(8,128)(2,1)}, bf16[640,256]{1,0:T(8,128)(2,1)S(1)}, u32[]{:S(2)}, u32[]{:S(2)}) %collective-permute-start.15) | collective-permute-done | bytes 327712 | tf_op jit(solution)/shard_map/ppermute | solution.py:168
  65.2 3.6 %project.4.rest_14_ = f32[2,512,256]{2,1,0:T(8,128)S(1)} custom-call(s32[3]{0:T(128)S(1)} %copy-done.8, bf16[8,256,640]{2,1,0:T(8,128)(2,1)S(1)} %norm.2.own, bf16[8,256,640]{2,1,0:T(8,128)(2,1)S(1)} %copy-done.1, bf16[640,256]{1,0:T(8,128)(2,1)} %collective-permute-done.7.rest_0_, bf16[640,256]{1,0:T(8,128)(2,1)S(1)} %collective-permute-done.13.rest_1_, ...), custom_call_target="tpu_custom_call" | custom-call | flops 1006632960 | bytes 3932160 | tf_op jit(solution)/shard_map/project/pallas_call | solution.py:309
  68.9 2.5 %project.5 = (bf16[256,512]{1,0:T(8,128)(2,1)S(1)}, bf16[256,512]{1,0:T(8,128)(2,1)S(1)}) custom-call(s32[3]{0:T(128)S(1)} %copy-done.8, bf16[8,256,640]{2,1,0:T(8,128)(2,1)S(1)} %norm.2.own, bf16[8,256,640]{2,1,0:T(8,128)(2,1)S(1)} %copy-done.1, bf16[640,256]{1,0:T(8,128)(2,1)S(1)} %collective-permute-done.10.rest_0_, ...), custom_call_target="tpu_custom_call" | custom-call | flops 335544320 | bytes 1310720 | tf_op jit(solution)/shard_map/project/pallas_call | solution.py:309
  71.4 0.8 collective-permute-start.20
  72.2 1.4 %collective-permute-start.19 = (bf16[256,512]{1,0:T(8,128)(2,1)S(1)}, bf16[256,512]{1,0:T(8,128)(2,1)S(1)}, u32[]{:S(2)}, u32[]{:S(2)}) collective-permute-start(bf16[256,512]{1,0:T(8,128)(2,1)S(1)} %get-tuple-element.49), channel_id=1, source_target_pairs={{0,3},{1,2},{2,1},{3,0},{4,7},{5,6},{6,5},{7,4},{8,11},{9,10},{10,... | collective-permute-start | bytes 786440 | tf_op jit(solution)/shard_map/ppermute | solution.py:191
  73.6 6.9 %collective-permute-done.20.rest_1_ = bf16[256,512]{1,0:T(8,128)(2,1)S(1)} collective-permute-done((bf16[256,512]{1,0:T(8,128)(2,1)S(1)}, bf16[256,512]{1,0:T(8,128)(2,1)S(1)}, u32[]{:S(2)}, u32[]{:S(2)}) %collective-permute-start.20) | collective-permute-done | bytes 262176 | tf_op jit(solution)/shard_map/ppermute | solution.py:191
  80.5 4.7 %attend.2.rest_2_ = bf16[256,4096]{1,0:T(8,128)(2,1)} custom-call(s32[1]{0:T(128)} %bitcast.place, s32[2]{0:T(128)S(1)} %get-tuple-element.31.needs, bf16[256,4096]{1,0:T(8,128)(2,1)S(1)} %bitcast.28, f32[256,512]{1,0:T(8,128)S(1)} %get-tuple-element.32.bias, bf16[256,512]{1,0:T(8,128)(2,1)S(1)} %get-tuple-element.50.rest_0_, ...), custom_call_target="tpu_custom_call" | custom-call | flops 1073741824 | bytes 2097152 | tf_op jit(solution)/shard_map/attend/pallas_call | solution.py:345
  85.2 4.9 %attend.3 = bf16[256,4096]{1,0:T(8,128)(2,1)} custom-call(s32[1]{0:T(128)} %bitcast.place, s32[2]{0:T(128)S(1)} %get-tuple-element.31.needs, bf16[256,4096]{1,0:T(8,128)(2,1)S(1)} %bitcast.29, f32[256,512]{1,0:T(8,128)S(1)} %get-tuple-element.32.bias, bf16[256,512]{1,0:T(8,128)(2,1)S(1)} %collective-permute-done.18.rest_0_, ...), custom_call_target="tpu_custom_call", output_to_operand_aliasing={{}: (6, {})} | custom-call | flops 1073741824 | bytes 2097152 | tf_op jit(solution)/shard_map/attend/pallas_call | solution.py:345
  (70 shorter events, 2.8 us)
Async XLA Ops:
  0.0 13.6 %copy-start.6 = (f32[5120]{0:T(1024)S(1)}, f32[5120]{0:T(1024)}, u32[]{:S(2)}) copy-start(f32[5120]{0:T(1024)} %param.11) | copy-start | bytes 61444
  0.0 24.3 %collective-permute-start.2 = (bf16[1,256,5120]{2,1,0:T(8,128)(2,1)}, bf16[1,256,5120]{2,1,0:T(8,128)(2,1)}, u32[]{:S(2)}, u32[]{:S(2)}) collective-permute-start(bf16[1,256,5120]{2,1,0:T(8,128)(2,1)} %param.9), channel_id=1, source_target_pairs={{0,2},{2,0},{1,3},{3,1},{4,6},{6,4},{5,7},{7,5},{8,10},{10,8},{9,1... | collective-permute-start | bytes 7864328 | tf_op jit(solution)/shard_map/ppermute | solution.py:168
  1.7 3.8 %collective-permute-start = (bf16[2,320,256]{2,1,0:T(8,128)(2,1)S(1)}, bf16[2,320,256]{2,1,0:T(8,128)(2,1)S(1)}, u32[]{:S(2)}, u32[]{:S(2)}) collective-permute-start(bf16[2,320,256]{2,1,0:T(8,128)(2,1)S(1)} %pad_maximum_fusion), channel_id=1, source_target_pairs={{0,2},{2,0},{1,3},{3,1},{4,6},{6,4},{5,7},{7,5},{8,10},{10,8},{9,1... | collective-permute-start | bytes 983048 | tf_op jit(solution)/shard_map/ppermute | solution.py:168
  5.5 18.1 %collective-permute-start.5 = (bf16[2,640,256]{2,1,0:T(8,128)(2,1)S(1)}, bf16[2,640,256]{2,1,0:T(8,128)(2,1)}, u32[]{:S(2)}, u32[]{:S(2)}) collective-permute-start(bf16[2,640,256]{2,1,0:T(8,128)(2,1)S(1)} %constant_dynamic-update-slice_fusion.rest_0_), channel_id=1, source_target_pairs={{0,4},{4,0},{1,5},{5,1},{2,6},{6,2},{3,7},{7,3},{8,12},{12,8},{9,1... | collective-permute-start | bytes 1966088 | tf_op jit(solution)/shard_map/ppermute | solution.py:168
  9.2 20.2 %collective-permute-start.3 = (bf16[640,256]{1,0:T(8,128)(2,1)}, bf16[640,256]{1,0:T(8,128)(2,1)}, u32[]{:S(2)}, u32[]{:S(2)}) collective-permute-start(bf16[640,256]{1,0:T(8,128)(2,1)} %dynamic-slice_bitcast_fusion), channel_id=1, source_target_pairs={{0,8},{8,16},{16,24},{24,0},{1,9},{9,17},{17,25},{25,1},{2,10},{10... | collective-permute-start | bytes 983048 | tf_op jit(solution)/shard_map/ppermute | solution.py:239
  10.8 18.6 %collective-permute-start.4 = (bf16[640,256]{1,0:T(8,128)(2,1)}, bf16[640,256]{1,0:T(8,128)(2,1)}, u32[]{:S(2)}, u32[]{:S(2)}) collective-permute-start(bf16[640,256]{1,0:T(8,128)(2,1)} %dynamic-slice_bitcast_fusion), channel_id=1, source_target_pairs={{0,24},{8,0},{16,8},{24,16},{1,25},{9,1},{17,9},{25,17},{2,26},{10... | collective-permute-start | bytes 983048 | tf_op jit(solution)/shard_map/ppermute | solution.py:239
  13.6 1.7 %copy-start.3 = (bf16[1,256,5120]{2,1,0:T(8,128)(2,1)S(1)}, bf16[1,256,5120]{2,1,0:T(8,128)(2,1)}, u32[]{:S(2)}) copy-start(bf16[1,256,5120]{2,1,0:T(8,128)(2,1)} %param.9) | copy-start | bytes 7864324
  15.4 1.8 %copy-start.14 = (s32[1,256]{1,0:T(1,128)S(1)}, s32[1,256]{1,0:T(1,128)}, u32[]{:S(2)}) copy-start(s32[1,256]{1,0:T(1,128)} %param.16) | copy-start | bytes 3076
  15.4 1.9 %copy-start.16 = (s32[1,256]{1,0:T(1,128)S(1)}, s32[1,256]{1,0:T(1,128)}, u32[]{:S(2)}) copy-start(s32[1,256]{1,0:T(1,128)} %param.15) | copy-start | bytes 3076
  17.1 2.3 %collective-permute-start.6 = (s32[1,256]{1,0:T(1,128)S(1)}, s32[1,256]{1,0:T(1,128)S(1)}, u32[]{:S(2)}, u32[]{:S(2)}) collective-permute-start(s32[1,256]{1,0:T(1,128)S(1)} %copy-done.14), channel_id=1, source_target_pairs={{0,2},{2,0},{1,3},{3,1},{4,6},{6,4},{5,7},{7,5},{8,10},{10,8},{9,1... | collective-permute-start | bytes 3080 | tf_op jit(solution)/shard_map/ppermute | solution.py:168
  19.5 3.6 %collective-permute-start.1 = (s32[2,256]{1,0:T(2,128)S(1)}, s32[2,256]{1,0:T(2,128)S(1)}, u32[]{:S(2)}, u32[]{:S(2)}) collective-permute-start(s32[2,256]{1,0:T(2,128)S(1)} %pad_add_fusion), channel_id=1, source_target_pairs={{0,1},{1,0},{2,3},{3,2},{4,5},{5,4},{6,7},{7,6},{8,9},{9,8},{10,11... | collective-permute-start | bytes 6152 | tf_op jit(solution)/shard_map/ppermute | solution.py:191
  23.0 13.9 %copy-start.15 = (s32[2,256]{1,0:T(2,128)}, s32[2,256]{1,0:T(2,128)S(1)}, u32[]{:S(2)}) copy-start(s32[2,256]{1,0:T(2,128)S(1)} %collective-permute-done.1) | copy-start | bytes 6148
  24.3 10.9 %copy-start.17 = (f32[64]{0:T(128)S(1)}, f32[64]{0:T(128)}, u32[]{:S(2)}) copy-start(f32[64]{0:T(128)} %constant.43) | copy-start | bytes 772
  27.9 1.5 %copy-start = (bf16[8,256,640]{2,1,0:T(8,128)(2,1)}, bf16[8,256,640]{2,1,0:T(8,128)(2,1)S(1)}, u32[]{:S(2)}) copy-start(bf16[8,256,640]{2,1,0:T(8,128)(2,1)S(1)} %norm.3.other) | copy-start | bytes 7864324
  29.4 20.1 %collective-permute-start.11 = (bf16[640,256]{1,0:T(8,128)(2,1)}, bf16[640,256]{1,0:T(8,128)(2,1)}, u32[]{:S(2)}, u32[]{:S(2)}) collective-permute-start(bf16[640,256]{1,0:T(8,128)(2,1)} %collective-permute-done.3.rest_2_), channel_id=1, source_target_pairs={{0,1},{1,0},{2,3},{3,2},{4,5},{5,4},{6,7},{7,6},{8,9},{9,8},{10,11... | collective-permute-start | bytes 983048 | tf_op jit(solution)/shard_map/ppermute | solution.py:168
  31.0 11.0 %collective-permute-start.8 = (bf16[640,256]{1,0:T(8,128)(2,1)}, bf16[640,256]{1,0:T(8,128)(2,1)}, u32[]{:S(2)}, u32[]{:S(2)}) collective-permute-start(bf16[640,256]{1,0:T(8,128)(2,1)} %collective-permute-done.3.rest_2_), channel_id=1, source_target_pairs={{0,4},{4,0},{1,5},{5,1},{2,6},{6,2},{3,7},{7,3},{8,12},{12,8},{9,1... | collective-permute-start | bytes 983048 | tf_op jit(solution)/shard_map/ppermute | solution.py:168
  32.6 14.2 %collective-permute-start.7 = (bf16[640,256]{1,0:T(8,128)(2,1)}, bf16[640,256]{1,0:T(8,128)(2,1)}, u32[]{:S(2)}, u32[]{:S(2)}) collective-permute-start(bf16[640,256]{1,0:T(8,128)(2,1)} %collective-permute-done.3.rest_2_), channel_id=1, source_target_pairs={{0,8},{8,16},{16,24},{24,0},{1,9},{9,17},{17,25},{25,1},{2,10},{10... | collective-permute-start | bytes 983048 | tf_op jit(solution)/shard_map/ppermute | solution.py:239
  34.1 11.9 %collective-permute-start.9 = (bf16[640,256]{1,0:T(8,128)(2,1)}, bf16[640,256]{1,0:T(8,128)(2,1)}, u32[]{:S(2)}, u32[]{:S(2)}) collective-permute-start(bf16[640,256]{1,0:T(8,128)(2,1)} %collective-permute-done.4.rest_4_), channel_id=1, source_target_pairs={{0,1},{1,0},{2,3},{3,2},{4,5},{5,4},{6,7},{7,6},{8,9},{9,8},{10,11... | collective-permute-start | bytes 983048 | tf_op jit(solution)/shard_map/ppermute | solution.py:168
  34.7 15.6 %collective-permute-start.16 = (bf16[640,256]{1,0:T(8,128)(2,1)}, bf16[640,256]{1,0:T(8,128)(2,1)}, u32[]{:S(2)}, u32[]{:S(2)}) collective-permute-start(bf16[640,256]{1,0:T(8,128)(2,1)} %collective-permute-done.4.rest_4_), channel_id=1, source_target_pairs={{0,4},{4,0},{1,5},{5,1},{2,6},{6,2},{3,7},{7,3},{8,12},{12,8},{9,1... | collective-permute-start | bytes 983048 | tf_op jit(solution)/shard_map/ppermute | solution.py:168
  46.7 13.5 %collective-permute-start.13 = (bf16[640,256]{1,0:T(8,128)(2,1)}, bf16[640,256]{1,0:T(8,128)(2,1)S(1)}, u32[]{:S(2)}, u32[]{:S(2)}) collective-permute-start(bf16[640,256]{1,0:T(8,128)(2,1)} %collective-permute-done.7.rest_0_), channel_id=1, source_target_pairs={{0,1},{1,0},{2,3},{3,2},{4,5},{5,4},{6,7},{7,6},{8,9},{9,8},{10,11... | collective-permute-start | bytes 983048 | tf_op jit(solution)/shard_map/ppermute | solution.py:168
  48.2 13.4 %collective-permute-start.10 = (bf16[640,256]{1,0:T(8,128)(2,1)}, bf16[640,256]{1,0:T(8,128)(2,1)S(1)}, u32[]{:S(2)}, u32[]{:S(2)}) collective-permute-start(bf16[640,256]{1,0:T(8,128)(2,1)} %collective-permute-done.7.rest_0_), channel_id=1, source_target_pairs={{0,4},{4,0},{1,5},{5,1},{2,6},{6,2},{3,7},{7,3},{8,12},{12,8},{9,1... | collective-permute-start | bytes 983048 | tf_op jit(solution)/shard_map/ppermute | solution.py:168
  49.5 15.7 %collective-permute-start.15 = (bf16[640,256]{1,0:T(8,128)(2,1)}, bf16[640,256]{1,0:T(8,128)(2,1)S(1)}, u32[]{:S(2)}, u32[]{:S(2)}) collective-permute-start(bf16[640,256]{1,0:T(8,128)(2,1)} %collective-permute-done.11.rest_3_), channel_id=1, source_target_pairs={{0,4},{4,0},{1,5},{5,1},{2,6},{6,2},{3,7},{7,3},{8,12},{12,8},{9,1... | collective-permute-start | bytes 983048 | tf_op jit(solution)/shard_map/ppermute | solution.py:168
  50.3 14.9 %collective-permute-start.17 = (bf16[640,256]{1,0:T(8,128)(2,1)}, bf16[640,256]{1,0:T(8,128)(2,1)S(1)}, u32[]{:S(2)}, u32[]{:S(2)}) collective-permute-start(bf16[640,256]{1,0:T(8,128)(2,1)} %collective-permute-done.16.rest_4_), channel_id=1, source_target_pairs={{0,1},{1,0},{2,3},{3,2},{4,5},{5,4},{6,7},{7,6},{8,9},{9,8},{10,11... | collective-permute-start | bytes 983048 | tf_op jit(solution)/shard_map/ppermute | solution.py:168
  50.8 0.9 %copy-start.4 = (s32[256,1]{1,0:T(8,128)S(1)}, s32[256,1]{1,0:T(8,128)}, u32[]{:S(2)}) copy-start(s32[256,1]{1,0:T(8,128)} %copy.15.seg_q) | copy-start | bytes 3076
  51.7 0.9 %copy-start.5 = (s32[256,1]{1,0:T(8,128)S(1)}, s32[256,1]{1,0:T(8,128)}, u32[]{:S(2)}) copy-start(s32[256,1]{1,0:T(8,128)} %copy.16.pos_q) | copy-start | bytes 3076
  53.5 1.7 %copy-start.1 = (bf16[8,256,640]{2,1,0:T(8,128)(2,1)S(1)}, bf16[8,256,640]{2,1,0:T(8,128)(2,1)}, u32[]{:S(2)}) copy-start(bf16[8,256,640]{2,1,0:T(8,128)(2,1)} %copy-done) | copy-start | bytes 7864324
  55.2 0.6 copy-start.7
  55.9 7.3 %copy-start.12 = (f32[512,64]{1,0:T(8,128)S(1)}, f32[512,64]{1,0:T(8,128)}, u32[]{:S(2)}) copy-start(f32[512,64]{1,0:T(8,128)} %get-tuple-element.57) | copy-start | bytes 393220
  55.9 7.3 %copy-start.13 = (f32[512,64]{1,0:T(8,128)S(1)}, f32[512,64]{1,0:T(8,128)}, u32[]{:S(2)}) copy-start(f32[512,64]{1,0:T(8,128)} %get-tuple-element.58) | copy-start | bytes 393220
  55.9 9.3 %copy-start.8 = (s32[3]{0:T(128)S(1)}, s32[3]{0:T(128)}, u32[]{:S(2)}) copy-start(s32[3]{0:T(128)} %pad_add_fusion.1.place) | copy-start | bytes 40
  60.2 8.6 %collective-permute-start.14 = (bf16[320,256]{1,0:T(8,128)(2,1)S(1)}, bf16[320,256]{1,0:T(8,128)(2,1)S(1)}, u32[]{:S(2)}, u32[]{:S(2)}) collective-permute-start(bf16[320,256]{1,0:T(8,128)(2,1)S(1)} %slice.77), channel_id=1, source_target_pairs={{0,4},{4,0},{1,5},{5,1},{2,6},{6,2},{3,7},{7,3},{8,12},{12,8},{9,1... | collective-permute-start | bytes 491528 | tf_op jit(solution)/shard_map/ppermute | solution.py:168
  61.6 7.2 %collective-permute-start.12 = (bf16[320,256]{1,0:T(8,128)(2,1)S(1)}, bf16[320,256]{1,0:T(8,128)(2,1)S(1)}, u32[]{:S(2)}, u32[]{:S(2)}) collective-permute-start(bf16[320,256]{1,0:T(8,128)(2,1)S(1)} %slice.75), channel_id=1, source_target_pairs={{0,1},{1,0},{2,3},{3,2},{4,5},{5,4},{6,7},{7,6},{8,9},{9,8},{10,11... | collective-permute-start | bytes 491528 | tf_op jit(solution)/shard_map/ppermute | solution.py:168
  63.3 5.5 %copy-start.9 = (s32[2,128]{1,0:T(2,128)S(1)}, s32[2,128]{1,0:T(2,128)}, u32[]{:S(2)}) copy-start(s32[2,128]{1,0:T(2,128)} %slice.72.rest_9_) | copy-start | bytes 3076
  63.3 5.5 %copy-start.10 = (f32[128]{0:T(128)S(1)}, f32[128]{0:T(128)}, u32[]{:S(2)}) copy-start(f32[128]{0:T(128)} %param.12) | copy-start | bytes 1540
  63.3 5.5 %copy-start.11 = (s32[1,128]{1,0:T(1,128)S(1)}, s32[1,128]{1,0:T(1,128)}, u32[]{:S(2)}) copy-start(s32[1,128]{1,0:T(1,128)} %slice.71.rest_8_) | copy-start | bytes 1540
  68.9 11.6 %copy-start.2 = (bf16[1,256,4096]{2,1,0:T(8,128)(2,1)S(1)}, bf16[1,256,4096]{2,1,0:T(8,128)(2,1)}, u32[]{:S(2)}) copy-start(bf16[1,256,4096]{2,1,0:T(8,128)(2,1)} %param.10) | copy-start | bytes 6291460
  71.4 9.1 %collective-permute-start.20 = (bf16[256,512]{1,0:T(8,128)(2,1)S(1)}, bf16[256,512]{1,0:T(8,128)(2,1)S(1)}, u32[]{:S(2)}, u32[]{:S(2)}) collective-permute-start(bf16[256,512]{1,0:T(8,128)(2,1)S(1)} %get-tuple-element.50.rest_0_), channel_id=1, source_target_pairs={{0,1},{1,0},{2,3},{3,2},{4,5},{5,4},{6,7},{7,6},{8,9},{9,8},{10,11... | collective-permute-start | bytes 786440 | tf_op jit(solution)/shard_map/ppermute | solution.py:191
  72.2 13.0 %collective-permute-start.18 = (bf16[256,512]{1,0:T(8,128)(2,1)S(1)}, bf16[256,512]{1,0:T(8,128)(2,1)S(1)}, u32[]{:S(2)}, u32[]{:S(2)}) collective-permute-start(bf16[256,512]{1,0:T(8,128)(2,1)S(1)} %get-tuple-element.49), channel_id=1, source_target_pairs={{0,2},{1,3},{2,0},{3,1},{4,6},{5,7},{6,4},{7,5},{8,10},{9,11},{10,... | collective-permute-start | bytes 786440 | tf_op jit(solution)/shard_map/ppermute | solution.py:191
  72.2 13.0 %collective-permute-start.19 = (bf16[256,512]{1,0:T(8,128)(2,1)S(1)}, bf16[256,512]{1,0:T(8,128)(2,1)S(1)}, u32[]{:S(2)}, u32[]{:S(2)}) collective-permute-start(bf16[256,512]{1,0:T(8,128)(2,1)S(1)} %get-tuple-element.49), channel_id=1, source_target_pairs={{0,3},{1,2},{2,1},{3,0},{4,7},{5,6},{6,5},{7,4},{8,11},{9,10},{10,... | collective-permute-start | bytes 786440 | tf_op jit(solution)/shard_map/ppermute | solution.py:191

commit v3 on v2

--- a/solution.py
+++ b/solution.py
@@ -20,20 +20,28 @@
 NORM_ROWS = 64
 
 
-def norm_kernel(chunks, hidden, gain, out):
-    inputs = hidden[...].astype(jnp.float32)
-    scale = lax.rsqrt(jnp.mean(inputs * inputs, axis=-1, keepdims=True) + EPS)
-    normed = (inputs * scale * gain[...]).astype(jnp.bfloat16)
-    rows = normed.shape[1] // chunks
-    for j in range(chunks):
-        out[j] = normed[:, j * rows : (j + 1) * rows]
-
-
-def project_kernel(chips_z, groups, first, last, count, tokens, place, own, other, *rest):
+def norm_kernel(chunks, hidden, gain, out, held, sems):
+    steps = held.shape[0] // NORM_ROWS
+    copies = []
+    for i in range(steps):
+        at = pl.ds(i * NORM_ROWS, NORM_ROWS)
+        copies.append(pltpu.make_async_copy(hidden.at[at], held.at[at], sems.at[i]))
+        copies[-1].start()
+    for i, copy in enumerate(copies):
+        copy.wait()
+        at = pl.ds(i * NORM_ROWS, NORM_ROWS)
+        inputs = held[at, :].astype(jnp.float32)
+        scale = lax.rsqrt(jnp.mean(inputs * inputs, axis=-1, keepdims=True) + EPS)
+        normed = (inputs * scale * gain[...]).astype(jnp.bfloat16)
+        rows = normed.shape[1] // chunks
+        for j in range(chunks):
+            out[j, at, :] = normed[:, j * rows : (j + 1) * rows]
+
+
+def project_kernel(chips_z, groups, first, last, count, place, own, other, *rest):
     z, y, x = place[0], place[1], place[2]
     rest = list(rest)
     weight, lhs, sems = rest[-3:]
-    rows = weight.shape[2]
     waits = []
     for g, (k, near) in enumerate(groups):
         p = lax.rem(z - k + chips_z, chips_z)
@@ -44,14 +52,9 @@
         ]
         if k == 0:
             pairs.append((rest.pop(0), weight.at[g]))
-        elif near or k != chips_z // 2:
+        else:
             pairs.append((rest.pop(0), weight.at[g, x]))
             pairs.append((rest.pop(0), weight.at[g, 1 - x]))
-        else:
-            pairs.append((rest.pop(0), weight.at[g, x]))
-            for part in range(2):
-                at = pl.ds(part * (rows // 2), rows // 2)
-                pairs.append((rest.pop(0), weight.at[g, 1 - x, at]))
         copies = [
             pltpu.make_async_copy(source, target, sems.at[g, i])
             for i, (source, target) in enumerate(pairs)
@@ -59,8 +62,6 @@
         for copy in copies:
             copy.start()
         waits.append(copies)
-    if last:
-        rest = rest[tokens:]
     earlier = None if first else rest.pop(0)
     terms = [None, None]
     for g, copies in enumerate(waits):
@@ -91,16 +92,25 @@
             )
 
 
-def mask_kernel(seg_q, pos_q, seg_k, pos_k, bias, needs):
-    allowed = (seg_k[...] == seg_q[...]) & (pos_k[...] <= pos_q[...])
-    bias[...] = jnp.where(allowed, 0.0, MASKED)
-    rows, columns = bias.shape[0] // 2, bias.shape[1] // 2
+def mask_kernel(*refs):
+    pieces, (bias, needs) = refs[:-2], refs[-2:]
+    count = bias.shape[0]
+    half_rows = count // 2
+    seg_q, pos_q = (
+        jnp.transpose(jnp.broadcast_to(pieces[0][i : i + 1, :], (half_rows, count)))
+        for i in range(2)
+    )
+    half_width = len(pieces) * half_rows
+    for half in range(2):
+        for i, piece in enumerate(pieces):
+            at = slice(half * half_rows, (half + 1) * half_rows)
+            allowed = (piece[:1, at] == seg_q) & (piece[1:, at] <= pos_q)
+            there = half * half_width + i * half_rows
+            bias[:, there : there + half_rows] = jnp.where(allowed, 0.0, MASKED)
     for tile in range(2):
+        rows = slice(tile * half_rows, (tile + 1) * half_rows)
         found = [
-            jnp.max(
-                bias[tile * rows : (tile + 1) * rows, half * columns : (half + 1) * columns]
-            )
-            == 0.0
+            jnp.max(bias[rows, half * half_width : (half + 1) * half_width]) == 0.0
             for half in range(2)
         ]
         needs[tile] = found[0].astype(jnp.int32) + 2 * found[1].astype(jnp.int32)
@@ -196,92 +206,83 @@
             [lax.dynamic_slice_in_dim(w, at, 2 * HD, 1) for w in (k_weight, v_weight)]
         )
 
-    tokens = []
-
-    def after(array, *others):
-        corners = [
-            other[tuple(slice(0, size) for size in (1, 16, 128)[-other.ndim :])]
-            for other in others
-        ]
-        array, corners = lax.optimization_barrier((array, corners))
-        tokens.extend(corners)
-        return array
-
-    def norm(array):
-        return pl.pallas_call(
-            functools.partial(norm_kernel, chunks),
-            out_shape=jax.ShapeDtypeStruct((chunks, count, rows), bf16),
-            grid=(count // NORM_ROWS,),
-            in_specs=[pl.BlockSpec((NORM_ROWS, width), lambda i: (i, 0)), whole],
-            out_specs=pl.BlockSpec((chunks, NORM_ROWS, rows), lambda i: (0, i, 0)),
-            compiler_params=params,
-            cost_estimate=pl.CostEstimate(
-                flops=4 * count * width, bytes_accessed=4 * count * width, transcendentals=0
-            ),
-            name="norm",
-        )(array[0], norm_gain[None])
-
     taken = swap(columns(1 - core), "core")
     kept = columns(core)
-    hidden_other = swap(hidden, "core")
     chip = lax.dynamic_update_slice(
         jnp.zeros((2, rows, 2 * HD), bf16), kept, (0, core * own_rows, 0)
     )
     chip = lax.dynamic_update_slice(chip, taken, (0, (1 - core) * own_rows, 0))
-    normed = norm(after(hidden, chip))
-    segment, position = after(segment, normed), after(position, normed)
-    normed_other = norm(hidden_other)
-    position_other = swap(position, "core")
+    hidden, segment, position, chip = lax.optimization_barrier((hidden, segment, position, chip))
+    normed = pl.pallas_call(
+        functools.partial(norm_kernel, chunks),
+        out_shape=jax.ShapeDtypeStruct((chunks, count, rows), bf16),
+        in_specs=[pl.BlockSpec(memory_space=pltpu.HBM), whole],
+        out_specs=whole,
+        scratch_shapes=[
+            pltpu.VMEM((count, width), bf16),
+            pltpu.SemaphoreType.DMA((count // NORM_ROWS,)),
+        ],
+        compiler_params=params,
+        cost_estimate=pl.CostEstimate(
+            flops=4 * count * width, bytes_accessed=4 * count * width, transcendentals=0
+        ),
+        name="norm",
+    )(hidden[0], norm_gain[None])
     ints = jnp.concatenate([segment, position])
     ints_all = [ints] + [along_ctx(ints, d) for d in range(1, m)]
+    ints_other = swap(ints, "core")
 
     def ring(array, step):
         return lax.ppermute(array, "z", [(i, (i + step) % chips_z) for i in range(chips_z)])
 
+    tie = lax.optimization_barrier
     middle = chips_z // 2
     mine = {0: lax.dynamic_index_in_dim(chip, x, 0, keepdims=False)}
     across, beside, corner = {}, {}, {}
     chip_beside = swap(chip, "y")
+    mine[1], mine[chips_z - 1] = ring(mine[0], 1), ring(mine[0], -1)
+    mine[1], normed, ints_all, ints_other = tie((mine[1], normed, ints_all, ints_other))
     for r in range(1, middle + 1):
-        arrived = [r] if r == middle else [r, chips_z - r]
-        for k in arrived:
-            mine[k] = ring(mine[k - 1], 1) if k == r else ring(mine[(k + 1) % chips_z], -1)
+        if r > 1:
+            mine[r], beside[r - 1], across[chips_z - r + 1] = tie(
+                (mine[r], beside[r - 1], across[chips_z - r + 1])
+            )
+        if r < middle:
+            mine[r + 1] = ring(mine[r], 1)
+        beside[r], across[r] = swap(mine[r], "y"), swap(mine[r], "x")
         if r == 1:
-            tied = (mine[1], mine[chips_z - 1])
-            others = (chip_beside, normed_other, position_other, *ints_all[1:])
-            mine[1], mine[chips_z - 1] = after(tied, *others)
-        elif r == middle:
-            mine[r] = after(mine[r], beside[r - 1], across[chips_z - r + 1])
-        for k in arrived:
+            mine[chips_z - 1], across[1], chip_beside, normed = tie(
+                (mine[chips_z - 1], across[1], chip_beside, normed)
+            )
+            normed_other = swap(normed, "core")
+        if r < middle:
+            k = chips_z - r
+            if k - 1 > middle:
+                mine[k - 1] = ring(mine[k], -1)
             beside[k], across[k] = swap(mine[k], "y"), swap(mine[k], "x")
+        if r == 1:
+            across[chips_z - 1], normed_other = tie((across[chips_z - 1], normed_other))
     for k in range(1, chips_z):
-        if k < middle:
-            corner[k] = swap(across[k], "y")
-        elif k > middle:
-            corner[k] = swap(beside[k], "x")
-
-    where = jnp.concatenate([position[0], position_other[0]]).astype(jnp.float32)
+        corner[k] = swap(beside[k], "x") if k <= middle else swap(across[k], "y")
+
+    where = jnp.concatenate([position[0], ints_other[1]]).astype(jnp.float32)
     half = HD // 2
     freq = np.exp(np.arange(half, dtype=np.float32) * np.float32(-2.0 * math.log(THETA) / HD))
     angle = where[:, None] * freq[None, :]
     cosine, sine = jnp.cos(angle), jnp.sin(angle)
     cosine = jnp.concatenate([cosine, cosine], axis=1)
     sine = jnp.concatenate([-sine, sine], axis=1)
-    order = (
-        jnp.stack(ints_all).reshape(m, 2, 2, count // 2).transpose(1, 2, 0, 3).reshape(2, m * count)
-    )
     bias, needs = pl.pallas_call(
         mask_kernel,
         out_shape=[
             jax.ShapeDtypeStruct((count, m * count), jnp.float32),
             jax.ShapeDtypeStruct((2,), jnp.int32),
         ],
-        in_specs=[whole] * 4,
+        in_specs=[whole] * m,
         out_specs=[whole, pl.BlockSpec(memory_space=pltpu.SMEM)],
         compiler_params=params,
         name="mask",
-    )(segment.reshape(count, 1), position.reshape(count, 1), order[:1], order[1:])
-
+    )(*ints_all)
 
     place = jnp.stack([z, y, x]).astype(jnp.int32)
     acc_shape = jax.ShapeDtypeStruct((2, 2 * count, 2 * HD), jnp.float32)
@@ -293,32 +294,24 @@
     acc = []
     for groups in (early, late, final):
         first, last = groups is early, groups is final
-        if groups is late:
-            top, bottom = beside[middle][: rows // 2], across[middle][rows // 2 :]
-            corner[middle] = (
-                swap(after(top, acc[0]), "x"), swap(after(bottom, bias), "y")
-            )
         arrays = []
         for k, near in groups:
             if k == 0:
                 arrays.append(chip if near else chip_beside)
             else:
                 arrays += [mine[k], across[k]] if near else [beside[k], corner[k]]
-        arrays = jax.tree.leaves(arrays)
         anywhere = pl.BlockSpec(memory_space=pl.ANY)
         outs = pl.pallas_call(
-            functools.partial(
-                project_kernel, chips_z, groups, first, last, count, len(tokens)
-            ),
+            functools.partial(project_kernel, chips_z, groups, first, last, count),
             out_shape=[kv_shape] * 2 if last else [acc_shape],
             in_specs=[pl.BlockSpec(memory_space=pltpu.SMEM)]
-            + [anywhere] * (2 + len(arrays) + (len(tokens) if last else 0))
+            + [anywhere] * (2 + len(arrays))
             + [whole] * (len(acc) + (3 if last else 0)),
             out_specs=[whole] * (2 if last else 1),
             scratch_shapes=[
                 pltpu.VMEM((len(groups), 2, rows, 2 * HD), bf16),
                 pltpu.VMEM((len(groups), 2 * count, rows), bf16),
-                pltpu.SemaphoreType.DMA((len(groups), 5)),
+                pltpu.SemaphoreType.DMA((len(groups), 4)),
             ],
             compiler_params=params,
             cost_estimate=pl.CostEstimate(
@@ -328,7 +321,7 @@
             ),
             name="project",
         )(
-            place, normed, normed_other, *arrays, *(tokens if last else []), *acc,
+            place, normed, normed_other, *arrays, *acc,
             *((cosine, sine, key_gain[None]) if last else ()),
         )
         acc = [outs[-1]]

time: 90.6 us -> 93.9 us (1.036)
  waiting for transfers between devices: 20.1 us -> 43 us
  local copies, waits for them, and re-layouts: 16.1 us -> 5 us
  starting transfers between devices: 23.9 us -> 20.7 us
  Pallas kernels: 26.4 us -> 23.3 us
  other arithmetic: 3.43 us -> 1.41 us
    ppermute x3, waiting for transfers between devices: 0.01 us -> 14 us  [ring(): lax.ppermute(array, 'z', [(i, (i + step) % chips_z) for i in range(chips_...]
    ppermute x14 -> x13, waiting for transfers between devices: 11.7 us -> 22.8 us  [swap(): return lax.ppermute(array, axis, [(0, 1), (1, 0)])]
    unnamed x36 -> x22, local copies, waits for them, and re-layouts: 7.4 us -> 3.66 us
    slice x15 -> x1, local copies, waits for them, and re-layouts: 3.22 us -> 0.01 us  [on_device(): where = jnp.concatenate([position[0], ints_other[1]]).astype(jnp.float32)]
    ppermute x14 -> x13, starting transfers between devices: 14.8 us -> 11.7 us  [swap(): return lax.ppermute(array, axis, [(0, 1), (1, 0)])]
    pallas_call x2 -> x1, Pallas kernels: 5.33 us -> 2.36 us  [on_device(): pl.pallas_call(functools.partial(norm_kernel, chunks), out_shape=jax.Shap...]
    ppermute x4, waiting for transfers between devices: 8.37 us -> 6.23 us  [along_ctx(): return lax.ppermute(array, ('core', 'ctx', 'x'), pairs)]
    another operation x2 -> x0, local copies, waits for them, and re-layouts: 1.86 us -> none  [on_device(): jnp.stack(ints_all).reshape(m, 2, 2, count // 2).transpose(1, 2, 0, 3)]
  transfers between devices with their start and end apart: 21 -> 20, of which waited for: 6 -> 12; matrix products, arithmetic and copies ran while one was open for 13% -> 2% of each run, Pallas kernels for 21% -> 17%
where the time goes in v3:
time: 93.9 us; the launch traced here: 93.6 us
  waiting for transfers between devices  43 us (46%)
  Pallas kernels  23.3 us (25%)
  starting transfers between devices  20.7 us (22%)
  local copies, waits for them, and re-layouts  5 us (5%)
  other arithmetic  1.41 us (2%)
    ppermute x13, waiting for transfers between devices, swap(): return lax.ppermute(array, axis, [(0, 1), (1, 0)])  22.8 us
    ppermute x3, waiting for transfers between devices, ring(): lax.ppermute(array, 'z', [(i, (i + step) % chips_z) for i in range(chips_...  14 us
    ppermute x13, starting transfers between devices, swap(): return lax.ppermute(array, axis, [(0, 1), (1, 0)])  11.7 us
    pallas_call x3, Pallas kernels, on_device(): pl.pallas_call(functools.partial(project_kernel, chips_z, groups, first,...  10.4 us
    pallas_call x2, Pallas kernels, on_device(): pl.pallas_call(functools.partial(attend_kernel, m, count), out_shape=jax....  9.61 us
    ppermute x4, waiting for transfers between devices, along_ctx(): return lax.ppermute(array, ('core', 'ctx', 'x'), pairs)  6.23 us
    ppermute x3, starting transfers between devices, ring(): lax.ppermute(array, 'z', [(i, (i + step) % chips_z) for i in range(chips_...  5.25 us
    ppermute x4, starting transfers between devices, along_ctx(): return lax.ppermute(array, ('core', 'ctx', 'x'), pairs)  3.76 us
  transfers between devices with their start and end apart: 20, of which 12 were waited for; matrix products, arithmetic and copies ran while one was open for 2% of the time, Pallas kernels for 17%

profile of v3, /device:TPU:0, one launch (start us, length us, event | category | flops | bytes accessed | tf_op | source)
XLA Modules:
  0.0 93.6 jit_solution(11963085389736531487)
XLA Ops:
  0.0 1.2 %dynamic-slice_bitcast_fusion.1 = (bf16[1,320,256]{2,1,0:T(8,128)(2,1)S(1)}, bf16[1,320,256]{2,1,0:T(8,128)(2,1)S(1)}, bf16[1,320,256]{2,1,0:T(8,128)(2,1)S(1)}, bf16[1,320,256]{2,1,0:T(8,128)(2,1)S(1)}) fusion(bf16[320,512]{1,0:T(8,128)(2,1)} %param.14, s32[]{:T(128)S(6)} %select_n.20, s32[]{:T(128)S(6)} %select_n.18, bf16[320,512]{1,0:T(8,128)(2,1)} %param.13), kind=kLoop, calls=%fused_computation.7 | loop fusion | bytes 1310728 | tf_op jit(solution)/shard_map/stack | solution.py:205
  1.3 0.5 collective-permute-start
  1.9 1.2 %collective-permute-done = bf16[2,320,256]{2,1,0:T(8,128)(2,1)S(1)} collective-permute-done((bf16[2,320,256]{2,1,0:T(8,128)(2,1)S(1)}, bf16[2,320,256]{2,1,0:T(8,128)(2,1)S(1)}, u32[]{:S(2)}, u32[]{:S(2)}) %collective-permute-start) | collective-permute-done | bytes 327712 | tf_op jit(solution)/shard_map/ppermute | solution.py:178
  3.1 3.0 %collective-permute-start.1 = (bf16[640,256]{1,0:T(8,128)(2,1)S(1)}, bf16[640,256]{1,0:T(8,128)(2,1)}, u32[]{:S(2)}, u32[]{:S(2)}) collective-permute-start(bf16[640,256]{1,0:T(8,128)(2,1)S(1)} %dynamic-slice_bitcast_fusion), channel_id=1, source_target_pairs={{0,8},{8,16},{16,24},{24,0},{1,9},{9,17},{17,25},{25,1},{2,10},{10... | collective-permute-start | bytes 983048 | tf_op jit(solution)/shard_map/ppermute | solution.py:236
  6.1 1.5 %collective-permute-start.6 = (bf16[2,640,256]{2,1,0:T(8,128)(2,1)S(1)}, bf16[2,640,256]{2,1,0:T(8,128)(2,1)S(1)}, u32[]{:S(2)}, u32[]{:S(2)}) collective-permute-start(bf16[2,640,256]{2,1,0:T(8,128)(2,1)S(1)} %constant_dynamic-update-slice_fusion.rest_0_), channel_id=1, source_target_pairs={{0,4},{4,0},{1,5},{5,1},{2,6},{6,2},{3,7},{7,3},{8,12},{12,8},{9,1... | collective-permute-start | bytes 1966088 | tf_op jit(solution)/shard_map/ppermute | solution.py:178
  7.7 1.6 %collective-permute-start.2 = (s32[2,256]{1,0:T(2,128)S(1)}, s32[2,256]{1,0:T(2,128)S(1)}, u32[]{:S(2)}, u32[]{:S(2)}) collective-permute-start(s32[2,256]{1,0:T(2,128)S(1)} %pad_add_fusion.refs_0_), channel_id=1, source_target_pairs={{0,1},{1,0},{2,3},{3,2},{4,5},{5,4},{6,7},{7,6},{8,9},{9,8},{10,11... | collective-permute-start | bytes 6152 | tf_op jit(solution)/shard_map/ppermute | solution.py:201
  9.2 2.2 %collective-permute-start.4 = (bf16[640,256]{1,0:T(8,128)(2,1)S(1)}, bf16[640,256]{1,0:T(8,128)(2,1)}, u32[]{:S(2)}, u32[]{:S(2)}) collective-permute-start(bf16[640,256]{1,0:T(8,128)(2,1)S(1)} %dynamic-slice_bitcast_fusion), channel_id=1, source_target_pairs={{0,24},{8,0},{16,8},{24,16},{1,25},{9,1},{17,9},{25,17},{2,26},{10... | collective-permute-start | bytes 983048 | tf_op jit(solution)/shard_map/ppermute | solution.py:236
  11.5 2.4 %norm.1.own = bf16[8,256,640]{2,1,0:T(8,128)(2,1)S(1)} custom-call(bf16[256,5120]{1,0:T(8,128)(2,1)S(1)} %bitcast.23, f32[1,5120]{1,0:T(1,128)S(1)} %bitcast.24), custom_call_target="tpu_custom_call" | custom-call | flops 5242880 | bytes 5242880 | tf_op jit(solution)/shard_map/norm/pallas_call | solution.py:216
  13.8 0.0 collective-permute-done.2.refs_1_
  13.9 2.9 %collective-permute-done.1.rest_2_ = bf16[640,256]{1,0:T(8,128)(2,1)} collective-permute-done((bf16[640,256]{1,0:T(8,128)(2,1)S(1)}, bf16[640,256]{1,0:T(8,128)(2,1)}, u32[]{:S(2)}, u32[]{:S(2)}) %collective-permute-start.1) | collective-permute-done | bytes 327712 | tf_op jit(solution)/shard_map/ppermute | solution.py:236
  16.8 1.7 %collective-permute-start.5 = (bf16[640,256]{1,0:T(8,128)(2,1)}, bf16[640,256]{1,0:T(8,128)(2,1)S(1)}, u32[]{:S(2)}, u32[]{:S(2)}) collective-permute-start(bf16[640,256]{1,0:T(8,128)(2,1)} %collective-permute-done.1.rest_2_), channel_id=1, source_target_pairs={{0,1},{1,0},{2,3},{3,2},{4,5},{5,4},{6,7},{7,6},{8,9},{9,8},{10,11... | collective-permute-start | bytes 983048 | tf_op jit(solution)/shard_map/ppermute | solution.py:178
  18.5 4.8 %collective-permute-done.4.rest_4_ = bf16[640,256]{1,0:T(8,128)(2,1)} collective-permute-done((bf16[640,256]{1,0:T(8,128)(2,1)S(1)}, bf16[640,256]{1,0:T(8,128)(2,1)}, u32[]{:S(2)}, u32[]{:S(2)}) %collective-permute-start.4) | collective-permute-done | bytes 327712 | tf_op jit(solution)/shard_map/ppermute | solution.py:236
  23.3 2.5 %collective-permute-done.5.rest_3_ = bf16[640,256]{1,0:T(8,128)(2,1)S(1)} collective-permute-done((bf16[640,256]{1,0:T(8,128)(2,1)}, bf16[640,256]{1,0:T(8,128)(2,1)S(1)}, u32[]{:S(2)}, u32[]{:S(2)}) %collective-permute-start.5) | collective-permute-done | bytes 327712 | tf_op jit(solution)/shard_map/ppermute | solution.py:178
  25.8 0.7 copy-done.4
  26.5 0.8 copy-done.2
  27.3 1.2 %collective-permute-start.7 = (bf16[640,256]{1,0:T(8,128)(2,1)}, bf16[640,256]{1,0:T(8,128)(2,1)}, u32[]{:S(2)}, u32[]{:S(2)}) collective-permute-start(bf16[640,256]{1,0:T(8,128)(2,1)} %collective-permute-done.4.rest_4_), channel_id=1, source_target_pairs={{0,1},{1,0},{2,3},{3,2},{4,5},{5,4},{6,7},{7,6},{8,9},{9,8},{10,11... | collective-permute-start | bytes 983048 | tf_op jit(solution)/shard_map/ppermute | solution.py:178
  28.6 1.5 %collective-permute-start.10 = (bf16[640,256]{1,0:T(8,128)(2,1)}, bf16[640,256]{1,0:T(8,128)(2,1)}, u32[]{:S(2)}, u32[]{:S(2)}) collective-permute-start(bf16[640,256]{1,0:T(8,128)(2,1)} %collective-permute-done.1.rest_2_), channel_id=1, source_target_pairs={{0,4},{4,0},{1,5},{5,1},{2,6},{6,2},{3,7},{7,3},{8,12},{12,8},{9,1... | collective-permute-start | bytes 983048 | tf_op jit(solution)/shard_map/ppermute | solution.py:178
  30.1 0.1 pad_add_fusion.1.place
  30.2 7.6 %collective-permute-done.7.rest_5_ = bf16[640,256]{1,0:T(8,128)(2,1)} collective-permute-done((bf16[640,256]{1,0:T(8,128)(2,1)}, bf16[640,256]{1,0:T(8,128)(2,1)}, u32[]{:S(2)}, u32[]{:S(2)}) %collective-permute-start.7) | collective-permute-done | bytes 327712 | tf_op jit(solution)/shard_map/ppermute | solution.py:178
  37.8 1.0 %collective-permute-done.10.rest_2_ = bf16[640,256]{1,0:T(8,128)(2,1)} collective-permute-done((bf16[640,256]{1,0:T(8,128)(2,1)}, bf16[640,256]{1,0:T(8,128)(2,1)}, u32[]{:S(2)}, u32[]{:S(2)}) %collective-permute-start.10) | collective-permute-done | bytes 327712 | tf_op jit(solution)/shard_map/ppermute | solution.py:178
  38.7 6.3 %collective-permute-done.9.rest_0_ = bf16[640,256]{1,0:T(8,128)(2,1)} collective-permute-done((bf16[640,256]{1,0:T(8,128)(2,1)}, bf16[640,256]{1,0:T(8,128)(2,1)}, u32[]{:S(2)}, u32[]{:S(2)}) %collective-permute-start.9) | collective-permute-done | bytes 327712 | tf_op jit(solution)/shard_map/ppermute | solution.py:236
  45.1 0.5 collective-permute-start.11
  45.6 1.0 %fusion = (f32[512,64]{1,0:T(8,128)S(1)}, f32[512,64]{1,0:T(8,128)S(1)}, f32[512,64]{1,0:T(8,128)S(1)}) fusion(f32[64]{0:T(128)S(1)} %copy-done.10, f32[512]{0:T(512)S(1)} %add_convert_fusion), kind=kLoop, calls=%fused_computation.11 | loop fusion | flops 65536 | bytes 395520 | tf_op jit(solution)/shard_map/neg | solution.py:274
  46.6 1.6 %collective-permute-start.15 = (bf16[640,256]{1,0:T(8,128)(2,1)}, bf16[640,256]{1,0:T(8,128)(2,1)S(1)}, u32[]{:S(2)}, u32[]{:S(2)}) collective-permute-start(bf16[640,256]{1,0:T(8,128)(2,1)} %collective-permute-done.4.rest_4_), channel_id=1, source_target_pairs={{0,4},{4,0},{1,5},{5,1},{2,6},{6,2},{3,7},{7,3},{8,12},{12,8},{9,1... | collective-permute-start | bytes 983048 | tf_op jit(solution)/shard_map/ppermute | solution.py:178
  48.2 0.5 collective-permute-start.13
  48.7 1.5 %collective-permute-start.14 = (bf16[640,256]{1,0:T(8,128)(2,1)}, bf16[640,256]{1,0:T(8,128)(2,1)S(1)}, u32[]{:S(2)}, u32[]{:S(2)}) collective-permute-start(bf16[640,256]{1,0:T(8,128)(2,1)} %collective-permute-done.10.rest_2_), channel_id=1, source_target_pairs={{0,1},{1,0},{2,3},{3,2},{4,5},{5,4},{6,7},{7,6},{8,9},{9,8},{10,11... | collective-permute-start | bytes 983048 | tf_op jit(solution)/shard_map/ppermute | solution.py:178
  50.2 0.5 collective-permute-start.16
  50.7 0.1 pad_maximum_fusion.1.rest_3_
  50.8 5.1 %collective-permute-done.11.rest_0_ = bf16[640,256]{1,0:T(8,128)(2,1)S(1)} collective-permute-done((bf16[640,256]{1,0:T(8,128)(2,1)}, bf16[640,256]{1,0:T(8,128)(2,1)S(1)}, u32[]{:S(2)}, u32[]{:S(2)}) %collective-permute-start.11) | collective-permute-done | bytes 327712 | tf_op jit(solution)/shard_map/ppermute | solution.py:178
  55.9 0.5 collective-permute-start.12
  56.5 0.1 pad_maximum_fusion.2.rest_4_
  56.6 0.0 copy-start.3
  56.6 1.1 %copy-done.3 = bf16[2,640,256]{2,1,0:T(8,128)(2,1)S(1)} copy-done((bf16[2,640,256]{2,1,0:T(8,128)(2,1)S(1)}, bf16[2,640,256]{2,1,0:T(8,128)(2,1)}, u32[]{:S(2)}) %copy-start.3) | copy-done | bytes 655384
  57.7 1.0 %copy-done.5 = bf16[640,256]{1,0:T(8,128)(2,1)S(1)} copy-done((bf16[640,256]{1,0:T(8,128)(2,1)S(1)}, bf16[640,256]{1,0:T(8,128)(2,1)}, u32[]{:S(2)}) %copy-start.5) | copy-done | bytes 327704
  58.7 4.2 %project.3.rest_6_ = f32[2,512,256]{2,1,0:T(8,128)S(1)} custom-call(s32[3]{0:T(128)S(1)} %pad_add_fusion.1.place, bf16[8,256,640]{2,1,0:T(8,128)(2,1)S(1)} %norm.1.own, bf16[8,256,640]{2,1,0:T(8,128)(2,1)} %collective-permute-done.8.other, bf16[2,640,256]{2,1,0:T(8,128)(2,1)S(1)} %constant_dynamic-update-slice_fusion.rest_0_, ...), custom_call_target="tpu_custom_call" | custom-call | flops 1342177280 | bytes 5242880 | tf_op jit(solution)/shard_map/project/pallas_call | solution.py:304
  62.9 0.0 copy-start.7
  62.9 0.1 collective-permute-done.15.rest_4_
  63.0 3.1 %collective-permute-done.14.rest_3_ = bf16[640,256]{1,0:T(8,128)(2,1)S(1)} collective-permute-done((bf16[640,256]{1,0:T(8,128)(2,1)}, bf16[640,256]{1,0:T(8,128)(2,1)S(1)}, u32[]{:S(2)}, u32[]{:S(2)}) %collective-permute-start.14) | collective-permute-done | bytes 327712 | tf_op jit(solution)/shard_map/ppermute | solution.py:178
  66.0 2.3 %collective-permute-done.16.rest_5_ = bf16[640,256]{1,0:T(8,128)(2,1)S(1)} collective-permute-done((bf16[640,256]{1,0:T(8,128)(2,1)}, bf16[640,256]{1,0:T(8,128)(2,1)S(1)}, u32[]{:S(2)}, u32[]{:S(2)}) %collective-permute-start.16) | collective-permute-done | bytes 327712 | tf_op jit(solution)/shard_map/ppermute | solution.py:178
  68.4 3.5 %project.4.rest_2_ = f32[2,512,256]{2,1,0:T(8,128)S(1)} custom-call(s32[3]{0:T(128)S(1)} %pad_add_fusion.1.place, bf16[8,256,640]{2,1,0:T(8,128)(2,1)S(1)} %norm.1.own, bf16[8,256,640]{2,1,0:T(8,128)(2,1)} %collective-permute-done.8.other, bf16[640,256]{1,0:T(8,128)(2,1)} %collective-permute-done.9.rest_0_, ...), custom_call_target="tpu_custom_call" | custom-call | flops 1006632960 | bytes 3932160 | tf_op jit(solution)/shard_map/project/pallas_call | solution.py:304
  71.9 0.0 copy-start
  71.9 2.7 %project.5 = (bf16[256,512]{1,0:T(8,128)(2,1)S(1)}, bf16[256,512]{1,0:T(8,128)(2,1)S(1)}) custom-call(s32[3]{0:T(128)S(1)} %pad_add_fusion.1.place, bf16[8,256,640]{2,1,0:T(8,128)(2,1)S(1)} %norm.1.own, bf16[8,256,640]{2,1,0:T(8,128)(2,1)} %collective-permute-done.8.other, bf16[640,256]{1,0:T(8,128)(2,1)S(1)} %collective-permute-done.11.rest_0_, ...), custom_call_target="tpu_custom_call" | custom-call | flops 335544320 | bytes 1310720 | tf_op jit(solution)/shard_map/project/pallas_call | solution.py:304
  74.7 0.6 collective-permute-start.19
  75.3 1.6 %collective-permute-start.18 = (bf16[256,512]{1,0:T(8,128)(2,1)S(1)}, bf16[256,512]{1,0:T(8,128)(2,1)S(1)}, u32[]{:S(2)}, u32[]{:S(2)}) collective-permute-start(bf16[256,512]{1,0:T(8,128)(2,1)S(1)} %get-tuple-element.47), channel_id=1, source_target_pairs={{0,3},{1,2},{2,1},{3,0},{4,7},{5,6},{6,5},{7,4},{8,11},{9,10},{10,... | collective-permute-start | bytes 786440 | tf_op jit(solution)/shard_map/ppermute | solution.py:201
  76.9 0.9 mask.1
  77.7 6.2 %collective-permute-done.19.rest_1_ = bf16[256,512]{1,0:T(8,128)(2,1)S(1)} collective-permute-done((bf16[256,512]{1,0:T(8,128)(2,1)S(1)}, bf16[256,512]{1,0:T(8,128)(2,1)S(1)}, u32[]{:S(2)}, u32[]{:S(2)}) %collective-permute-start.19) | collective-permute-done | bytes 262176 | tf_op jit(solution)/shard_map/ppermute | solution.py:201
  84.0 4.8 %attend.2.rest_2_ = bf16[256,4096]{1,0:T(8,128)(2,1)} custom-call(s32[1]{0:T(128)} %bitcast.place, s32[2]{0:T(128)S(1)} %get-tuple-element.33.needs, bf16[256,4096]{1,0:T(8,128)(2,1)S(1)} %bitcast.21, f32[256,512]{1,0:T(8,128)S(1)} %get-tuple-element.34.bias, bf16[256,512]{1,0:T(8,128)(2,1)S(1)} %get-tuple-element.48.rest_0_, ...), custom_call_target="tpu_custom_call" | custom-call | flops 1073741824 | bytes 2097152 | tf_op jit(solution)/shard_map/attend/pallas_call | solution.py:338
  88.8 4.8 %attend.3 = bf16[256,4096]{1,0:T(8,128)(2,1)} custom-call(s32[1]{0:T(128)} %bitcast.place, s32[2]{0:T(128)S(1)} %get-tuple-element.33.needs, bf16[256,4096]{1,0:T(8,128)(2,1)S(1)} %bitcast.22, f32[256,512]{1,0:T(8,128)S(1)} %get-tuple-element.34.bias, bf16[256,512]{1,0:T(8,128)(2,1)S(1)} %collective-permute-done.17.rest_0_, ...), custom_call_target="tpu_custom_call", output_to_operand_aliasing={{}: (6, {})} | custom-call | flops 1073741824 | bytes 2097152 | tf_op jit(solution)/shard_map/attend/pallas_call | solution.py:338
  (34 shorter events, 0.2 us)
Async XLA Ops:
  0.0 7.6 %copy-start.9 = (s32[1,256]{1,0:T(1,128)S(1)}, s32[1,256]{1,0:T(1,128)}, u32[]{:S(2)}) copy-start(s32[1,256]{1,0:T(1,128)} %param.15) | copy-start | bytes 3076
  0.0 7.6 %copy-start.8 = (s32[1,256]{1,0:T(1,128)S(1)}, s32[1,256]{1,0:T(1,128)}, u32[]{:S(2)}) copy-start(s32[1,256]{1,0:T(1,128)} %param.16) | copy-start | bytes 3076
  0.0 11.5 %copy-start.6 = (f32[5120]{0:T(1024)S(1)}, f32[5120]{0:T(1024)}, u32[]{:S(2)}) copy-start(f32[5120]{0:T(1024)} %param.11) | copy-start | bytes 61444
  1.3 1.8 %collective-permute-start = (bf16[2,320,256]{2,1,0:T(8,128)(2,1)S(1)}, bf16[2,320,256]{2,1,0:T(8,128)(2,1)S(1)}, u32[]{:S(2)}, u32[]{:S(2)}) collective-permute-start(bf16[2,320,256]{2,1,0:T(8,128)(2,1)S(1)} %pad_maximum_fusion), channel_id=1, source_target_pairs={{0,2},{2,0},{1,3},{3,1},{4,6},{6,4},{5,7},{7,5},{8,10},{10,8},{9,1... | collective-permute-start | bytes 983048 | tf_op jit(solution)/shard_map/ppermute | solution.py:178
  1.8 9.7 %copy-start.1 = (bf16[1,256,5120]{2,1,0:T(8,128)(2,1)S(1)}, bf16[1,256,5120]{2,1,0:T(8,128)(2,1)}, u32[]{:S(2)}) copy-start(bf16[1,256,5120]{2,1,0:T(8,128)(2,1)} %param.9) | copy-start | bytes 7864324
  3.1 13.7 %collective-permute-start.1 = (bf16[640,256]{1,0:T(8,128)(2,1)S(1)}, bf16[640,256]{1,0:T(8,128)(2,1)}, u32[]{:S(2)}, u32[]{:S(2)}) collective-permute-start(bf16[640,256]{1,0:T(8,128)(2,1)S(1)} %dynamic-slice_bitcast_fusion), channel_id=1, source_target_pairs={{0,8},{8,16},{16,24},{24,0},{1,9},{9,17},{17,25},{25,1},{2,10},{10... | collective-permute-start | bytes 983048 | tf_op jit(solution)/shard_map/ppermute | solution.py:236
  6.1 20.4 %collective-permute-start.6 = (bf16[2,640,256]{2,1,0:T(8,128)(2,1)S(1)}, bf16[2,640,256]{2,1,0:T(8,128)(2,1)S(1)}, u32[]{:S(2)}, u32[]{:S(2)}) collective-permute-start(bf16[2,640,256]{2,1,0:T(8,128)(2,1)S(1)} %constant_dynamic-update-slice_fusion.rest_0_), channel_id=1, source_target_pairs={{0,4},{4,0},{1,5},{5,1},{2,6},{6,2},{3,7},{7,3},{8,12},{12,8},{9,1... | collective-permute-start | bytes 1966088 | tf_op jit(solution)/shard_map/ppermute | solution.py:178
  7.7 6.2 %collective-permute-start.2 = (s32[2,256]{1,0:T(2,128)S(1)}, s32[2,256]{1,0:T(2,128)S(1)}, u32[]{:S(2)}, u32[]{:S(2)}) collective-permute-start(s32[2,256]{1,0:T(2,128)S(1)} %pad_add_fusion.refs_0_), channel_id=1, source_target_pairs={{0,1},{1,0},{2,3},{3,2},{4,5},{5,4},{6,7},{7,6},{8,9},{9,8},{10,11... | collective-permute-start | bytes 6152 | tf_op jit(solution)/shard_map/ppermute | solution.py:201
  9.2 4.6 %collective-permute-start.3 = (s32[2,256]{1,0:T(2,128)S(1)}, s32[2,256]{1,0:T(2,128)S(1)}, u32[]{:S(2)}, u32[]{:S(2)}) collective-permute-start(s32[2,256]{1,0:T(2,128)S(1)} %pad_add_fusion.refs_0_), channel_id=1, source_target_pairs={{0,2},{2,0},{1,3},{3,1},{4,6},{6,4},{5,7},{7,5},{8,10},{10,8},{9,1... | collective-permute-start | bytes 6152 | tf_op jit(solution)/shard_map/ppermute | solution.py:178
  9.2 14.1 %collective-permute-start.4 = (bf16[640,256]{1,0:T(8,128)(2,1)S(1)}, bf16[640,256]{1,0:T(8,128)(2,1)}, u32[]{:S(2)}, u32[]{:S(2)}) collective-permute-start(bf16[640,256]{1,0:T(8,128)(2,1)S(1)} %dynamic-slice_bitcast_fusion), channel_id=1, source_target_pairs={{0,24},{8,0},{16,8},{24,16},{1,25},{9,1},{17,9},{25,17},{2,26},{10... | collective-permute-start | bytes 983048 | tf_op jit(solution)/shard_map/ppermute | solution.py:236
  11.5 34.1 %copy-start.10 = (f32[64]{0:T(128)S(1)}, f32[64]{0:T(128)}, u32[]{:S(2)}) copy-start(f32[64]{0:T(128)} %constant.43) | copy-start | bytes 772
  16.8 9.0 %collective-permute-start.5 = (bf16[640,256]{1,0:T(8,128)(2,1)}, bf16[640,256]{1,0:T(8,128)(2,1)S(1)}, u32[]{:S(2)}, u32[]{:S(2)}) collective-permute-start(bf16[640,256]{1,0:T(8,128)(2,1)} %collective-permute-done.1.rest_2_), channel_id=1, source_target_pairs={{0,1},{1,0},{2,3},{3,2},{4,5},{5,4},{6,7},{7,6},{8,9},{9,8},{10,11... | collective-permute-start | bytes 983048 | tf_op jit(solution)/shard_map/ppermute | solution.py:178
  25.8 0.7 copy-start.4
  26.5 0.8 copy-start.2
  27.3 10.4 %collective-permute-start.8 = (bf16[8,256,640]{2,1,0:T(8,128)(2,1)S(1)}, bf16[8,256,640]{2,1,0:T(8,128)(2,1)}, u32[]{:S(2)}, u32[]{:S(2)}) collective-permute-start(bf16[8,256,640]{2,1,0:T(8,128)(2,1)S(1)} %norm.1.own), channel_id=1, source_target_pairs={{0,2},{2,0},{1,3},{3,1},{4,6},{6,4},{5,7},{7,5},{8,10},{10,8},{9,1... | collective-permute-start | bytes 7864328 | tf_op jit(solution)/shard_map/ppermute | solution.py:178
  27.3 10.4 %collective-permute-start.7 = (bf16[640,256]{1,0:T(8,128)(2,1)}, bf16[640,256]{1,0:T(8,128)(2,1)}, u32[]{:S(2)}, u32[]{:S(2)}) collective-permute-start(bf16[640,256]{1,0:T(8,128)(2,1)} %collective-permute-done.4.rest_4_), channel_id=1, source_target_pairs={{0,1},{1,0},{2,3},{3,2},{4,5},{5,4},{6,7},{7,6},{8,9},{9,8},{10,11... | collective-permute-start | bytes 983048 | tf_op jit(solution)/shard_map/ppermute | solution.py:178
  28.6 10.2 %collective-permute-start.10 = (bf16[640,256]{1,0:T(8,128)(2,1)}, bf16[640,256]{1,0:T(8,128)(2,1)}, u32[]{:S(2)}, u32[]{:S(2)}) collective-permute-start(bf16[640,256]{1,0:T(8,128)(2,1)} %collective-permute-done.1.rest_2_), channel_id=1, source_target_pairs={{0,4},{4,0},{1,5},{5,1},{2,6},{6,2},{3,7},{7,3},{8,12},{12,8},{9,1... | collective-permute-start | bytes 983048 | tf_op jit(solution)/shard_map/ppermute | solution.py:178
  30.1 15.0 %collective-permute-start.9 = (bf16[640,256]{1,0:T(8,128)(2,1)}, bf16[640,256]{1,0:T(8,128)(2,1)}, u32[]{:S(2)}, u32[]{:S(2)}) collective-permute-start(bf16[640,256]{1,0:T(8,128)(2,1)} %collective-permute-done.1.rest_2_), channel_id=1, source_target_pairs={{0,8},{8,16},{16,24},{24,0},{1,9},{9,17},{17,25},{25,1},{2,10},{10... | collective-permute-start | bytes 983048 | tf_op jit(solution)/shard_map/ppermute | solution.py:236
  45.1 10.9 %collective-permute-start.11 = (bf16[640,256]{1,0:T(8,128)(2,1)}, bf16[640,256]{1,0:T(8,128)(2,1)S(1)}, u32[]{:S(2)}, u32[]{:S(2)}) collective-permute-start(bf16[640,256]{1,0:T(8,128)(2,1)} %collective-permute-done.9.rest_0_), channel_id=1, source_target_pairs={{0,4},{4,0},{1,5},{5,1},{2,6},{6,2},{3,7},{7,3},{8,12},{12,8},{9,1... | collective-permute-start | bytes 983048 | tf_op jit(solution)/shard_map/ppermute | solution.py:178
  46.6 16.4 %collective-permute-start.15 = (bf16[640,256]{1,0:T(8,128)(2,1)}, bf16[640,256]{1,0:T(8,128)(2,1)S(1)}, u32[]{:S(2)}, u32[]{:S(2)}) collective-permute-start(bf16[640,256]{1,0:T(8,128)(2,1)} %collective-permute-done.4.rest_4_), channel_id=1, source_target_pairs={{0,4},{4,0},{1,5},{5,1},{2,6},{6,2},{3,7},{7,3},{8,12},{12,8},{9,1... | collective-permute-start | bytes 983048 | tf_op jit(solution)/shard_map/ppermute | solution.py:178
  48.2 14.8 %collective-permute-start.13 = (bf16[640,256]{1,0:T(8,128)(2,1)}, bf16[640,256]{1,0:T(8,128)(2,1)S(1)}, u32[]{:S(2)}, u32[]{:S(2)}) collective-permute-start(bf16[640,256]{1,0:T(8,128)(2,1)} %collective-permute-done.9.rest_0_), channel_id=1, source_target_pairs={{0,1},{1,0},{2,3},{3,2},{4,5},{5,4},{6,7},{7,6},{8,9},{9,8},{10,11... | collective-permute-start | bytes 983048 | tf_op jit(solution)/shard_map/ppermute | solution.py:178
  48.7 17.3 %collective-permute-start.14 = (bf16[640,256]{1,0:T(8,128)(2,1)}, bf16[640,256]{1,0:T(8,128)(2,1)S(1)}, u32[]{:S(2)}, u32[]{:S(2)}) collective-permute-start(bf16[640,256]{1,0:T(8,128)(2,1)} %collective-permute-done.10.rest_2_), channel_id=1, source_target_pairs={{0,1},{1,0},{2,3},{3,2},{4,5},{5,4},{6,7},{7,6},{8,9},{9,8},{10,11... | collective-permute-start | bytes 983048 | tf_op jit(solution)/shard_map/ppermute | solution.py:178
  50.2 18.2 %collective-permute-start.16 = (bf16[640,256]{1,0:T(8,128)(2,1)}, bf16[640,256]{1,0:T(8,128)(2,1)S(1)}, u32[]{:S(2)}, u32[]{:S(2)}) collective-permute-start(bf16[640,256]{1,0:T(8,128)(2,1)} %collective-permute-done.7.rest_5_), channel_id=1, source_target_pairs={{0,4},{4,0},{1,5},{5,1},{2,6},{6,2},{3,7},{7,3},{8,12},{12,8},{9,1... | collective-permute-start | bytes 983048 | tf_op jit(solution)/shard_map/ppermute | solution.py:178
  55.9 16.0 %collective-permute-start.12 = (bf16[640,256]{1,0:T(8,128)(2,1)S(1)}, bf16[640,256]{1,0:T(8,128)(2,1)S(1)}, u32[]{:S(2)}, u32[]{:S(2)}) collective-permute-start(bf16[640,256]{1,0:T(8,128)(2,1)S(1)} %collective-permute-done.11.rest_0_), channel_id=1, source_target_pairs={{0,1},{1,0},{2,3},{3,2},{4,5},{5,4},{6,7},{7,6},{8,9},{9,8},{10,11... | collective-permute-start | bytes 983048 | tf_op jit(solution)/shard_map/ppermute | solution.py:178
  56.6 1.1 %copy-start.3 = (bf16[2,640,256]{2,1,0:T(8,128)(2,1)S(1)}, bf16[2,640,256]{2,1,0:T(8,128)(2,1)}, u32[]{:S(2)}) copy-start(bf16[2,640,256]{2,1,0:T(8,128)(2,1)} %copy-done.2) | copy-start | bytes 1966084
  57.7 1.0 %copy-start.5 = (bf16[640,256]{1,0:T(8,128)(2,1)S(1)}, bf16[640,256]{1,0:T(8,128)(2,1)}, u32[]{:S(2)}) copy-start(bf16[640,256]{1,0:T(8,128)(2,1)} %copy-done.4) | copy-start | bytes 983044
  62.9 9.0 %copy-start.7 = (f32[128]{0:T(128)S(1)}, f32[128]{0:T(128)}, u32[]{:S(2)}) copy-start(f32[128]{0:T(128)} %param.12) | copy-start | bytes 1540
  71.9 12.0 %copy-start = (bf16[1,256,4096]{2,1,0:T(8,128)(2,1)S(1)}, bf16[1,256,4096]{2,1,0:T(8,128)(2,1)}, u32[]{:S(2)}) copy-start(bf16[1,256,4096]{2,1,0:T(8,128)(2,1)} %param.10) | copy-start | bytes 6291460
  74.7 9.3 %collective-permute-start.19 = (bf16[256,512]{1,0:T(8,128)(2,1)S(1)}, bf16[256,512]{1,0:T(8,128)(2,1)S(1)}, u32[]{:S(2)}, u32[]{:S(2)}) collective-permute-start(bf16[256,512]{1,0:T(8,128)(2,1)S(1)} %get-tuple-element.48.rest_0_), channel_id=1, source_target_pairs={{0,1},{1,0},{2,3},{3,2},{4,5},{5,4},{6,7},{7,6},{8,9},{9,8},{10,11... | collective-permute-start | bytes 786440 | tf_op jit(solution)/shard_map/ppermute | solution.py:201
  75.3 13.5 %collective-permute-start.17 = (bf16[256,512]{1,0:T(8,128)(2,1)S(1)}, bf16[256,512]{1,0:T(8,128)(2,1)S(1)}, u32[]{:S(2)}, u32[]{:S(2)}) collective-permute-start(bf16[256,512]{1,0:T(8,128)(2,1)S(1)} %get-tuple-element.47), channel_id=1, source_target_pairs={{0,2},{1,3},{2,0},{3,1},{4,6},{5,7},{6,4},{7,5},{8,10},{9,11},{10,... | collective-permute-start | bytes 786440 | tf_op jit(solution)/shard_map/ppermute | solution.py:201
  75.3 13.5 %collective-permute-start.18 = (bf16[256,512]{1,0:T(8,128)(2,1)S(1)}, bf16[256,512]{1,0:T(8,128)(2,1)S(1)}, u32[]{:S(2)}, u32[]{:S(2)}) collective-permute-start(bf16[256,512]{1,0:T(8,128)(2,1)S(1)} %get-tuple-element.47), channel_id=1, source_target_pairs={{0,3},{1,2},{2,1},{3,0},{4,7},{5,6},{6,5},{7,4},{8,11},{9,10},{10,... | collective-permute-start | bytes 786440 | tf_op jit(solution)/shard_map/ppermute | solution.py:201
